TPU v7x, 32 devices: a whole 2x2x4 slice. The times are simulated.
32 devices in a mesh: grp: 8 (over z, y), ep: 4 (over x, core).
Axes of the slice: x: 2, y: 2, z: 4, core: 2. Of those that a mesh axis runs over, the one named last changes fastest.
Arguments:
- block_entry_states: bfloat16 [2, 2048, 2048], P(None, ('grp', 'ep')), may hold values from -6 to 6
- document_labels: int32 [2, 2048], P(None, 'grp'), may hold values from 0 to 125, as said below
- token_assignments: int32 [2, 2048, 8], P(None, ('grp', 'ep')), may hold values from 0 to 15, as said below
- worker_quota_tallies: int32 [16], replicated, may hold values from 24 to 48
- rescale_factors_both: bfloat16 [2, 2048], replicated, may hold values from 0.5 to 1.5
- triple_projection_matrix: bfloat16 [2048, 3, 2048], P(None, None, 'ep'), may hold values from -0.125 to 0.125
- probe_lookup_scalers: bfloat16 [2, 2048], P(None, 'ep'), may hold values from 0.5 to 1.5
- heads_merge_matrix: bfloat16 [2048, 2048], P('ep'), may hold values from -1 to 1
- dispatcher_matrix: bfloat16 [2048, 16], replicated, may hold values from -0.0625 to 0.0625
- specialist_widen_matrix: bfloat16 [16, 2048, 2048], P('ep'), may hold values from -0.125 to 0.125
- specialist_shrink_matrix: bfloat16 [16, 1024, 2048], P('ep'), may hold values from -2 to 2
- output_gradient: bfloat16 [2, 2048, 2048], P(None, ('grp', 'ep')), may hold values from -6 to 6
Outputs:
- output: bfloat16 [2, 2048, 2048], P(None, ('grp', 'ep'))
- grad_input: float32 [2, 2048, 2048], P(None, ('grp', 'ep'))
- grad_norm_gains: float32 [2, 2048], replicated
- grad_qkv: float32 [2048, 3, 2048], P(None, None, 'ep')
- grad_qk_gain: float32 [2, 2048], P(None, 'ep')
- grad_w_out: float32 [2048, 2048], P('ep')
- grad_router: float32 [2048, 16], replicated
- grad_w_in: float32 [16, 2048, 2048], P('ep', 'grp')
- grad_w_down: float32 [16, 1024, 2048], P('ep', 'grp')
Inputs may be any that keep to these rules, and one draw needn't show every extreme that they name: `document_labels`: within each sequence of 256 tokens the numbers start at 0 and never fall. `token_assignments`: each row names 8 different experts in increasing order.
All inputs are finite; a program needn't handle non-finite values.
Results may differ from a plain program's by a relative error of at most 0.02.
Values may be sent and summed in bfloat16 or wider, within the bound.
A program may use at most 448 MiB of HBM per device.

v0:
```python
import math

import jax
import jax.numpy as jnp
from jax import lax
from jax.sharding import PartitionSpec as P

HD = 128
TOP = 8


EPS = 1e-05
THETA = 10000.0
NEG = -1e30
HIGH = lax.Precision.HIGHEST


def apply_silu(content_vectors):
    return content_vectors * jax.nn.sigmoid(content_vectors)


def rope_tables(length, head_dim):
    half = head_dim // 2
    freq = THETA ** (-jnp.arange(half, dtype=jnp.float32) * 2.0 / head_dim)
    angle = jnp.arange(length, dtype=jnp.float32)[:, None] * freq[None, :]
    angle = jnp.concatenate([angle, angle], axis=-1)
    return (jnp.cos(angle), jnp.sin(angle))


def rotate_fwd(content_vectors, rotary_cos_values, rotary_sin_values):
    half = content_vectors.shape[-1] // 2
    turned = jnp.concatenate([-content_vectors[..., half:], content_vectors[..., :half]], axis=-1)
    return content_vectors * rotary_cos_values[:, None, :] + turned * rotary_sin_values[:, None, :]


def rotate_back(derivative, rotary_cos_values, rotary_sin_values):
    half = derivative.shape[-1] // 2
    swing = derivative * rotary_sin_values[:, None, :]
    turned = jnp.concatenate([swing[..., half:], -swing[..., :half]], axis=-1)
    return derivative * rotary_cos_values[:, None, :] + turned


def allowed_rows(document_label, first, count):
    place_rows = first + jnp.arange(count, dtype=jnp.int32)
    place_cols = jnp.arange(document_label.shape[0], dtype=jnp.int32)
    return (document_label[:, None] == document_label[None, :]) & (
        place_cols[None, :] <= place_rows[:, None]
    )


def attend_forward(queries, keys, values, document_label, block, scale):
    length = queries.shape[0]

    def one_block(index):
        first = index * block
        allowed = allowed_rows(document_label, first, block)
        scores = (
            jnp.einsum("ihd,jhd->hij", queries, keys, preferred_element_type=jnp.float32) * scale
        )
        scores = jnp.where(allowed[None], scores, NEG)
        highest = jnp.max(scores, axis=-1, keepdims=True)
        exponent = jnp.exp(scores - highest)
        totals = jnp.sum(exponent, axis=-1, keepdims=True)
        weights = (exponent / totals).astype(jnp.bfloat16)
        mixed = jnp.einsum("hij,jhd->ihd", weights, values, preferred_element_type=jnp.float32)
        return (mixed, highest[..., 0] + jnp.log(totals[..., 0]))

    mixed, logsum = lax.map(one_block, jnp.arange(length // block, dtype=jnp.int32))
    return (mixed.reshape(queries.shape), logsum)


def attend_backward(queries, keys, values, document_label, logsum, grad_mixed, block, scale):
    length = queries.shape[0]

    def one_block(carry, index):
        grad_keys, grad_values = carry
        first = index * block
        allowed = allowed_rows(document_label, first, block)
        scores = (
            jnp.einsum("ihd,jhd->hij", queries, keys, preferred_element_type=jnp.float32) * scale
        )
        scores = jnp.where(allowed[None], scores, NEG)
        weights = jnp.exp(scores - logsum[index][..., None])
        grad_weights = jnp.einsum(
            "ihd,jhd->hij", grad_mixed, values, preferred_element_type=jnp.float32
        )
        grad_values = grad_values + jnp.einsum(
            "hij,ihd->jhd",
            weights.astype(jnp.bfloat16),
            grad_mixed,
            preferred_element_type=jnp.float32,
        )
        inner = jnp.sum(weights * grad_weights, axis=-1, keepdims=True)
        grad_scores = (weights * (grad_weights - inner)).astype(jnp.bfloat16)
        grad_query = (
            jnp.einsum("hij,jhd->ihd", grad_scores, keys, preferred_element_type=jnp.float32)
            * scale
        )
        grad_keys = (
            grad_keys
            + jnp.einsum("hij,ihd->jhd", grad_scores, queries, preferred_element_type=jnp.float32)
            * scale
        )
        return ((grad_keys, grad_values), grad_query)

    zeros = jnp.zeros(keys.shape, jnp.float32)
    (grad_keys, grad_values), grad_query = lax.scan(
        one_block, (zeros, zeros), jnp.arange(length // block, dtype=jnp.int32)
    )
    return (grad_query.reshape(queries.shape), grad_keys, grad_values)


def share_experts(grad_in, grad_down):
    return (
        lax.psum_scatter(
            grad_in.astype(jnp.bfloat16), "grp", scatter_dimension=1, tiled=True
        ).astype(jnp.float32),
        lax.psum_scatter(
            grad_down.astype(jnp.bfloat16), "grp", scatter_dimension=1, tiled=True
        ).astype(jnp.float32),
    )


def per_device(
    block_entry_states,
    document_labels,
    token_assignments,
    worker_quota_tallies,
    rescale_factors_both,
    triple_projection_matrix,
    probe_lookup_scalers,
    heads_merge_matrix,
    dispatcher_matrix,
    specialist_widen_matrix,
    specialist_shrink_matrix,
    output_gradient,
):
    micro, local_rows, width = block_entry_states.shape
    parts = lax.axis_size("ep")
    seq_len = document_labels.shape[1]
    experts = dispatcher_matrix.shape[1]
    local_exp = specialist_widen_matrix.shape[0]
    inner_width = specialist_shrink_matrix.shape[1]
    head_dim = HD
    local_width = triple_projection_matrix.shape[2]
    local_heads = local_width // head_dim
    slots = min(local_rows, local_rows * TOP * 3 // (2 * experts))
    overall_seat_tally = local_exp * parts * slots
    block = min(512, seq_len)
    scale = 1.0 / math.sqrt(head_dim)
    scaling_factors = rescale_factors_both.astype(jnp.float32)
    head_gains = probe_lookup_scalers.astype(jnp.float32)
    router_wide = dispatcher_matrix.astype(jnp.float32)
    rotary_cos_values, rotary_sin_values = rope_tables(seq_len, head_dim)
    expert_ids = jnp.arange(experts, dtype=jnp.int32)
    slot_ids = jnp.arange(overall_seat_tally, dtype=jnp.int32)
    shape_heads = (seq_len, local_heads, head_dim)
    acc_qkv = jnp.zeros(triple_projection_matrix.shape, jnp.float32)
    acc_wo = jnp.zeros(heads_merge_matrix.shape, jnp.float32)
    acc_heads = jnp.zeros(probe_lookup_scalers.shape, jnp.float32)
    acc_first = jnp.zeros((width,), jnp.float32)
    acc_second = jnp.zeros((width,), jnp.float32)
    acc_router = jnp.zeros(dispatcher_matrix.shape, jnp.float32)
    acc_in = jnp.zeros(specialist_widen_matrix.shape, jnp.float32)
    acc_down = jnp.zeros(specialist_shrink_matrix.shape, jnp.float32)
    outputs = []
    input_grads = []
    for micro_index in range(micro):
        skip_connection_sum = block_entry_states[micro_index].astype(jnp.float32)
        adjoint_lines = output_gradient[micro_index].astype(jnp.float32)
        document_label = document_labels[micro_index]
        pick_routed_workers = token_assignments[micro_index]
        inv_first = lax.rsqrt(
            jnp.mean(skip_connection_sum * skip_connection_sum, axis=-1, keepdims=True) + EPS
        )
        hat_first = skip_connection_sum * inv_first
        attn_in = (hat_first * scaling_factors[0]).astype(jnp.bfloat16)
        gathered = lax.all_gather(attn_in, "ep", axis=0, tiled=True)
        projected = jnp.einsum(
            "td,dcf->tcf", gathered, triple_projection_matrix, preferred_element_type=jnp.float32
        )
        query_raw = projected[:, 0]
        key_raw = projected[:, 1]
        query_sq, key_sq = lax.psum(
            (jnp.sum(query_raw * query_raw, axis=-1), jnp.sum(key_raw * key_raw, axis=-1)), "ep"
        )
        query_inv = lax.rsqrt(query_sq / width + EPS)[:, None]
        key_inv = lax.rsqrt(key_sq / width + EPS)[:, None]
        query_hat = query_raw * query_inv
        key_hat = key_raw * key_inv
        queries = rotate_fwd(
            (query_hat * head_gains[0]).reshape(shape_heads), rotary_cos_values, rotary_sin_values
        ).astype(jnp.bfloat16)
        keys = rotate_fwd(
            (key_hat * head_gains[1]).reshape(shape_heads), rotary_cos_values, rotary_sin_values
        ).astype(jnp.bfloat16)
        values = projected[:, 2].reshape(shape_heads).astype(jnp.bfloat16)
        mixed, logsum = attend_forward(queries, keys, values, document_label, block, scale)
        mixed_low = mixed.reshape(seq_len, local_width).astype(jnp.bfloat16)
        attention = lax.psum_scatter(
            jnp.dot(mixed_low, heads_merge_matrix, preferred_element_type=jnp.float32),
            "ep",
            scatter_dimension=0,
            tiled=True,
        )
        hidden = skip_connection_sum + attention
        inv_second = lax.rsqrt(jnp.mean(hidden * hidden, axis=-1, keepdims=True) + EPS)
        hat_second = hidden * inv_second
        ffn_in = (hat_second * scaling_factors[1]).astype(jnp.bfloat16)
        logits = jnp.dot(ffn_in, dispatcher_matrix, preferred_element_type=jnp.float32)
        highest = jnp.max(logits, axis=-1, keepdims=True)
        exponent = jnp.exp(logits - highest)
        router_probs = exponent / jnp.sum(exponent, axis=-1, keepdims=True)
        bucket_agreements = (pick_routed_workers[..., None] == expert_ids).astype(jnp.int32)
        counts = jnp.sum(bucket_agreements, axis=1)
        prior = jnp.cumsum(counts, axis=0) - counts
        bin_start_shift = jnp.sum(bucket_agreements * prior[:, None, :], axis=-1)
        quota_upper_bound = jnp.sum(bucket_agreements * worker_quota_tallies, axis=-1)
        kept_indicator_array = bin_start_shift < quota_upper_bound
        hits_wide = bucket_agreements.astype(jnp.float32)
        router_coefficient = jnp.sum(hits_wide * router_probs[:, None, :], axis=-1)
        mixing_coefficient = jnp.where(kept_indicator_array, router_coefficient, 0.0)
        destination_spot = (
            pick_routed_workers % local_exp * (parts * slots)
            + pick_routed_workers // local_exp * slots
            + bin_start_shift
        )
        destination_spot = jnp.where(kept_indicator_array, destination_spot, overall_seat_tally)
        slot_hit = (destination_spot[..., None] == slot_ids).astype(jnp.float32)
        picked = jnp.sum(slot_hit, axis=1)
        send = lax.dot_general(
            picked.astype(jnp.bfloat16),
            ffn_in,
            (((0,), (0,)), ((), ())),
            preferred_element_type=jnp.float32,
        )
        send = send.astype(jnp.bfloat16).reshape(local_exp, parts, slots, width)
        received = lax.all_to_all(send, "ep", split_axis=1, concat_axis=1, tiled=True)
        count = received.shape[2]
        run_rows = received.reshape(local_exp, parts * count, width)
        gate_up = jnp.einsum(
            "erd,edf->erf", run_rows, specialist_widen_matrix, preferred_element_type=jnp.float32
        )
        act = (apply_silu(gate_up[..., :inner_width]) * gate_up[..., inner_width:]).astype(
            jnp.bfloat16
        )
        result = jnp.einsum(
            "erf,efd->erd", act, specialist_shrink_matrix, preferred_element_type=jnp.float32
        ).astype(jnp.bfloat16)
        returned = lax.all_to_all(
            result.reshape(local_exp, parts, count, width),
            "ep",
            split_axis=1,
            concat_axis=1,
            tiled=True,
        )
        returned, expert_rows, expert_gu, expert_act = (
            returned,
            received,
            gate_up.reshape(local_exp, parts, count, 2 * inner_width),
            act.reshape(local_exp, parts, count, inner_width),
        )
        index = jnp.minimum(destination_spot, overall_seat_tally - 1)
        returned_lines = jnp.take(
            returned.reshape(overall_seat_tally, width), index, axis=0
        ).astype(jnp.float32)
        moe = jnp.sum(mixing_coefficient[..., None] * returned_lines, axis=1)
        outputs.append((hidden + moe).astype(jnp.bfloat16))
        grad_gate = jnp.where(
            kept_indicator_array, jnp.sum(returned_lines * adjoint_lines[:, None, :], axis=-1), 0.0
        )
        spread = jnp.sum(slot_hit * mixing_coefficient[..., None], axis=1)
        grad_send = lax.dot_general(
            spread,
            adjoint_lines,
            (((0,), (0,)), ((), ())),
            precision=HIGH,
            preferred_element_type=jnp.float32,
        )
        grad_send = grad_send.astype(jnp.bfloat16).reshape(local_exp, parts, slots, width)
        grad_recv = lax.all_to_all(grad_send, "ep", split_axis=1, concat_axis=1, tiled=True)
        grad_out_rows = grad_recv.reshape(local_exp, parts * slots, width)
        in_rows = expert_rows.reshape(local_exp, parts * slots, width)
        gate_up = expert_gu.reshape(local_exp, parts * slots, 2 * inner_width)
        act = expert_act.reshape(local_exp, parts * slots, inner_width)
        gate_part = gate_up[..., :inner_width]
        up_part = gate_up[..., inner_width:]
        sigma = jax.nn.sigmoid(gate_part)
        grad_act = jnp.einsum(
            "erd,efd->erf",
            grad_out_rows,
            specialist_shrink_matrix,
            preferred_element_type=jnp.float32,
        )
        grad_gate_part = grad_act * up_part * sigma * (1.0 + gate_part * (1.0 - sigma))
        grad_up_part = grad_act * apply_silu(gate_part)
        grad_gu = jnp.concatenate([grad_gate_part, grad_up_part], axis=-1).astype(jnp.bfloat16)
        acc_in = acc_in + jnp.einsum(
            "erd,erf->edf", in_rows, grad_gu, preferred_element_type=jnp.float32
        )
        acc_down = acc_down + jnp.einsum(
            "erf,erd->efd", act, grad_out_rows, preferred_element_type=jnp.float32
        )
        grad_expert_in = jnp.einsum(
            "erf,edf->erd", grad_gu, specialist_widen_matrix, preferred_element_type=jnp.float32
        ).astype(jnp.bfloat16)
        grad_back = lax.all_to_all(
            grad_expert_in.reshape(local_exp, parts, slots, width),
            "ep",
            split_axis=1,
            concat_axis=1,
            tiled=True,
        )
        derivative_returned_lines = jnp.take(
            grad_back.reshape(overall_seat_tally, width), index, axis=0
        ).astype(jnp.float32)
        derivative_feedforward = jnp.sum(
            jnp.where(kept_indicator_array[..., None], derivative_returned_lines, 0.0), axis=1
        )
        grad_probs = jnp.sum(hits_wide * grad_gate[..., None], axis=1)
        grad_logits = router_probs * (
            grad_probs - jnp.sum(router_probs * grad_probs, axis=-1, keepdims=True)
        )
        derivative_feedforward = derivative_feedforward + jnp.dot(
            grad_logits, router_wide.T, precision=HIGH
        )
        acc_router = acc_router + jnp.dot(ffn_in.astype(jnp.float32).T, grad_logits, precision=HIGH)
        scaled_second = derivative_feedforward * scaling_factors[1]
        grad_hidden = adjoint_lines + inv_second * (
            scaled_second
            - hat_second * jnp.mean(scaled_second * hat_second, axis=-1, keepdims=True)
        )
        acc_second = acc_second + jnp.sum(derivative_feedforward * hat_second, axis=0)
        grad_branch = grad_hidden.astype(jnp.bfloat16)
        piece = lax.all_gather(grad_branch, "ep", axis=0, tiled=True)
        grad_wo = acc_wo
        grad_wo = grad_wo + lax.dot_general(
            mixed_low, piece, (((0,), (0,)), ((), ())), preferred_element_type=jnp.float32
        )
        partial_rows = lax.dot_general(
            piece, heads_merge_matrix, (((1,), (1,)), ((), ())), preferred_element_type=jnp.float32
        )
        grad_mixed = partial_rows
        acc_wo = grad_wo
        grad_mixed = grad_mixed.astype(jnp.bfloat16).reshape(shape_heads)
        grad_query, grad_key, grad_value = attend_backward(
            queries, keys, values, document_label, logsum, grad_mixed, block, scale
        )
        grad_qn = rotate_back(grad_query, rotary_cos_values, rotary_sin_values).reshape(
            seq_len, local_width
        )
        grad_kn = rotate_back(grad_key, rotary_cos_values, rotary_sin_values).reshape(
            seq_len, local_width
        )
        scaled_query = grad_qn * head_gains[0]
        scaled_key = grad_kn * head_gains[1]
        inner_query, inner_key = lax.psum(
            (jnp.sum(scaled_query * query_hat, axis=-1), jnp.sum(scaled_key * key_hat, axis=-1)),
            "ep",
        )
        grad_query_raw = query_inv * (scaled_query - query_hat * (inner_query / width)[:, None])
        grad_key_raw = key_inv * (scaled_key - key_hat * (inner_key / width)[:, None])
        acc_heads = acc_heads + jnp.stack(
            [jnp.sum(grad_qn * query_hat, axis=0), jnp.sum(grad_kn * key_hat, axis=0)]
        )
        grad_proj = jnp.stack(
            [grad_query_raw, grad_key_raw, grad_value.reshape(seq_len, local_width)], axis=1
        ).astype(jnp.bfloat16)
        acc_qkv = acc_qkv + jnp.einsum(
            "td,tcf->dcf", gathered, grad_proj, preferred_element_type=jnp.float32
        )
        grad_attn_in = lax.psum_scatter(
            jnp.einsum(
                "tcf,dcf->td",
                grad_proj,
                triple_projection_matrix,
                preferred_element_type=jnp.float32,
            ).astype(jnp.bfloat16),
            "ep",
            scatter_dimension=0,
            tiled=True,
        ).astype(jnp.float32)
        scaled_first = grad_attn_in * scaling_factors[0]
        grad_residual = grad_hidden + inv_first * (
            scaled_first - hat_first * jnp.mean(scaled_first * hat_first, axis=-1, keepdims=True)
        )
        acc_first = acc_first + jnp.sum(grad_attn_in * hat_first, axis=0)
        input_grads.append(grad_residual)
    gain_sum, router_sum = lax.psum((jnp.stack([acc_first, acc_second]), acc_router), ("grp", "ep"))
    qkv_sum, wo_sum, head_sum = (
        lax.psum(acc_qkv.astype(jnp.bfloat16), "grp").astype(jnp.float32),
        lax.psum(acc_wo.astype(jnp.bfloat16), "grp").astype(jnp.float32),
        lax.psum(acc_heads.astype(jnp.bfloat16), "grp").astype(jnp.float32),
    )
    in_share, down_share = share_experts(acc_in, acc_down)
    return (
        jnp.stack(outputs),
        jnp.stack(input_grads),
        gain_sum,
        qkv_sum,
        head_sum,
        wo_sum,
        router_sum,
        in_share,
        down_share,
    )


def solution(mesh):
    return jax.shard_map(
        per_device,
        mesh=mesh,
        in_specs=(
            P(None, ("grp", "ep"), None),
            P(None, "grp"),
            P(None, ("grp", "ep"), None),
            P(),
            P(),
            P(None, None, "ep"),
            P(None, "ep"),
            P("ep", None),
            P(),
            P("ep", None, None),
            P("ep", None, None),
            P(None, ("grp", "ep"), None),
        ),
        out_specs=(
            P(None, ("grp", "ep"), None),
            P(None, ("grp", "ep"), None),
            P(),
            P(None, None, "ep"),
            P(None, "ep"),
            P("ep", None),
            P(),
            P("ep", "grp", None),
            P("ep", "grp", None),
        ),
        check_vma=False,
    )
```

profile of v0, /device:TPU:0, one launch (start us, length us, event | category | flops | bytes accessed | tf_op | source)
XLA Modules:
  0.0 1995.5 jit_solution(13770719261951458342)
XLA Ops:
  94.6 25.4 %reduce-scatter.9.cloned.1.call-done = f32[64,2048]{1,0:T(8,128)} async-done(((f32[256,2048]{1,0:T(8,128)}), f32[64,2048]{1,0:T(8,128)}) %reduce-scatter.9.cloned.1.call-update) | async-done | bytes 524304 | tf_op jit(solution)/shard_map/reduce_scatter | solution.py:200
  120.0 34.5 %reduce-scatter.7.cloned.1.call-done = f32[64,2048]{1,0:T(8,128)} async-done(((f32[256,2048]{1,0:T(8,128)}), f32[64,2048]{1,0:T(8,128)}) %reduce-scatter.7.cloned.1.call-update) | async-done | bytes 524304 | tf_op jit(solution)/shard_map/reduce_scatter | solution.py:200
  175.9 31.2 %all-to-all-done = bf16[4,4,48,2048]{3,2,0,1:T(8,128)(2,1)} async-done(((bf16[4,4,48,2048]{3,2,0,1:T(8,128)(2,1)}), bf16[4,4,48,2048]{3,2,0,1:T(8,128)(2,1)}, u32[]{:S(2)}, u32[]{:S(2)}) %all-to-all-start) | async-done | bytes 3145760 | tf_op jit(solution)/shard_map/all_to_all | solution.py:238
  215.7 17.4 fusion.132
  233.1 15.6 all-to-all-done.4
  266.1 16.6 convolution_convert_fusion.5
  301.1 25.4 %all-to-all-done.5 = bf16[4,4,48,2048]{3,2,0,1:T(8,128)(2,1)} async-done(((bf16[4,4,48,2048]{3,2,0,1:T(8,128)(2,1)}), bf16[4,4,48,2048]{3,2,0,1:T(8,128)(2,1)}, u32[]{:S(2)}, u32[]{:S(2)}) %all-to-all-start.5) | async-done | bytes 3145760 | tf_op jit(solution)/shard_map/all_to_all | solution.py:307
  346.4 21.7 %all-to-all-done.1 = bf16[4,4,48,2048]{3,2,0,1:T(8,128)(2,1)} async-done(((bf16[4,4,48,2048]{3,2,0,1:T(8,128)(2,1)}), bf16[4,4,48,2048]{3,2,0,1:T(8,128)(2,1)}, u32[]{:S(2)}, u32[]{:S(2)}) %all-to-all-start.1) | async-done | bytes 3145760 | tf_op jit(solution)/shard_map/all_to_all | solution.py:250
  407.4 31.1 %all-to-all-done.2 = bf16[4,4,48,2048]{3,2,0,1:T(8,128)(2,1)} async-done(((bf16[4,4,48,2048]{3,2,0,1:T(8,128)(2,1)}), bf16[4,4,48,2048]{3,2,0,1:T(8,128)(2,1)}, u32[]{:S(2)}, u32[]{:S(2)}) %all-to-all-start.2) | async-done | bytes 3145760 | tf_op jit(solution)/shard_map/all_to_all | solution.py:238
  447.1 17.4 fusion.134
  464.6 15.6 all-to-all-done.6
  497.6 16.6 convolution_convert_fusion.4
  532.5 25.4 %all-to-all-done.7 = bf16[4,4,48,2048]{3,2,0,1:T(8,128)(2,1)} async-done(((bf16[4,4,48,2048]{3,2,0,1:T(8,128)(2,1)}), bf16[4,4,48,2048]{3,2,0,1:T(8,128)(2,1)}, u32[]{:S(2)}, u32[]{:S(2)}) %all-to-all-start.7) | async-done | bytes 3145760 | tf_op jit(solution)/shard_map/all_to_all | solution.py:307
  574.6 24.9 %all-to-all-done.3 = bf16[4,4,48,2048]{3,2,0,1:T(8,128)(2,1)} async-done(((bf16[4,4,48,2048]{3,2,0,1:T(8,128)(2,1)}), bf16[4,4,48,2048]{3,2,0,1:T(8,128)(2,1)}, u32[]{:S(2)}, u32[]{:S(2)}) %all-to-all-start.3) | async-done | bytes 3145760 | tf_op jit(solution)/shard_map/all_to_all | solution.py:250
  622.9 16.0 all-gather.11.cloned.1.call-done
  730.2 17.4 add_convert_fusion.1
  749.0 26.5 %fusion.8 = f32[4,2048,2048]{2,1,0:T(8,128)} fusion(bf16[4,192,2048]{2,1,0:T(8,128)(2,1)} %bitcast.226, bf16[4,192,1024]{2,1,0:T(8,128)(2,1)} %get-tuple-element.177, bf16[4,192,1024]{2,1,0:T(8,128)(2,1)S(1)} %copy-done.51), kind=kOutput, calls=%fused_computation.49 | convolution fusion | flops 6448742400 | bytes 73400320 | tf_op jit(solution)/shard_map/erd,erf->edf/dot_general | solution.py:298
  775.6 34.2 %add_convert_fusion = bf16[4,2048,2048]{2,1,0:T(8,128)(2,1)} fusion(f32[4,2048,2048]{2,1,0:T(8,128)} %fusion.8, bf16[4,192,2048]{2,1,0:T(8,128)(2,1)S(1)} %bitcast.228, bf16[4,192,1024]{2,1,0:T(8,128)(2,1)} %get-tuple-element.179, bf16[4,192,1024]{2,1,0:T(8,128)(2,1)S(1)} %copy-done.52), kind=kOutput, calls=%fused_computation.4 | convolution fusion | flops 6482296832 | bytes 106954752 | tf_op jit(solution)/shard_map/erd,erf->edf/dot_general | solution.py:298
  813.3 22.5 %psum.101 = bf16[2,512]{1,0:T(2,128)(2,1)S(1)} all-reduce(bf16[2,512]{1,0:T(2,128)(2,1)S(1)} %fusion.98), channel_id=1, replica_groups=mesh['grp'=8,'ep'=4] {'grp'}, use_global_device_ids=true, to_apply=%region_72.74 | all-reduce | flops 1024 | bytes 4096 | tf_op jit(solution)/shard_map/psum | solution.py:393
  841.9 38.3 %psum.99 = f32[2,2048]{1,0:T(2,128)} all-reduce(f32[2,2048]{1,0:T(2,128)S(1)} %pad_maximum_fusion.15), channel_id=1, replica_groups=mesh['grp'=8,'ep'=4] {'grp','ep'}, use_global_device_ids=true, to_apply=%region_66.68 | all-reduce | flops 4096 | bytes 32768 | tf_op jit(solution)/shard_map/psum | solution.py:389
  880.2 146.5 %all-reduce.8.cloned.1.call-done = (bf16[2048,3,512]{2,0,1:T(8,128)(2,1)}, bf16[512,2048]{1,0:T(8,128)(2,1)}) async-done(((bf16[2048,3,512]{2,0,1:T(8,128)(2,1)}, bf16[512,2048]{1,0:T(8,128)(2,1)}), (bf16[2048,3,512]{2,0,1:T(8,128)(2,1)}, bf16[512,2048]{1,0:T(8,128)(2,1)})) %all-reduce.8.cloned.1.call-update) | async-done | bytes 8388624 | tf_op jit(solution)/shard_map/psum | solution.py:391
  1038.8 273.3 %reduce-scatter.17.cloned.1.call-done = bf16[4,128,2048]{2,1,0:T(8,128)(2,1)} async-done(((bf16[4,1024,2048]{2,1,0:T(8,128)(2,1)}), bf16[4,128,2048]{2,1,0:T(8,128)(2,1)}) %reduce-scatter.17.cloned.1.call-update) | async-done | bytes 2097168 | tf_op jit(solution)/shard_map/reduce_scatter | solution.py:118
  1316.2 542.3 %reduce-scatter.15.cloned.1.call-done = bf16[4,256,2048]{2,1,0:T(8,128)(2,1)} async-done(((bf16[4,2048,2048]{2,1,0:T(8,128)(2,1)}), bf16[4,256,2048]{2,1,0:T(8,128)(2,1)}) %reduce-scatter.15.cloned.1.call-update) | async-done | bytes 4194320 | tf_op jit(solution)/shard_map/reduce_scatter | solution.py:115
  1865.3 121.7 %all-reduce.6.cloned.1.call-done = f32[2048,16]{0,1:T(8,128)} async-done(((f32[2048,16]{0,1:T(8,128)}), f32[2048,16]{0,1:T(8,128)}) %all-reduce.6.cloned.1.call-update) | async-done | bytes 131088 | tf_op jit(solution)/shard_map/psum | solution.py:389
  (540 shorter events, 421.3 us)
Async XLA Ops:
  7.2 24.5 %all-gather.7.cloned.1.call-start = ((), (), s32[]{:S(2)}) async-start(), calls=%async_computation.16 | async-start | bytes 1310720 | tf_op jit(solution)/shard_map/all_gather | solution.py:178
  9.4 609.9 %copy-start.73 = (f32[1,2048]{1,0:T(1,128)}, f32[1,2048]{1,0:T(1,128)S(1)}, u32[]{:S(2)}) copy-start(f32[1,2048]{1,0:T(1,128)S(1)} %get-tuple-element.241) | copy-start | bytes 24580
  12.0 38.5 %all-gather.5.cloned.1.call-start = ((), (), s32[]{:S(2)}) async-start(), calls=%async_computation.14 | async-start | bytes 1310720 | tf_op jit(solution)/shard_map/all_gather | solution.py:178
  12.8 107.2 %reduce-scatter.9.cloned.1.call-start = ((), (), s32[]{:S(2)}) async-start(), calls=%async_computation.17 | async-start | bytes 2621440 | tf_op jit(solution)/shard_map/reduce_scatter | solution.py:200
  87.3 67.2 %reduce-scatter.7.cloned.1.call-start = ((), (), s32[]{:S(2)}) async-start(), calls=%async_computation.15 | async-start | bytes 2621440 | tf_op jit(solution)/shard_map/reduce_scatter | solution.py:200
  156.8 462.5 %copy-start.8 = (f32[64,2048]{1,0:T(8,128)}, f32[64,2048]{1,0:T(8,128)S(1)}, u32[]{:S(2)}) copy-start(f32[64,2048]{1,0:T(8,128)S(1)} %get-tuple-element.170) | copy-start | bytes 1572868
  156.8 462.5 %copy-start.10 = (f32[64,2048]{1,0:T(8,128)}, f32[64,2048]{1,0:T(8,128)S(1)}, u32[]{:S(2)}) copy-start(f32[64,2048]{1,0:T(8,128)S(1)} %get-tuple-element.208) | copy-start | bytes 1572868
  165.0 42.1 %all-to-all-start = ((bf16[4,4,48,2048]{3,2,0,1:T(8,128)(2,1)}), bf16[4,4,48,2048]{3,2,0,1:T(8,128)(2,1)}, u32[]{:S(2)}, u32[]{:S(2)}) async-start(bf16[4,4,48,2048]{3,2,0,1:T(8,128)(2,1)} %copy.183), calls=%async_computation.1 | async-start | bytes 6291456 | tf_op jit(solution)/shard_map/all_to_all | solution.py:238
  207.1 41.6 %all-to-all-start.4 = ((bf16[4,4,48,2048]{3,2,0,1:T(8,128)(2,1)}), bf16[4,4,48,2048]{3,2,0,1:T(8,128)(2,1)}, u32[]{:S(2)}, u32[]{:S(2)}) async-start(bf16[4,4,48,2048]{3,2,0,1:T(8,128)(2,1)} %copy.208), calls=%async_computation.6 | async-start | bytes 6291456 | tf_op jit(solution)/shard_map/all_to_all | solution.py:281
  284.7 41.8 %all-to-all-start.5 = ((bf16[4,4,48,2048]{3,2,0,1:T(8,128)(2,1)}), bf16[4,4,48,2048]{3,2,0,1:T(8,128)(2,1)}, u32[]{:S(2)}, u32[]{:S(2)}) async-start(bf16[4,4,48,2048]{3,2,0,1:T(8,128)(2,1)} %copy.210), calls=%async_computation.7 | async-start | bytes 6291456 | tf_op jit(solution)/shard_map/all_to_all | solution.py:307
  326.5 41.7 %all-to-all-start.1 = ((bf16[4,4,48,2048]{3,2,0,1:T(8,128)(2,1)}), bf16[4,4,48,2048]{3,2,0,1:T(8,128)(2,1)}, u32[]{:S(2)}, u32[]{:S(2)}) async-start(bf16[4,4,48,2048]{3,2,0,1:T(8,128)(2,1)} %copy.185), calls=%async_computation.2 | async-start | bytes 6291456 | tf_op jit(solution)/shard_map/all_to_all | solution.py:250
  389.4 227.7 %copy-start.78 = (f32[64,16]{0,1:T(8,128)}, f32[64,16]{0,1:T(8,128)S(1)}, u32[]{:S(2)}) copy-start(f32[64,16]{0,1:T(8,128)S(1)} %fusion.86) | copy-start | bytes 12292
  396.5 42.0 %all-to-all-start.2 = ((bf16[4,4,48,2048]{3,2,0,1:T(8,128)(2,1)}), bf16[4,4,48,2048]{3,2,0,1:T(8,128)(2,1)}, u32[]{:S(2)}, u32[]{:S(2)}) async-start(bf16[4,4,48,2048]{3,2,0,1:T(8,128)(2,1)} %copy.200), calls=%async_computation.4 | async-start | bytes 6291456 | tf_op jit(solution)/shard_map/all_to_all | solution.py:238
  438.5 41.7 %all-to-all-start.6 = ((bf16[4,4,48,2048]{3,2,0,1:T(8,128)(2,1)}), bf16[4,4,48,2048]{3,2,0,1:T(8,128)(2,1)}, u32[]{:S(2)}, u32[]{:S(2)}) async-start(bf16[4,4,48,2048]{3,2,0,1:T(8,128)(2,1)} %copy.226), calls=%async_computation.9 | async-start | bytes 6291456 | tf_op jit(solution)/shard_map/all_to_all | solution.py:281
  516.1 41.8 %all-to-all-start.7 = ((bf16[4,4,48,2048]{3,2,0,1:T(8,128)(2,1)}), bf16[4,4,48,2048]{3,2,0,1:T(8,128)(2,1)}, u32[]{:S(2)}, u32[]{:S(2)}) async-start(bf16[4,4,48,2048]{3,2,0,1:T(8,128)(2,1)} %copy.228), calls=%async_computation.10 | async-start | bytes 6291456 | tf_op jit(solution)/shard_map/all_to_all | solution.py:307
  557.9 41.7 %all-to-all-start.3 = ((bf16[4,4,48,2048]{3,2,0,1:T(8,128)(2,1)}), bf16[4,4,48,2048]{3,2,0,1:T(8,128)(2,1)}, u32[]{:S(2)}, u32[]{:S(2)}) async-start(bf16[4,4,48,2048]{3,2,0,1:T(8,128)(2,1)} %copy.202), calls=%async_computation.5 | async-start | bytes 6291456 | tf_op jit(solution)/shard_map/all_to_all | solution.py:250
  562.6 76.4 %all-gather.11.cloned.1.call-start = ((), (), s32[]{:S(2)}) async-start(), calls=%async_computation.20 | async-start | bytes 1310720 | tf_op jit(solution)/shard_map/all_gather | solution.py:335
  622.1 35.1 %all-gather.9.cloned.1.call-start = ((), (), s32[]{:S(2)}) async-start(), calls=%async_computation.18 | async-start | bytes 1310720 | tf_op jit(solution)/shard_map/all_gather | solution.py:335
  622.6 213.7 %reduce-scatter.13.cloned.1.call-start = ((), (), s32[]{:S(2)}) async-start(), calls=%async_computation.21 | async-start | bytes 1310720 | tf_op jit(solution)/shard_map/reduce_scatter | solution.py:372
  695.7 140.7 %reduce-scatter.11.cloned.1.call-start = ((), (), s32[]{:S(2)}) async-start(), calls=%async_computation.19 | async-start | bytes 1310720 | tf_op jit(solution)/shard_map/reduce_scatter | solution.py:372
  702.4 324.3 %all-reduce.8.cloned.1.call-start = ((), (), s32[]{:S(2)}) async-start(), calls=%async_computation.25 | async-start | bytes 16777216 | tf_op jit(solution)/shard_map/psum | solution.py:391
  713.5 598.6 %reduce-scatter.17.cloned.1.call-start = ((), (), s32[]{:S(2)}) async-start(), calls=%async_computation.24 | async-start | bytes 18874368 | tf_op jit(solution)/shard_map/reduce_scatter | solution.py:118
  747.6 1110.8 %reduce-scatter.15.cloned.1.call-start = ((), (), s32[]{:S(2)}) async-start(), calls=%async_computation.23 | async-start | bytes 37748736 | tf_op jit(solution)/shard_map/reduce_scatter | solution.py:115
  810.1 1176.8 %all-reduce.6.cloned.1.call-start = ((), (), s32[]{:S(2)}) async-start(), calls=%async_computation.22 | async-start | bytes 262144 | tf_op jit(solution)/shard_map/psum | solution.py:389
  (152 other events, 1989.4 us)
Sparse Core Ops, SparseCore 0:
  12.2 19.4 all-gather.6
  33.8 16.7 all-gather.4
  87.4 32.5 reduce-scatter.8
  123.1 31.3 reduce-scatter.6
  622.2 16.7 all-gather.10
  640.4 16.7 all-gather.8
  695.8 25.9 reduce-scatter.12
  725.1 24.8 reduce-scatter.10
  754.7 271.9 all-reduce.7
  1030.3 281.6 reduce-scatter.16
  1316.3 542.1 reduce-scatter.14
  1865.4 121.5 all-reduce.5
where the time goes:
time: 2010 us; the launch traced here: 2000 us
  waiting for transfers between devices  1390 us (69%)
  matrix products  275 us (14%)
  local copies, waits for them, and re-layouts  117 us (6%)
  other arithmetic  85.6 us (4%)
  blocking collectives  73.2 us (4%)
  starting transfers between devices  39.7 us (2%)
    reduce_scatter x1, waiting for transfers between devices, share_experts(): lax.psum_scatter(grad_in.astype(jnp.bfloat16), 'grp', scatter_dimension=1...  542 us
    reduce_scatter x1, waiting for transfers between devices, share_experts(): lax.psum_scatter(grad_down.astype(jnp.bfloat16), 'grp', scatter_dimension...  273 us
    psum x1, waiting for transfers between devices, per_device(): lax.psum(acc_qkv.astype(jnp.bfloat16), 'grp').astype(jnp.float32)  147 us
    psum x1, waiting for transfers between devices, per_device(): lax.psum((jnp.stack([acc_first, acc_second]), acc_router), ('grp', 'ep'))  122 us
    all_to_all x2, waiting for transfers between devices, per_device(): lax.all_to_all(send, 'ep', split_axis=1, concat_axis=1, tiled=True)  62.3 us
    dot_general x2, matrix products, per_device(): jnp.einsum('erd,erf->edf', in_rows, grad_gu, preferred_element_type=jnp.f...  60.8 us
    reduce_scatter x2, waiting for transfers between devices, per_device(): lax.psum_scatter(jnp.dot(mixed_low, heads_merge_matrix, preferred_element...  60 us
    all_to_all x2, waiting for transfers between devices, per_device(): lax.all_to_all(grad_expert_in.reshape(local_exp, parts, slots, width), 'e...  50.8 us
  transfers between devices with their start and end apart: 20, of which 18 were waited for; matrix products, arithmetic and copies ran while one was open for 14% of the time, Pallas kernels for 0%

commit v1 on v0

v1 whole, which is shorter than its diff:
```python
import functools
import math

import jax
import jax.numpy as jnp
from jax import lax
from jax.experimental import pallas as pl
from jax.experimental.pallas import tpu as pltpu
from jax.sharding import PartitionSpec as P

HD = 128
TOP = 8
EPS = 1e-05
THETA = 10000.0
NEG = -1e30
HIGH = lax.Precision.HIGHEST
ALL = ("grp", "ep")
MESH = pl.DeviceIdType.MESH
ROWS = 16
BF = jnp.bfloat16
F32 = jnp.float32


def apply_silu(v):
    return v * jax.nn.sigmoid(v)


def rope_tables(length, head_dim):
    half = head_dim // 2
    freq = THETA ** (-jnp.arange(half, dtype=F32) * 2.0 / head_dim)
    angle = jnp.arange(length, dtype=F32)[:, None] * freq[None, :]
    angle = jnp.concatenate([angle, angle], axis=-1)
    return (jnp.cos(angle), jnp.sin(angle))


def swap_halves(v):
    half = v.shape[-1] // 2
    return jnp.concatenate([v[..., half:], v[..., :half]], axis=-1)


def mesh_sizes(groups, parts):
    major = 4 if groups % 4 == 0 else groups
    return major, groups // major, parts // 2


class Line:
    def __init__(self, size, place, step):
        self.size, self.place, self.step = size, place, step

    def at(self, hops):
        return (
            lax.axis_index("grp") + hops * self.step[0],
            lax.axis_index("ep") + hops * self.step[1],
        )


def lines(groups, parts):
    major, minor, xs = mesh_sizes(groups, parts)
    g, e = lax.axis_index("grp"), lax.axis_index("ep")
    core = lax.rem(e, 2)
    x_pos, minor_pos = lax.div(e, 2), lax.rem(g, minor)
    if xs == minor:
        first = Line(xs, jnp.where(core == 0, x_pos, minor_pos), (core, 2 - 2 * core))
        second = Line(xs, jnp.where(core == 0, minor_pos, x_pos), (1 - core, 2 * core))
    else:
        first = Line(xs, x_pos, (0, 2))
        second = Line(minor, minor_pos, (1, 0))
    return Line(2, core, (0, 1)), first, second, Line(major, lax.div(g, minor), (minor, 0))


def greet(some):
    barrier = pltpu.get_barrier_semaphore()
    peers = 0
    for line in some:
        if line.size == 2:
            pl.semaphore_signal(barrier, inc=1, device_id=line.at(1 - 2 * line.place), device_id_type=MESH)
            peers = peers + 1
        else:
            for way, there in ((1, line.place < line.size - 1), (-1, line.place > 0)):

                @pl.when(there)
                def _(line=line, way=way):
                    pl.semaphore_signal(barrier, inc=1, device_id=line.at(way), device_id_type=MESH)

                peers = peers + there.astype(jnp.int32)
    pl.semaphore_wait(barrier, peers)


def remote(src, dst, send, recv, target):
    return pltpu.make_async_remote_copy(
        src_ref=src, dst_ref=dst, send_sem=send, recv_sem=recv, device_id=target, device_id_type=MESH
    )


class Hop:
    def __init__(self, legs, after=None):
        self.legs, self.after = legs, after

    def _each(self, which, act):
        for leg in self.legs:
            if leg[which] is None:
                act(leg)
            else:
                pl.when(leg[which])(functools.partial(act, leg))

    def start(self):
        self._each(0, lambda leg: leg[2]().start())

    def arrive(self):
        def act(leg):
            leg[3]().wait_recv()
            if leg[4] is not None:
                leg[4]()

        self._each(1, act)

    def sent(self):
        self._each(0, lambda leg: leg[2]().wait_send())


def gather_hops(line, at, send, recv):
    n, a = line.size, line.place
    if n == 2:
        mine, theirs, peer = at(a), at(1 - a), line.at(1 - 2 * a)
        return [
            Hop([(None, None, lambda: remote(mine, mine, send(0), recv(0), peer),
                  lambda: remote(theirs, theirs, send(0), recv(0), peer), None)])
        ]
    hops = []
    for s in range(1, n):
        legs = []
        for d, way in enumerate((1, -1)):
            k = (s - 1) * 2 + d
            out = a - way * (s - 1)
            into = a - way * s
            sends = (out >= 0) & (out < n) & (a + way >= 0) & (a + way < n)
            gets = (into >= 0) & (into < n)
            out, into = jnp.clip(out, 0, n - 1), jnp.clip(into, 0, n - 1)
            legs.append((
                sends, gets,
                lambda out=out, way=way, k=k: remote(at(out), at(out), send(k), recv(k), line.at(way)),
                lambda into=into, way=way, k=k: remote(at(into), at(into), send(k), recv(k), line.at(-way)),
                None,
            ))
        hops.append(Hop(legs))
    return hops


def reduce_hops(line, acc, land, add, send, recv):
    n, a = line.size, line.place
    if n == 2:
        peer = line.at(1 - 2 * a)
        return [
            Hop([(None, None, lambda: remote(acc(1 - a), land(0), send(0), recv(0), peer),
                  lambda: remote(land(0), land(0), send(0), recv(0), peer),
                  lambda: add(acc(a), land(0)))])
        ]
    hops = []
    for s in range(n - 1):
        legs = []
        for d, way in enumerate((1, -1)):
            k = s * 2 + d
            b = a if way == 1 else n - 1 - a
            sends = (b <= s) & (b < n - 1)
            gets = (b - 1 <= s) & (b >= 1)
            out = b + n - 1 - s
            into = b + n - 2 - s
            out, into = jnp.clip(out, 0, n - 1), jnp.clip(into, 0, n - 1)
            if way == -1:
                out, into = n - 1 - out, n - 1 - into
            legs.append((
                sends, gets,
                lambda out=out, way=way, k=k: remote(acc(out), land(k), send(k), recv(k), line.at(way)),
                lambda way=way, k=k: remote(land(k), land(k), send(k), recv(k), line.at(-way)),
                lambda into=into, k=k: add(acc(into), land(k)),
            ))
        hops.append(Hop(legs))
    return hops


def hop_count(n):
    return 1 if n == 2 else n - 1


def leg_count(n):
    return 1 if n == 2 else 2 * (n - 1)


def flow(chains):
    depth, count = max(len(c) for c in chains), len(chains)
    for t in range(count + depth):
        for k in range(count):
            i = t - k
            if 1 <= i <= len(chains[k]):
                chains[k][i - 1].arrive()
            if 0 <= i < len(chains[k]):
                chains[k][i].start()
    for chain in chains:
        for hop in chain:
            hop.sent()


def add(acc, land):
    lead = acc.shape[:-2]

    def one(i):
        where = []
        for size in reversed(lead):
            where.insert(0, lax.rem(i, size))
            i = lax.div(i, size)
        where = tuple(where) + (slice(None), slice(None))
        acc[where] = (acc[where].astype(F32) + land[where].astype(F32)).astype(acc.dtype)

    if lead:
        pl.loop(0, math.prod(lead))(one)
    else:
        one(0)


def gather_kernel(groups, parts, x, out, local, send, recv):
    core, first, second, long = lines(groups, parts)
    c, p, q, z = core.place, first.place, second.place, long.place
    greet([core, first, second, long])
    chunks = x.shape[0]
    own = [pltpu.make_async_copy(x.at[k], out.at[k, c, p, q, z], local.at[k]) for k in range(chunks)]
    for copy in own:
        copy.start()
    chains = []
    for k in range(chunks):
        base = [0]

        def sems(n, k=k, base=base):
            b = base[0]
            base[0] += leg_count(n)
            return (lambda i: send.at[k, b + i]), (lambda i: recv.at[k, b + i])

        chain = []
        chain += gather_hops(long, lambda i, k=k: out.at[k, c, p, q, i], *sems(long.size))
        chain += gather_hops(second, lambda i, k=k: out.at[k, c, p, i], *sems(second.size))
        chain += gather_hops(first, lambda i, k=k: out.at[k, c, i], *sems(first.size))
        chain += gather_hops(core, lambda i, k=k: out.at[k, i], *sems(2))
        chains.append(chain)
    for copy in own:
        copy.wait()
    flow(chains)


def gather_all(x, collective_id):
    groups, parts = lax.axis_size("grp"), lax.axis_size("ep")
    major, minor, xs = mesh_sizes(groups, parts)
    width = x.shape[-1]
    x = x.reshape(-1, ROWS, width)
    legs = sum(leg_count(n) for n in (2, xs, minor, major))
    chunks = x.shape[0]
    return pl.pallas_call(
        functools.partial(gather_kernel, groups, parts),
        out_shape=jax.ShapeDtypeStruct((chunks, 2, xs, minor, major, ROWS, width), x.dtype),
        in_specs=[pl.BlockSpec(memory_space=pl.ANY)],
        out_specs=pl.BlockSpec(memory_space=pl.ANY),
        scratch_shapes=[
            pltpu.SemaphoreType.DMA((chunks,)),
            pltpu.SemaphoreType.DMA((chunks, legs)),
            pltpu.SemaphoreType.DMA((chunks, legs)),
        ],
        compiler_params=pltpu.CompilerParams(collective_id=collective_id, has_side_effects=True),
    )(x)


def scatter_kernel(groups, parts, part, out, acc, land_c, land_p, land_q, land_z, local, send, recv):
    core, first, second, long = lines(groups, parts)
    c, p, q, z = core.place, first.place, second.place, long.place
    chunks = part.shape[0]
    own = [pltpu.make_async_copy(part.at[k, c], acc.at[k], local.at[k]) for k in range(chunks)]
    for copy in own:
        copy.start()
    greet([core, first, second, long])
    chains = []
    for k in range(chunks):
        base = [0]

        def sems(n, k=k, base=base):
            b = base[0]
            base[0] += leg_count(n)
            return (lambda i: send.at[k, b + i]), (lambda i: recv.at[k, b + i])

        def add_own(acc_ref, land_ref, k=k):
            own[k].wait()
            add(acc_ref, land_ref)

        s, r = sems(2)
        peer = core.at(1 - 2 * c)
        other = part.at[k, 1 - c]
        chain = [Hop([(
            None, None,
            lambda other=other, s=s, r=r, k=k: remote(other, land_c.at[k], s(0), r(0), peer),
            lambda s=s, r=r, k=k: remote(land_c.at[k], land_c.at[k], s(0), r(0), peer),
            lambda k=k, add_own=add_own: add_own(acc.at[k], land_c.at[k]),
        )])]
        chain += reduce_hops(first, lambda i, k=k: acc.at[k, i], lambda i, k=k: land_p.at[k, i], add, *sems(first.size))
        chain += reduce_hops(second, lambda i, k=k: acc.at[k, p, i], lambda i, k=k: land_q.at[k, i], add, *sems(second.size))
        chain += reduce_hops(long, lambda i, k=k: acc.at[k, p, q, i], lambda i, k=k: land_z.at[k, i], add, *sems(long.size))
        chains.append(chain)
    flow(chains)
    for k in range(chunks):
        out[k] = acc[k, p, q, z]


def scatter_all(part, collective_id):
    groups, parts = lax.axis_size("grp"), lax.axis_size("ep")
    major, minor, xs = mesh_sizes(groups, parts)
    legs = sum(leg_count(n) for n in (2, xs, minor, major))
    chunks, width = part.shape[0], part.shape[-1]
    unit = 2 * ROWS * width
    need = unit * (2 * xs * minor * major + leg_count(xs) * minor * major + leg_count(minor) * major + leg_count(major) + 2)
    per = chunks
    while per > 1 and per * need > 44 * 2**20:
        per //= 2
    call = pl.pallas_call(
        functools.partial(scatter_kernel, groups, parts),
        out_shape=jax.ShapeDtypeStruct((per, ROWS, width), BF),
        in_specs=[pl.BlockSpec(memory_space=pl.ANY)],
        out_specs=pl.BlockSpec(memory_space=pltpu.VMEM),
        scratch_shapes=[
            pltpu.VMEM((per, xs, minor, major, ROWS, width), BF),
            pltpu.VMEM((per, xs, minor, major, ROWS, width), BF),
            pltpu.VMEM((per, leg_count(xs), minor, major, ROWS, width), BF),
            pltpu.VMEM((per, leg_count(minor), major, ROWS, width), BF),
            pltpu.VMEM((per, leg_count(major), ROWS, width), BF),
            pltpu.SemaphoreType.DMA((per,)),
            pltpu.SemaphoreType.DMA((per, legs)),
            pltpu.SemaphoreType.DMA((per, legs)),
        ],
        compiler_params=pltpu.CompilerParams(
            collective_id=collective_id, has_side_effects=True, vmem_limit_bytes=56 * 2**20
        ),
    )
    return jnp.concatenate([call(part[i:i + per]) for i in range(0, chunks, per)]) if per < chunks else call(part)


def total_kernel(groups, parts, spans, *refs):
    count = len(spans)
    ins, outs = refs[:count], refs[count:2 * count]
    acc, land_y, land_z = refs[2 * count:3 * count], refs[3 * count:4 * count], refs[4 * count:5 * count]
    local, stored, send, recv = refs[5 * count:]
    major, minor, _ = mesh_sizes(groups, parts)
    g = lax.axis_index("grp")
    short = Line(minor, lax.rem(g, minor), (1, 0))
    long = Line(major, lax.div(g, minor), (minor, 0))
    y, z = short.place, long.place
    loads, chains, number = [], [], 0
    for j in range(count):
        for k in range(spans[j]):
            load = pltpu.make_async_copy(ins[j].at[k], acc[j].at[k], local.at[number])
            load.start()
            loads.append(load)
            store = pltpu.make_async_copy(acc[j].at[k, y, z], outs[j].at[k, y, z], stored.at[number])
            base = [0]

            def sems(n, number=number, base=base):
                b = base[0]
                base[0] += leg_count(n)
                return (lambda i: send.at[number, b + i]), (lambda i: recv.at[number, b + i])

            down = reduce_hops(short, lambda i, j=j, k=k: acc[j].at[k, i], lambda i, j=j, k=k: land_y[j].at[k, i], add, *sems(minor))
            down += reduce_hops(long, lambda i, j=j, k=k: acc[j].at[k, y, i], lambda i, j=j, k=k: land_z[j].at[k, i], add, *sems(major))
            up = gather_hops(long, lambda i, j=j, k=k: outs[j].at[k, y, i], *sems(major))
            up += gather_hops(short, lambda i, j=j, k=k: outs[j].at[k, i], *sems(minor))
            chains.append((load, down, store, up))
            number += 1
    greet([short, long])
    whole = []
    for load, down, store, up in chains:
        hops = down + up
        turn = len(down)

        class Loaded:
            def __init__(self, hop, before):
                self.hop, self.before = hop, before

            def start(self):
                self.before()
                self.hop.start()

            def arrive(self):
                self.hop.arrive()

            def sent(self):
                self.hop.sent()

        def put(store=store):
            store.start()
            store.wait()

        hops[0] = Loaded(hops[0], load.wait)
        hops[turn] = Loaded(hops[turn], put)
        whole.append(hops)
    flow(whole)


def total_over_groups(arrays, spans, collective_id):
    groups, parts = lax.axis_size("grp"), lax.axis_size("ep")
    major, minor, _ = mesh_sizes(groups, parts)
    legs = 2 * (leg_count(minor) + leg_count(major))
    total = sum(spans)
    any_spec = pl.BlockSpec(memory_space=pl.ANY)
    scratch = [pltpu.VMEM(a.shape, BF) for a in arrays]
    scratch += [pltpu.VMEM((a.shape[0], leg_count(minor)) + a.shape[2:], BF) for a in arrays]
    scratch += [pltpu.VMEM((a.shape[0], leg_count(major)) + a.shape[3:], BF) for a in arrays]
    return pl.pallas_call(
        functools.partial(total_kernel, groups, parts, spans),
        out_shape=[jax.ShapeDtypeStruct(a.shape, BF) for a in arrays],
        in_specs=[any_spec] * len(arrays),
        out_specs=[any_spec] * len(arrays),
        scratch_shapes=scratch + [
            pltpu.SemaphoreType.DMA((total,)),
            pltpu.SemaphoreType.DMA((total,)),
            pltpu.SemaphoreType.DMA((total, legs)),
            pltpu.SemaphoreType.DMA((total, legs)),
        ],
        compiler_params=pltpu.CompilerParams(
            collective_id=collective_id, has_side_effects=True, vmem_limit_bytes=48 * 2**20
        ),
    )(*arrays)


def per_device(
    block_entry_states,
    document_labels,
    token_assignments,
    worker_quota_tallies,
    rescale_factors_both,
    triple_projection_matrix,
    probe_lookup_scalers,
    heads_merge_matrix,
    dispatcher_matrix,
    specialist_widen_matrix,
    specialist_shrink_matrix,
    output_gradient,
):
    micro, local_rows, width = block_entry_states.shape
    groups, parts = lax.axis_size("grp"), lax.axis_size("ep")
    major, minor, xs = mesh_sizes(groups, parts)
    group = lax.axis_index("grp")
    part = lax.axis_index("ep")
    seq_len = document_labels.shape[1]
    experts = dispatcher_matrix.shape[1]
    local_exp = specialist_widen_matrix.shape[0]
    inner = specialist_shrink_matrix.shape[1]
    share = inner // groups
    local_width = triple_projection_matrix.shape[2]
    heads = local_width // HD
    scale = 1.0 / math.sqrt(HD)
    gains = rescale_factors_both.astype(F32)
    head_gains = probe_lookup_scalers.astype(F32)
    cos, sin = rope_tables(seq_len, HD)
    signed_sin = jnp.concatenate([-sin[:, : HD // 2], sin[:, HD // 2:]], axis=-1)
    expert_ids = jnp.arange(experts, dtype=jnp.int32)

    hits = (token_assignments[..., None] == expert_ids).astype(jnp.int32)
    counts = jnp.sum(hits, axis=2)
    prior = jnp.cumsum(counts, axis=1) - counts
    keep = jnp.where((counts > 0) & (prior < worker_quota_tallies), 1.0, 0.0).astype(F32)
    keep_all = lax.all_gather(keep.astype(BF), ALL, axis=1, tiled=True).astype(F32)
    keep_all = keep_all.reshape(micro, major, minor, xs, 2, local_rows // ROWS, ROWS, experts)
    one = keep_all[:, :, :, :, 0].transpose(0, 4, 3, 2, 1, 5, 6)
    two = keep_all[:, :, :, :, 1].transpose(0, 4, 3, 2, 1, 5, 6)
    if xs == minor:
        two = keep_all[:, :, :, :, 1].transpose(0, 4, 2, 3, 1, 5, 6)
    keep_all = jnp.stack([one, two], axis=2).reshape(-1, experts)

    widen = specialist_widen_matrix.reshape(local_exp, width, 2, groups, share)
    widen = lax.dynamic_index_in_dim(widen, group, 3, keepdims=False)
    widen = widen.transpose(1, 2, 0, 3).reshape(width, 2 * local_exp * share)
    shrink = specialist_shrink_matrix.reshape(local_exp, groups, share, width)
    shrink = lax.dynamic_index_in_dim(shrink, group, 1, keepdims=False).reshape(local_exp * share, width)

    dy_all = gather_all(output_gradient, 0)
    chunk_shape = dy_all.shape[:-1]
    dy_all = dy_all.reshape(-1, width)

    skip = block_entry_states.astype(F32)
    inv_first = lax.rsqrt(jnp.mean(skip * skip, axis=-1, keepdims=True) + EPS)
    hat_first = skip * inv_first
    attn_in = (hat_first * gains[0]).astype(BF)
    gathered = lax.all_gather(attn_in, "ep", axis=1, tiled=True)
    projected = jnp.einsum("mtd,dcf->cmtf", gathered, triple_projection_matrix, preferred_element_type=F32)
    qk_raw = projected[:2]
    squares = lax.psum(jnp.sum(qk_raw * qk_raw, axis=-1), "ep")
    qk_inv = lax.rsqrt(squares / width + EPS)[..., None]
    qk_hat = qk_raw * qk_inv
    qk_n = (qk_hat * head_gains[:, None, None, :]).reshape(2, micro, seq_len, heads, HD).transpose(0, 1, 3, 2, 4)
    qk = (qk_n * cos + swap_halves(qk_n) * signed_sin).astype(BF)
    queries, keys = qk[0], qk[1]
    values = projected[2].astype(BF).reshape(micro, seq_len, heads, HD).transpose(0, 2, 1, 3)
    places = jnp.arange(seq_len, dtype=jnp.int32)
    allowed = (document_labels[:, :, None] == document_labels[:, None, :]) & (places[None, :] <= places[:, None])
    scores = jnp.einsum("mhsd,mhtd->mhst", queries, keys, preferred_element_type=F32) * scale
    scores = jnp.where(allowed[:, None], scores, NEG)
    exponent = jnp.exp(scores - jnp.max(scores, axis=-1, keepdims=True))
    weights = exponent / jnp.sum(exponent, axis=-1, keepdims=True)
    weights_low = weights.astype(BF)
    mixed = jnp.einsum("mhst,mhtd->mshd", weights_low, values, preferred_element_type=F32)
    mixed = mixed.astype(BF).reshape(micro, seq_len, local_width)
    attention = lax.psum_scatter(
        jnp.einsum("msf,fd->msd", mixed, heads_merge_matrix, preferred_element_type=F32).astype(BF),
        "ep", scatter_dimension=1, tiled=True,
    ).astype(F32)

    hidden = skip + attention
    inv_second = lax.rsqrt(jnp.mean(hidden * hidden, axis=-1, keepdims=True) + EPS)
    hat_second = hidden * inv_second
    ffn_in = (hat_second * gains[1]).astype(BF)
    x_all = gather_all(ffn_in, 1).reshape(-1, width)
    router = jax.nn.softmax(jnp.dot(x_all, dispatcher_matrix, preferred_element_type=F32), axis=-1)
    gate = lax.dynamic_slice_in_dim(router * keep_all, part * local_exp, local_exp, axis=1)
    gate = jnp.repeat(gate, share, axis=1)
    gate_up = jnp.dot(x_all, widen, preferred_element_type=F32)
    g, u = gate_up[:, : local_exp * share], gate_up[:, local_exp * share:]
    sigma = jax.nn.sigmoid(g)
    act = g * sigma * u
    gated = (gate * act).astype(BF)
    moe_part = jnp.dot(gated, shrink, preferred_element_type=F32).astype(BF)
    d_raw = lax.dot_general(dy_all, shrink, (((1,), (1,)), ((), ())), preferred_element_type=F32)
    d_gate = jnp.sum((act * d_raw).reshape(-1, local_exp, share), axis=-1)
    d_act = gate * d_raw
    d_gu = jnp.concatenate([d_act * u * sigma * (1.0 + g * (1.0 - sigma)), d_act * (g * sigma)], axis=1).astype(BF)
    dx_part = lax.dot_general(d_gu, widen, (((1,), (1,)), ((), ())), preferred_element_type=F32).astype(BF)
    lanes = jnp.arange(128, dtype=jnp.int32)
    place = (lanes[None, :] == part * local_exp + jnp.arange(local_exp, dtype=jnp.int32)[:, None])
    d_gate = jnp.sum(jnp.where(place[None], d_gate[:, :, None], 0.0), axis=1)
    dx_part = jnp.concatenate([dx_part, d_gate.astype(BF)], axis=1)
    dx_sum = scatter_all(dx_part.reshape(chunk_shape + (width + 128,)), 2).astype(F32)
    dx_sum = dx_sum.reshape(micro, local_rows, width + 128)
    grad_widen = lax.dot_general(x_all, d_gu, (((0,), (0,)), ((), ())), preferred_element_type=F32)
    grad_shrink = lax.dot_general(gated, dy_all, (((0,), (0,)), ((), ())), preferred_element_type=F32)
    grad_widen = grad_widen.astype(BF).reshape(groups, width // groups, 2, local_exp, share)
    grad_widen = lax.all_to_all(grad_widen, "grp", 0, 0, tiled=True)
    grad_widen = grad_widen.transpose(3, 1, 2, 0, 4).reshape(local_exp, width // groups, 2 * inner).astype(F32)
    grad_shrink = grad_shrink.reshape(local_exp, share, width)
    moe = scatter_all(moe_part.reshape(chunk_shape + (width,)), 3).astype(F32).reshape(micro, local_rows, width)
    output = (hidden + moe).astype(BF)

    probs = jax.nn.softmax(jnp.einsum("mtd,de->mte", ffn_in, dispatcher_matrix, preferred_element_type=F32), axis=-1)
    d_probs = dx_sum[..., width: width + experts] * keep
    d_logits = probs * (d_probs - jnp.sum(probs * d_probs, axis=-1, keepdims=True))
    d_ffn = dx_sum[..., :width] + jnp.einsum("mte,de->mtd", d_logits, dispatcher_matrix.astype(F32), precision=HIGH)
    grad_router = jnp.einsum("mtd,mte->ed", ffn_in.astype(F32), d_logits, precision=HIGH)
    scaled = d_ffn * gains[1]
    adjoint = output_gradient.astype(F32)
    d_hidden = adjoint + inv_second * (scaled - hat_second * jnp.mean(scaled * hat_second, axis=-1, keepdims=True))
    grad_second = jnp.sum(d_ffn * hat_second, axis=(0, 1))

    branch = lax.all_gather(d_hidden.astype(BF), "ep", axis=1, tiled=True)
    grad_out = jnp.einsum("msf,msd->fd", mixed, branch, preferred_element_type=F32)
    d_mixed = jnp.einsum("msd,fd->msf", branch, heads_merge_matrix, preferred_element_type=F32).astype(BF)
    d_mixed = d_mixed.reshape(micro, seq_len, heads, HD).transpose(0, 2, 1, 3)
    d_weights = jnp.einsum("mhsd,mhtd->mhst", d_mixed, values, preferred_element_type=F32)
    d_scores = (weights * (d_weights - jnp.sum(weights * d_weights, axis=-1, keepdims=True))).astype(BF)
    d_values = jnp.einsum("mhst,mhsd->mthd", weights_low, d_mixed, preferred_element_type=F32)
    d_queries = jnp.einsum("mhst,mhtd->mshd", d_scores, keys, preferred_element_type=F32) * scale
    d_keys = jnp.einsum("mhst,mhsd->mthd", d_scores, queries, preferred_element_type=F32) * scale
    d_qk = jnp.stack([d_queries, d_keys])
    d_qk = d_qk * cos[:, None] - swap_halves(d_qk) * signed_sin[:, None]
    d_qk = d_qk.reshape(2, micro, seq_len, local_width)
    scaled = d_qk * head_gains[:, None, None, :]
    inner_sums = lax.psum(jnp.sum(scaled * qk_hat, axis=-1), "ep")
    d_qk_raw = qk_inv * (scaled - qk_hat * (inner_sums / width)[..., None])
    grad_heads = jnp.sum(d_qk * qk_hat, axis=(1, 2))
    d_proj = jnp.concatenate([d_qk_raw, d_values.reshape(1, micro, seq_len, local_width)]).astype(BF)
    grad_qkv = jnp.einsum("mtd,cmtf->dcf", gathered, d_proj, preferred_element_type=F32)
    d_attn_in = lax.psum_scatter(
        jnp.einsum("cmtf,dcf->mtd", d_proj, triple_projection_matrix, preferred_element_type=F32).astype(BF),
        "ep", scatter_dimension=1, tiled=True,
    ).astype(F32)
    scaled = d_attn_in * gains[0]
    grad_input = d_hidden + inv_first * (scaled - hat_first * jnp.mean(scaled * hat_first, axis=-1, keepdims=True))
    grad_first = jnp.sum(d_attn_in * hat_first, axis=(0, 1))

    misc = jnp.concatenate([grad_first[None], grad_second[None], grad_router])
    misc = lax.psum(misc, "ep").reshape(-1)
    misc = jnp.concatenate([misc, grad_heads.reshape(-1)])
    small = major * minor * ROWS * 128
    misc_size = misc.shape[0]
    misc = jnp.pad(misc, (0, -misc_size % small)).reshape(1, minor, major, ROWS, -1).astype(BF)
    spans = 4
    qkv_cut = grad_qkv.astype(BF).reshape(spans, minor, major, -1, 3 * local_width)
    out_cut = grad_out.astype(BF).reshape(1, minor, major, -1, width)
    qkv_sum, out_sum, misc_sum = total_over_groups([qkv_cut, out_cut, misc], (spans, 1, 1), 4)
    qkv_sum = qkv_sum.reshape(grad_qkv.shape).astype(F32)
    out_sum = out_sum.reshape(grad_out.shape).astype(F32)
    misc_sum = misc_sum.reshape(-1)[:misc_size].astype(F32)
    rows = misc_sum[: (2 + experts) * width].reshape(2 + experts, width)
    return (
        output,
        grad_input,
        rows[:2],
        qkv_sum,
        misc_sum[(2 + experts) * width:].reshape(2, local_width),
        out_sum,
        rows[2:].T,
        grad_widen,
        grad_shrink,
    )


def solution(mesh):
    return jax.shard_map(
        per_device,
        mesh=mesh,
        in_specs=(
            P(None, ALL, None),
            P(None, "grp"),
            P(None, ALL, None),
            P(),
            P(),
            P(None, None, "ep"),
            P(None, "ep"),
            P("ep", None),
            P(),
            P("ep", None, None),
            P("ep", None, None),
            P(None, ALL, None),
        ),
        out_specs=(
            P(None, ALL, None),
            P(None, ALL, None),
            P(),
            P(None, None, "ep"),
            P(None, "ep"),
            P("ep", None),
            P(),
            P("ep", "grp", None),
            P("ep", "grp", None),
        ),
        check_vma=False,
    )
```

time: 2010 us -> 1310 us (0.65)
  waiting for transfers between devices: 1390 us -> 23.8 us
  Pallas kernels: 0 us -> 700 us
  local copies, waits for them, and re-layouts: 117 us -> 225 us
  matrix products: 275 us -> 172 us
  starting transfers between devices: 39.7 us -> 4.73 us
    reduce_scatter x6 -> x2, waiting for transfers between devices: 876 us -> 0.01 us  [the longest x1 0.01 us: per_device(): lax.psum_scatter(jnp.einsum('msf,fd->msd', mixed, heads_merge_matrix, pre...]
    pallas_call x0 -> x5, Pallas kernels: none -> 700 us  [the longest x2 256 us: scatter_all(): call(part)]
    psum x2 -> x0, waiting for transfers between devices: 268 us -> none  [the longest x1 147 us: per_device(): lax.psum(acc_qkv.astype(jnp.bfloat16), 'grp').astype(jnp.float32)]
    all_to_all x8 -> x1, waiting for transfers between devices: 191 us -> 0.01 us  [per_device(): grad_widen = lax.all_to_all(grad_widen, 'grp', 0, 0, tiled=True)]
    dot_general x46 -> x20, matrix products: 275 us -> 169 us  [the longest x1 25.3 us: per_device(): lax.dot_general(d_gu, widen, (((1,), (1,)), ((), ())), preferred_element_...]
    convert_element_type x2 -> x7, local copies, waits for them, and re-layouts: 0.85 us -> 66 us  [the longest x1 27.3 us: per_device(): grad_qkv.astype(BF).reshape(spans, minor, major, -1, 3 * local_width)]
    unnamed x313 -> x102, local copies, waits for them, and re-layouts: 15.4 us -> 71.7 us
    psum x4 -> x3, blocking collectives: 73.2 us -> 27 us  [the longest x1 14.5 us: per_device(): misc = lax.psum(misc, 'ep').reshape(-1)]
  transfers between devices with their start and end apart: 20 -> 5, of which waited for: 18 -> 1; matrix products, arithmetic and copies ran while one was open for 14% -> 17% of each run, Pallas kernels for 0% -> 36%
where the time goes in v1:
time: 1310 us; the launch traced here: 1300 us
  Pallas kernels  700 us (53%)
  local copies, waits for them, and re-layouts  225 us (17%)
  matrix products  172 us (13%)
  other arithmetic  87.4 us (7%)
  blocking collectives  72.1 us (6%)
  waiting for transfers between devices  23.8 us (2%)
  between operations  14.9 us (1%)
    pallas_call x2, Pallas kernels, scatter_all(): call(part)  256 us
    pallas_call x2, Pallas kernels, gather_all(): pl.pallas_call(functools.partial(gather_kernel, groups, parts), out_shape...  252 us
    pallas_call x1, Pallas kernels, total_over_groups(): pl.pallas_call(functools.partial(total_kernel, groups, parts, spans), out...  191 us
    unnamed x102, local copies, waits for them, and re-layouts  71.7 us
    all_gather x1, blocking collectives, per_device(): lax.all_gather(keep.astype(BF), ALL, axis=1, tiled=True).astype(F32)  45.1 us
    convert_element_type x1, local copies, waits for them, and re-layouts, per_device(): grad_qkv.astype(BF).reshape(spans, minor, major, -1, 3 * local_width)  27.3 us
  transfers between devices with their start and end apart: 5, of which 1 were waited for; matrix products, arithmetic and copies ran while one was open for 17% of the time, Pallas kernels for 36%

profile of v1, /device:TPU:0, one launch (start us, length us, event | category | flops | bytes accessed | tf_op | source)
XLA Modules:
  0.0 1300.3 jit_solution(17490043983197833331)
XLA Ops:
  13.8 23.7 %all-gather.3.cloned.1.call-done = bf16[2,256,2048]{2,1,0:T(8,128)(2,1)} async-done(((bf16[2,64,2048]{2,1,0:T(8,128)(2,1)}), bf16[2,256,2048]{2,1,0:T(8,128)(2,1)}) %all-gather.3.cloned.1.call-update) | async-done | bytes 2097168 | tf_op jit(solution)/shard_map/all_gather | solution.py:485
  75.4 45.1 %all_gather.10 = bf16[2,2048,16]{2,0,1:T(2,128)(2,1)S(1)} all-gather(bf16[2,64,16]{2,0,1:T(2,128)(2,1)S(1)} %copy.206), channel_id=1, replica_groups=mesh['grp'=8,'ep'=4] {'grp','ep'}, dimensions={1}, use_global_device_ids=true | all-gather | bytes 135168 | tf_op jit(solution)/shard_map/all_gather | solution.py:463
  134.9 42.7 %copy.209 = bf16[4,2048,2048]{1,2,0:T(8,128)(2,1)} copy(bf16[4,2048,2048]{2,1,0:T(8,128)(2,1)} %param.21) | data formatting | bytes 67108864 | tf_op args[9]
  182.4 126.1 %shard_map.189 = bf16[8,2,2,2,4,16,2048]{6,5,4,3,2,1,0:T(8,128)(2,1)} custom-call(bf16[8,16,2048]{2,1,0:T(8,128)(2,1)} %bitcast.238), custom_call_target="tpu_custom_call" | custom-call | tf_op jit(solution)/shard_map/pallas_call | solution.py:255
  316.4 126.3 %shard_map.187 = bf16[8,2,2,2,4,16,2048]{6,5,4,3,2,1,0:T(8,128)(2,1)} custom-call(bf16[8,16,2048]{2,1,0:T(8,128)(2,1)} %bitcast.237), custom_call_target="tpu_custom_call" | custom-call | tf_op jit(solution)/shard_map/pallas_call | solution.py:255
  443.1 10.4 fusion.76
  453.6 21.8 %fusion.80 = f32[4096,1024]{0,1:T(8,128)} fusion(bf16[4096,2048]{1,0:T(8,128)(2,1)S(1)} %bitcast.223, bf16[2048,1024]{0,1:T(8,128)(2,1)} %bitcast.240), kind=kOutput, calls=%fused_computation.159 | convolution fusion | flops 17179869184 | bytes 37748736 | tf_op jit(solution)/shard_map/dot_general | solution.py:517
  475.5 19.7 %bitcast_reduce_fusion = (f32[4096,4]{0,1:T(4,128)S(1)}, f32[512,4096]{1,0:T(8,128)}) fusion(f32[4096,1024]{0,1:T(8,128)} %fusion.80, bf16[512,2048]{1,0:T(8,128)(2,1)} %bitcast.246, bf16[4096,2048]{1,0:T(8,128)(2,1)} %bitcast.232), kind=kOutput, calls=%fused_computation.10 | convolution fusion | flops 8604598272 | bytes 44105728 | tf_op jit(solution)/shard_map/dot_general | solution.py:523
  505.9 14.4 %multiply_convert_fusion.1 = (bf16[4096,512]{0,1:T(8,128)(2,1)}, bf16[4096,512]{0,1:T(8,128)(2,1)}, bf16[4096,512]{0,1:T(8,128)(2,1)}) fusion(f32[512,4096]{1,0:T(8,128)} %get-tuple-element.107, f32[4096,1024]{0,1:T(8,128)} %fusion.80, f32[4096,4]{0,1:T(4,128)S(1)} %divide_multiply_fusion), kind=kLoop, calls=%fused_computation.15 | loop fusion | flops 35651584 | bytes 37814272 | tf_op jit(solution)/shard_map/convert.18
  520.3 25.3 %convolution_convert_fusion = bf16[4096,2048]{0,1:T(8,128)(2,1)} fusion(bf16[2048,1024]{0,1:T(8,128)(2,1)} %bitcast.241, bf16[4096,512]{0,1:T(8,128)(2,1)} %get-tuple-element.90, bf16[4096,512]{0,1:T(8,128)(2,1)} %get-tuple-element.89), kind=kOutput, calls=%fused_computation.3 | convolution fusion | flops 17205035008 | bytes 29360128 | tf_op jit(solution)/shard_map/dot_general | solution.py:527
  545.6 19.0 %pad_maximum_fusion = bf16[4096,2176]{0,1:T(8,128)(2,1)} fusion(bf16[4096,128]{0,1:T(8,128)(2,1)} %copy.212, bf16[4096,2048]{0,1:T(8,128)(2,1)} %convolution_convert_fusion), kind=kLoop, calls=%fused_computation.2 | loop fusion | flops 35651584 | bytes 35651584 | tf_op jit(solution)/shard_map/concatenate | solution.py:531
  564.6 22.2 %copy.213 = bf16[4096,2176]{1,0:T(8,128)(2,1)} copy(bf16[4096,2176]{0,1:T(8,128)(2,1)} %pad_maximum_fusion) | data formatting | bytes 35651584 | tf_op jit(solution)/shard_map/concatenate | solution.py:531
  586.8 109.7 %shard_map.190 = bf16[8,16,2176]{2,1,0:T(8,128)(2,1)} custom-call(bf16[8,2,2,2,4,16,2176]{6,5,4,3,2,1,0:T(8,128)(2,1)} %bitcast.220), custom_call_target="tpu_custom_call" | custom-call | tf_op jit(solution)/shard_map/pallas_call | solution.py:337
  703.4 23.9 %fusion.9 = bf16[2048,1024]{1,0:T(8,128)(2,1)} fusion(bf16[4096,2048]{1,0:T(8,128)(2,1)} %bitcast.222, bf16[4096,512]{0,1:T(8,128)(2,1)} %get-tuple-element.90, bf16[4096,512]{0,1:T(8,128)(2,1)} %get-tuple-element.89), kind=kOutput, calls=%fused_computation.27 | convolution fusion | flops 17198743552 | bytes 29360128 | tf_op jit(solution)/shard_map/dot_general | solution.py:534
  739.6 15.4 %convolution_convert_fusion.1 = bf16[4096,2048]{1,0:T(8,128)(2,1)} fusion(bf16[4096,512]{0,1:T(8,128)(2,1)} %get-tuple-element.91, bf16[512,2048]{1,0:T(8,128)(2,1)} %bitcast.247), kind=kOutput, calls=%fused_computation.4 | convolution fusion | flops 8598323200 | bytes 23068672 | tf_op jit(solution)/shard_map/dot_general | solution.py:522
  755.0 146.8 %shard_map.188 = bf16[8,16,2048]{2,1,0:T(8,128)(2,1)} custom-call(bf16[8,2,2,2,4,16,2048]{6,5,4,3,2,1,0:T(8,128)(2,1)} %bitcast.234), custom_call_target="tpu_custom_call" | custom-call | tf_op jit(solution)/shard_map/pallas_call | solution.py:337
  947.8 15.3 %fusion.81 = f32[4,128,2048]{2,1,0:T(8,128)} fusion(bf16[4,128,4096]{2,1,0:T(8,128)(2,1)} %bitcast.239, bf16[4096,2048,1]{1,0,2:T(8,128)(2,1)} %bitcast.233), kind=kOutput, calls=%fused_computation.160 | convolution fusion | flops 8589934592 | bytes 25165824 | tf_op jit(solution)/shard_map/dot_general | solution.py:535
  967.1 27.3 %copy.228 = bf16[2048,3,512]{2,1,0:T(4,128)(2,1)} copy(bf16[2048,3,512]{2,0,1:T(8,128)(2,1)S(1)} %bitcast_convert_fusion) | data formatting | bytes 12582912 | tf_op jit(solution)/shard_map/convert_element_type | solution.py:586
  994.5 17.9 %reshape.312.refs_0_ = bf16[4,2,4,64,1536]{4,3,2,1,0:T(8,128)(2,1)} reshape(bf16[2048,3,512]{2,1,0:T(4,128)(2,1)} %copy.228) | data formatting | bytes 12582912 | tf_op jit(solution)/shard_map/reshape | solution.py:586
  1018.1 14.5 %all-reduce.2 = bf16[18,2048]{1,0:T(8,128)(2,1)S(1)} all-reduce(f32[18,2048]{1,0:T(8,128)S(1)} %pad_maximum_fusion.11), channel_id=1, replica_groups=mesh['grp'=8,'ep'=4] {'ep'}, use_global_device_ids=true, to_apply=%region_24.25 | all-reduce | flops 36864 | bytes 221184 | tf_op jit(solution)/shard_map/psum | solution.py:580
  1034.3 191.0 %shard_map.191 = (bf16[4,2,4,64,1536]{4,3,2,1,0:T(8,128)(2,1)}, bf16[1,2,4,64,2048]{4,3,2,1,0:T(8,128)(2,1)S(1)}, bf16[1,2,4,16,384]{4,3,2,1,0:T(8,128)(2,1)S(1)}) custom-call(bf16[4,2,4,64,1536]{4,3,2,1,0:T(8,128)(2,1)} %reshape.312.refs_0_, bf16[1,2,4,64,2048]{4,3,2,1,0:T(8,128)(2,1)S(1)} %bitcast.219, ...), custom_call_target="tpu_custom_call" | custom-call | tf_op jit(solution)/shard_map/pallas_call | solution.py:409
  1239.0 9.2 reshape.326
  1248.3 20.0 %reshape.324 = f32[2048,3,512]{2,1,0:T(4,128)} reshape(bf16[4,2,4,64,1536]{4,3,2,1,0:T(8,128)(2,1)} %get-tuple-element.13) | data formatting | bytes 18874368 | tf_op jit(solution)/shard_map/convert_element_type | solution.py:589
  1268.2 14.6 %copy.230 = f32[2048,3,512]{2,0,1:T(8,128)} copy(f32[2048,3,512]{2,1,0:T(4,128)} %reshape.324) | data formatting | bytes 25165824
  (212 shorter events, 183.2 us)
Async XLA Ops:
  7.2 64.5 %copy-start = (bf16[512,2048]{1,0:T(8,128)(2,1)S(1)}, bf16[512,2048]{1,0:T(8,128)(2,1)}, u32[]{:S(2)}) copy-start(bf16[512,2048]{1,0:T(8,128)(2,1)} %param.19) | copy-start | bytes 6291460
  7.2 6.4 copy-start.43
  7.2 30.2 %all-gather.3.cloned.1.call-start = ((), (), s32[]{:S(2)}) async-start(), calls=%async_computation.3 | async-start | bytes 2621440 | tf_op jit(solution)/shard_map/all_gather | solution.py:485
  8.1 692.9 %copy-start.25 = (f32[1,2048]{1,0:T(1,128)}, f32[1,2048]{1,0:T(1,128)S(1)}, u32[]{:S(2)}) copy-start(f32[1,2048]{1,0:T(1,128)S(1)} %get-tuple-element.102) | copy-start | bytes 24580
  12.0 301.1 %reduce-scatter.3.cloned.1.call-start = ((), (), s32[]{:S(2)}) async-start(), calls=%async_computation.4 | async-start | bytes 2621440 | tf_op jit(solution)/shard_map/reduce_scatter | solution.py:504
  12.7 38.6 %copy-start.30 = (f32[2,512]{1,0:T(2,128)}, f32[2,512]{1,0:T(2,128)S(1)}, u32[]{:S(2)}) copy-start(f32[2,512]{1,0:T(2,128)S(1)} %convert_element_type.127) | copy-start | bytes 12292
  74.3 827.9 %all-gather.5.cloned.1.call-start = ((), (), s32[]{:S(2)}) async-start(), calls=%async_computation.5 | async-start | bytes 2621440 | tf_op jit(solution)/shard_map/all_gather | solution.py:553
  314.4 386.7 %copy-start.34 = (f32[2,64]{1,0:T(2,128)}, f32[2,64]{1,0:T(2,128)S(1)}, u32[]{:S(2)}) copy-start(f32[2,64]{1,0:T(2,128)S(1)} %add_rsqrt_fusion.1) | copy-start | bytes 1540
  316.4 126.3 %copy-start.11 = (bf16[2,64,2048]{2,1,0:T(8,128)(2,1)S(1)}, bf16[2,64,2048]{2,1,0:T(8,128)(2,1)}, u32[]{:S(2)}) copy-start(bf16[2,64,2048]{2,1,0:T(8,128)(2,1)} %multiply_convert_fusion.4) | copy-start | bytes 1572868
  316.4 126.3 %copy-start.22 = (bf16[2048,16]{0,1:T(8,128)(2,1)S(1)}, bf16[2048,16]{0,1:T(8,128)(2,1)}, u32[]{:S(2)}) copy-start(bf16[2048,16]{0,1:T(8,128)(2,1)} %param.20) | copy-start | bytes 196612
  443.1 10.6 copy-start.3
  586.8 111.9 %copy-start.29 = (pred[2,64,16]{1,2,0:T(8,128)(4,1)S(1)}, pred[2,64,16]{1,2,0:T(8,128)(4,1)}, u32[]{:S(2)}) copy-start(pred[2,64,16]{1,2,0:T(8,128)(4,1)} %get-tuple-element.88) | copy-start | bytes 6148
  586.8 112.0 %copy-start.8 = (bf16[2,64,2048]{2,1,0:T(8,128)(2,1)S(1)}, bf16[2,64,2048]{2,1,0:T(8,128)(2,1)}, u32[]{:S(2)}) copy-start(bf16[2,64,2048]{2,1,0:T(8,128)(2,1)} %reduce-scatter.3.cloned.1.call-done) | copy-start | bytes 1572868
  701.0 26.2 %copy-start.38 = (f32[2,64]{1,0:T(2,128)}, f32[2,64]{1,0:T(2,128)S(1)}, u32[]{:S(2)}) copy-start(f32[2,64]{1,0:T(2,128)S(1)} %broadcast_multiply_fusion.2) | copy-start | bytes 1540
  735.0 492.5 %all-to-all-start = ((bf16[8,256,2,4,128]{4,3,2,1,0:T(4,128)(2,1)}), bf16[8,256,2,4,128]{4,3,2,1,0:T(4,128)(2,1)}, u32[]{:S(2)}, u32[]{:S(2)}) async-start(bf16[8,256,2,4,128]{4,3,2,1,0:T(4,128)(2,1)} %reshape.317), calls=%async_computation.2 | async-start | bytes 8388608 | tf_op jit(solution)/shard_map/all_to_all | solution.py:537
  739.5 277.0 %reduce-scatter.5.cloned.1.call-start = ((), (), s32[]{:S(2)}) async-start(), calls=%async_computation.6 | async-start | bytes 2621440 | tf_op jit(solution)/shard_map/reduce_scatter | solution.py:571
  755.0 146.8 %copy-start.12 = (bf16[2,64,2048]{2,1,0:T(8,128)(2,1)S(1)}, bf16[2,64,2048]{2,1,0:T(8,128)(2,1)}, u32[]{:S(2)}) copy-start(bf16[2,64,2048]{2,1,0:T(8,128)(2,1)} %multiply_convert_fusion.4) | copy-start | bytes 1572868
  947.8 15.4 %copy-start.20 = (bf16[2,2,256,512]{3,2,0,1:T(8,128)(2,1)S(1)}, bf16[2,2,256,512]{3,2,0,1:T(8,128)(2,1)}, u32[]{:S(2)}) copy-start(bf16[2,2,256,512]{3,2,0,1:T(8,128)(2,1)} %copy-done.19) | copy-start | bytes 3145732
  947.8 15.4 %copy-start.45 = (bf16[2,256,2048]{2,1,0:T(8,128)(2,1)S(1)}, bf16[2,256,2048]{2,1,0:T(8,128)(2,1)}, u32[]{:S(2)}) copy-start(bf16[2,256,2048]{2,1,0:T(8,128)(2,1)} %all-gather.3.cloned.1.call-done) | copy-start | bytes 6291460
  994.5 17.9 %copy-start.47 = (bf16[2,4,128,256]{3,2,1,0:T(8,128)(2,1)S(1)}, bf16[2,4,128,256]{3,2,1,0:T(8,128)(2,1)}, u32[]{:S(2)}) copy-start(bf16[2,4,128,256]{3,2,1,0:T(8,128)(2,1)} %copy-done.46) | copy-start | bytes 1572868
  1282.8 6.8 copy-start.9
  1282.8 6.8 copy-start.26
  1282.8 6.8 copy-start.35
  1282.8 6.8 copy-start.39
  (31 other events, 93.1 us)
Sparse Core Ops, SparseCore 0:
  12.1 25.2 all-gather.2
  74.4 36.5 reduce-scatter.2
  703.5 21.4 all-gather.4
  947.9 30.3 reduce-scatter.4

commit v2 on v1

--- a/solution.py
+++ b/solution.py
@@ -84,6 +84,15 @@
 
                 peers = peers + there.astype(jnp.int32)
     pl.semaphore_wait(barrier, peers)
+
+
+def greet_lines(some):
+    barrier = pltpu.get_barrier_semaphore()
+    for line in some:
+        for j in range(1, line.size):
+            to = lax.rem(line.place + j, line.size)
+            pl.semaphore_signal(barrier, inc=1, device_id=line.at(to - line.place), device_id_type=MESH)
+    pl.semaphore_wait(barrier, sum(line.size - 1 for line in some))
 
 
 def remote(src, dst, send, recv, target):
@@ -421,6 +430,397 @@
             collective_id=collective_id, has_side_effects=True, vmem_limit_bytes=48 * 2**20
         ),
     )(*arrays)
+
+
+def swap_legs(line, source, target, send, recv):
+    n, a = line.size, line.place
+    legs = []
+    for j in range(1, n):
+        to, off = lax.rem(a + j, n), lax.rem(a + n - j, n)
+        legs.append((
+            lambda to=to, j=j: remote(source(to), target(j - 1, a), send(j - 1), recv(j - 1), line.at(to - a)),
+            lambda off=off, j=j: remote(target(j - 1, off), target(j - 1, off), send(j - 1), recv(j - 1), line.at(off - a)),
+        ))
+    return legs
+
+
+def start_legs(legs):
+    for out, _ in legs:
+        out().start()
+
+
+def end_legs(legs):
+    for out, into in legs:
+        into().wait_recv()
+    for out, into in legs:
+        out().wait_send()
+
+
+def add_rows(acc, first, land, rows):
+    @pl.loop(0, rows // ROWS)
+    def _(i):
+        here = pl.ds(pl.multiple_of(first + i * ROWS, ROWS), ROWS)
+        there = pl.ds(pl.multiple_of(i * ROWS, ROWS), ROWS)
+        acc[here, :] = (acc[here, :].astype(F32) + land[there, :].astype(F32)).astype(acc.dtype)
+
+
+def experts_kernel(
+    groups, parts, local_rows, ring, acc_ring, experts,
+    x, dy, widen, shrink, dispatch, keep,
+    summed, moe, grad_widen, grad_shrink,
+    xs, dys, wide, down, sum_wide, sum_down, stage, acc, other, land_c, land_p, land_q, land_z,
+    hid, raw, gated, d_gu, gate, d_gate,
+    load, dy_sem, stage_sem, g_send, g_recv, s_send, s_recv,
+):
+    core, first, second, long = lines(groups, parts)
+    c, p, q, z = core.place, first.place, second.place, long.place
+    pn, qn, zn = first.size, second.size, long.size
+    chunks, _, width = x.shape
+    local_exp, inner = shrink.shape[0], shrink.shape[1]
+    share = inner // groups
+    group, part = lax.axis_index("grp"), lax.axis_index("ep")
+    rz, rq, rp, rc = ROWS, ROWS * zn, ROWS * zn * qn, ROWS * zn * qn * pn
+    rows = 2 * rc
+    cuts = local_rows // ROWS
+    base = part * local_exp
+    pairs = local_exp // 2
+
+    loads = []
+    for e in range(local_exp):
+        for half in range(2):
+            to = (e // 2) * 4 * share + half * 2 * share + (e % 2) * share
+            loads.append(pltpu.make_async_copy(
+                widen.at[e, :, pl.ds(pl.multiple_of(half * inner + group * share, share), share)],
+                wide.at[:, pl.ds(to, share)], load.at[2 * e + half]))
+        loads.append(pltpu.make_async_copy(
+            shrink.at[e, pl.ds(pl.multiple_of(group * share, share), share), :],
+            down.at[pl.ds(e * share, share), :], load.at[2 * local_exp + e]))
+    for copy in loads:
+        copy.start()
+
+    def dy_start(k):
+        m, r = lax.div(k, cuts), lax.rem(k, cuts)
+        for cc in range(2):
+            for pp in range(pn):
+                for qq in range(qn):
+                    for zz in range(zn):
+                        xx, yy = (pp, qq) if (cc == 0 or pn != qn) else (qq, pp)
+                        device = (zz * (groups // zn) + yy) * parts + xx * 2 + cc
+                        pltpu.make_async_copy(
+                            dy.at[m, pl.ds(pl.multiple_of(device * local_rows + r * ROWS, ROWS), ROWS), :],
+                            dys.at[lax.rem(k, 2), pl.ds((((cc * pn + pp) * qn + qq) * zn + zz) * ROWS, ROWS), :],
+                            dy_sem.at[lax.rem(k, 2)],
+                        ).start()
+
+    dy_start(0)
+    greet_lines([core, first, second, long])
+    sum_wide[...] = jnp.zeros_like(sum_wide)
+    sum_down[...] = jnp.zeros_like(sum_down)
+
+    def rows_at(start, size):
+        return pl.ds(pl.multiple_of(start, ROWS), size)
+
+    def g_long(k):
+        buf = xs.at[lax.rem(k, ring)]
+        return swap_legs(
+            long, lambda i: x.at[k], lambda j, i: buf.at[rows_at(c * rc + p * rp + q * rq + i * rz, rz), :],
+            lambda j: g_send.at[k, j], lambda j: g_recv.at[k, j])
+
+    def g_line(k, line, at, offset):
+        return swap_legs(line, lambda i: at(line.place), lambda j, i: at(i),
+                         lambda j: g_send.at[k, offset + j], lambda j: g_recv.at[k, offset + j])
+
+    def g_second(k):
+        buf = xs.at[lax.rem(k, ring)]
+        return g_line(k, second, lambda i: buf.at[rows_at(c * rc + p * rp + i * rq, rq), :], zn - 1)
+
+    def g_first(k):
+        buf = xs.at[lax.rem(k, ring)]
+        return g_line(k, first, lambda i: buf.at[rows_at(c * rc + i * rp, rp), :], zn + qn - 2)
+
+    def g_core(k):
+        buf = xs.at[lax.rem(k, ring)]
+        return g_line(k, core, lambda i: buf.at[rows_at(i * rc, rc), :], zn + qn + pn - 3)
+
+    def s_line(k, line, at, land, offset):
+        return swap_legs(line, at, lambda j, i: land.at[lax.rem(k, 2), j],
+                         lambda j: s_send.at[k, offset + j], lambda j: s_recv.at[k, offset + j])
+
+    def s_core(k):
+        return s_line(k, core, lambda i: other, land_c, 0)
+
+    def s_first(k):
+        buf = acc.at[lax.rem(k, acc_ring)]
+        return s_line(k, first, lambda i: buf.at[rows_at(i * rp, rp), :], land_p, 1)
+
+    def s_second(k):
+        buf = acc.at[lax.rem(k, acc_ring)]
+        return s_line(k, second, lambda i: buf.at[rows_at(p * rp + i * rq, rq), :], land_q, pn)
+
+    def s_long(k):
+        buf = acc.at[lax.rem(k, acc_ring)]
+        return s_line(k, long, lambda i: buf.at[rows_at(p * rp + q * rq + i * rz, rz), :], land_z, pn + qn - 1)
+
+    def after(t, lag, act):
+        k = t - lag
+
+        @pl.when((k >= 0) & (k < chunks))
+        def _():
+            act(k)
+
+    lane = lax.broadcasted_iota(jnp.int32, (1, 128), 1)
+
+    def compute(k):
+        buf, dyk = xs.at[lax.rem(k, ring)], dys.at[lax.rem(k, 2)]
+
+        @pl.when(k == 0)
+        def _():
+            for copy in loads:
+                copy.wait()
+
+        pltpu.make_async_copy(moe.at[0], dyk, dy_sem.at[lax.rem(k, 2)]).wait()
+
+        @pl.when(k + 1 < chunks)
+        def _():
+            dy_start(k + 1)
+
+        hid[:, :128] = jnp.dot(buf[...], dispatch[...], preferred_element_type=F32)
+
+        @pl.loop(0, rows // 64)
+        def _(i):
+            here = pl.ds(pl.multiple_of(i * 64, 64), 64)
+            logits = jnp.where(lane < experts, hid[here, :128], NEG)
+            grown = jnp.exp(logits - jnp.max(logits, axis=-1, keepdims=True))
+            probs = grown / jnp.sum(grown, axis=-1, keepdims=True)
+            gate[here, :] = probs * keep[k, here, :].astype(F32)
+            d_gate[here, :] = jnp.zeros((64, 128), F32)
+
+        @pl.loop(0, pairs)
+        def _(j):
+            cols = pl.ds(pl.multiple_of(j * 4 * share, 4 * share), 4 * share)
+            some = pl.ds(pl.multiple_of(j * 2 * share, 2 * share), 2 * share)
+            hid[...] = jnp.dot(buf[...], wide[:, cols], preferred_element_type=F32)
+            raw[...] = lax.dot_general(dyk[...], down[some, :], (((1,), (1,)), ((), ())), preferred_element_type=F32)
+
+            @pl.loop(0, rows // 32)
+            def _(i):
+                here = pl.ds(pl.multiple_of(i * 32, 32), 32)
+                gates = gate[here, :]
+                marks = d_gate[here, :]
+                for e in range(2):
+                    mark = lane == base + 2 * j + e
+                    weight = jnp.sum(jnp.where(mark, gates, 0.0), axis=-1, keepdims=True)
+                    g = hid[here, e * share: (e + 1) * share]
+                    u = hid[here, (2 + e) * share: (3 + e) * share]
+                    d = raw[here, e * share: (e + 1) * share]
+                    sigma = jax.nn.sigmoid(g)
+                    swish = g * sigma
+                    act = swish * u
+                    marks = marks + jnp.where(mark, jnp.sum(act * d, axis=-1, keepdims=True), 0.0)
+                    d = d * weight
+                    gated[here, pl.ds(pl.multiple_of(j * 2 * share + e * share, share), share)] = (act * weight).astype(BF)
+                    d_gu[here, pl.ds(pl.multiple_of(j * 4 * share + e * share, share), share)] = (
+                        d * u * (sigma + swish * (1.0 - sigma))).astype(BF)
+                    d_gu[here, pl.ds(pl.multiple_of(j * 4 * share + (2 + e) * share, share), share)] = (d * swish).astype(BF)
+                d_gate[here, :] = marks
+
+        tiles = width // 512
+
+        def input_grads(half, to):
+            here = pl.ds(pl.multiple_of(half * rc, rc), rc)
+
+            @pl.loop(0, tiles)
+            def _(n):
+                cols = pl.ds(pl.multiple_of(n * 512, 512), 512)
+                to[:, cols] = lax.dot_general(
+                    d_gu[here, :], wide[cols, :], (((1,), (1,)), ((), ())), preferred_element_type=F32).astype(BF)
+
+            to[:, width:] = d_gate[here, :].astype(BF)
+
+        input_grads(1 - c, other)
+        start_legs(s_core(k))
+        input_grads(c, acc.at[lax.rem(k, acc_ring)])
+        slot = lax.rem(k, 2)
+
+        @pl.when(k >= 2)
+        def _():
+            pltpu.make_async_copy(stage.at[slot], moe.at[k - 2], stage_sem.at[slot]).wait()
+
+        @pl.loop(0, tiles)
+        def _(n):
+            cols = pl.ds(pl.multiple_of(n * 512, 512), 512)
+            stage[slot, :, cols] = jnp.dot(gated[...], down[:, cols], preferred_element_type=F32).astype(BF)
+            sum_wide[cols, :] += lax.dot_general(
+                buf[:, cols], d_gu[...], (((0,), (0,)), ((), ())), preferred_element_type=F32)
+            sum_down[:, cols] += lax.dot_general(
+                gated[...], dyk[:, cols], (((0,), (0,)), ((), ())), preferred_element_type=F32)
+
+        pltpu.make_async_copy(stage.at[slot], moe.at[k], stage_sem.at[slot]).start()
+
+    def end_long(k):
+        end_legs(s_long(k))
+        buf = acc.at[lax.rem(k, acc_ring)]
+        total = buf[rows_at(p * rp + q * rq + z * rz, rz), :].astype(F32)
+        for j in range(zn - 1):
+            total = total + land_z[lax.rem(k, 2), j].astype(F32)
+        summed[k] = total.astype(BF)
+
+    def end_second(k):
+        end_legs(s_second(k))
+        for j in range(qn - 1):
+            add_rows(acc.at[lax.rem(k, acc_ring)], p * rp + q * rq, land_q.at[lax.rem(k, 2), j], rq)
+        start_legs(s_long(k))
+
+    def end_first(k):
+        end_legs(s_first(k))
+        for j in range(pn - 1):
+            add_rows(acc.at[lax.rem(k, acc_ring)], p * rp, land_p.at[lax.rem(k, 2), j], rp)
+        start_legs(s_second(k))
+
+    def end_core(k):
+        end_legs(s_core(k))
+        add_rows(acc.at[lax.rem(k, acc_ring)], 0, land_c.at[lax.rem(k, 2), 0], rc)
+        start_legs(s_first(k))
+
+    def begin(k):
+        xs[lax.rem(k, ring), rows_at(c * rc + p * rp + q * rq + z * rz, rz), :] = x[k]
+        start_legs(g_long(k))
+
+    def then(one, two):
+        def act(k):
+            end_legs(one(k))
+            start_legs(two(k))
+
+        return act
+
+    @pl.loop(0, chunks + 8)
+    def _(t):
+        after(t, 8, end_long)
+        after(t, 7, end_second)
+        after(t, 6, end_first)
+        after(t, 5, end_core)
+        after(t, 4, lambda k: end_legs(g_core(k)))
+        after(t, 3, then(g_first, g_core))
+        after(t, 2, then(g_second, g_first))
+        after(t, 1, then(g_long, g_second))
+        after(t, 0, begin)
+        after(t, 4, compute)
+
+    out_down = pltpu.make_async_copy(sum_down, grad_shrink, load.at[0])
+    out_down.start()
+    for k in range(chunks - 2, chunks):
+        pltpu.make_async_copy(stage.at[k % 2], moe.at[k], stage_sem.at[k % 2]).wait()
+    for i in range(width // rows):
+        here = pl.ds(i * rows, rows)
+        if i:
+            pltpu.make_async_copy(d_gu, grad_widen.at[here, :], load.at[1]).wait()
+        d_gu[...] = sum_wide[here, :].astype(BF)
+        pltpu.make_async_copy(d_gu, grad_widen.at[here, :], load.at[1]).start()
+    pltpu.make_async_copy(d_gu, grad_widen.at[pl.ds(0, rows), :], load.at[1]).wait()
+    out_down.wait()
+
+
+def experts_together(x, dy, widen, shrink, dispatch, keep, collective_id):
+    experts = keep.shape[-1]
+    dispatch = jnp.pad(dispatch, ((0, 0), (0, 128 - experts)))
+    keep = jnp.pad(keep, ((0, 0), (0, 0), (0, 128 - experts)))
+    groups, parts = lax.axis_size("grp"), lax.axis_size("ep")
+    major, minor, xn = mesh_sizes(groups, parts)
+    micro, local_rows, width = x.shape
+    x = x.reshape(-1, ROWS, width)
+    chunks = x.shape[0]
+    local_exp, inner = shrink.shape[:2]
+    share = inner // groups
+    hidden = local_exp * share
+    half = ROWS * major * minor * xn
+    rows, wide = 2 * half, width + 128
+    ring, acc_ring = min(chunks, 6), 4
+    legs = major + minor + xn - 2
+    vmem = pl.BlockSpec(memory_space=pltpu.VMEM)
+    hbm = pl.BlockSpec(memory_space=pl.ANY)
+    flops = 2 * chunks * rows * width * hidden * 9
+    return pl.pallas_call(
+        functools.partial(experts_kernel, groups, parts, local_rows, ring, acc_ring, experts),
+        out_shape=[
+            jax.ShapeDtypeStruct((chunks, ROWS, wide), BF),
+            jax.ShapeDtypeStruct((chunks, rows, width), BF),
+            jax.ShapeDtypeStruct((width, 2 * hidden), BF),
+            jax.ShapeDtypeStruct((hidden, width), F32),
+        ],
+        in_specs=[vmem, hbm, hbm, hbm, vmem, vmem],
+        out_specs=[vmem, hbm, hbm, hbm],
+        scratch_shapes=[
+            pltpu.VMEM((ring, rows, width), BF),
+            pltpu.VMEM((2, rows, width), BF),
+            pltpu.VMEM((width, 2 * hidden), BF),
+            pltpu.VMEM((hidden, width), BF),
+            pltpu.VMEM((width, 2 * hidden), F32),
+            pltpu.VMEM((hidden, width), F32),
+            pltpu.VMEM((2, rows, width), BF),
+            pltpu.VMEM((acc_ring, half, wide), BF),
+            pltpu.VMEM((half, wide), BF),
+            pltpu.VMEM((2, 1, half, wide), BF),
+            pltpu.VMEM((2, xn - 1, half // xn, wide), BF),
+            pltpu.VMEM((2, minor - 1, half // xn // minor, wide), BF),
+            pltpu.VMEM((2, major - 1, ROWS, wide), BF),
+            pltpu.VMEM((rows, 4 * share), F32),
+            pltpu.VMEM((rows, 2 * share), F32),
+            pltpu.VMEM((rows, hidden), BF),
+            pltpu.VMEM((rows, 2 * hidden), BF),
+            pltpu.VMEM((rows, 128), F32),
+            pltpu.VMEM((rows, 128), F32),
+            pltpu.SemaphoreType.DMA((3 * local_exp,)),
+            pltpu.SemaphoreType.DMA((2,)),
+            pltpu.SemaphoreType.DMA((2,)),
+            pltpu.SemaphoreType.DMA((chunks, legs)),
+            pltpu.SemaphoreType.DMA((chunks, legs)),
+            pltpu.SemaphoreType.DMA((chunks, legs)),
+            pltpu.SemaphoreType.DMA((chunks, legs)),
+        ],
+        compiler_params=pltpu.CompilerParams(
+            collective_id=collective_id, has_side_effects=True, vmem_limit_bytes=60 * 2**20
+        ),
+        cost_estimate=pl.CostEstimate(flops=flops, bytes_accessed=80 * 2**20, transcendentals=chunks * rows * hidden),
+    )(x, dy, widen, shrink, dispatch, keep)
+
+
+def experts_apart(x, dy_all, keep_all, specialist_widen_matrix, specialist_shrink_matrix, dispatcher_matrix):
+    groups, parts = lax.axis_size("grp"), lax.axis_size("ep")
+    group, part = lax.axis_index("grp"), lax.axis_index("ep")
+    local_exp, inner, width = specialist_shrink_matrix.shape
+    share = inner // groups
+    widen = specialist_widen_matrix.reshape(local_exp, width, 2, groups, share)
+    widen = lax.dynamic_index_in_dim(widen, group, 3, keepdims=False)
+    widen = widen.transpose(1, 2, 0, 3).reshape(width, 2 * local_exp * share)
+    shrink = specialist_shrink_matrix.reshape(local_exp, groups, share, width)
+    shrink = lax.dynamic_index_in_dim(shrink, group, 1, keepdims=False).reshape(local_exp * share, width)
+    x_all = gather_all(x, 1)
+    chunk_shape = x_all.shape[:-1]
+    x_all, dy_all = x_all.reshape(-1, width), dy_all.reshape(-1, width)
+    keep_all = keep_all.reshape(x_all.shape[0], -1)
+    router = jax.nn.softmax(jnp.dot(x_all, dispatcher_matrix, preferred_element_type=F32), axis=-1)
+    gate = lax.dynamic_slice_in_dim(router * keep_all, part * local_exp, local_exp, axis=1)
+    gate = jnp.repeat(gate, share, axis=1)
+    gate_up = jnp.dot(x_all, widen, preferred_element_type=F32)
+    g, u = gate_up[:, : local_exp * share], gate_up[:, local_exp * share:]
+    sigma = jax.nn.sigmoid(g)
+    act = g * sigma * u
+    gated = (gate * act).astype(BF)
+    moe_part = jnp.dot(gated, shrink, preferred_element_type=F32).astype(BF)
+    d_raw = lax.dot_general(dy_all, shrink, (((1,), (1,)), ((), ())), preferred_element_type=F32)
+    d_gate = jnp.sum((act * d_raw).reshape(-1, local_exp, share), axis=-1)
+    d_act = gate * d_raw
+    d_gu = jnp.concatenate([d_act * u * sigma * (1.0 + g * (1.0 - sigma)), d_act * (g * sigma)], axis=1).astype(BF)
+    dx_part = lax.dot_general(d_gu, widen, (((1,), (1,)), ((), ())), preferred_element_type=F32).astype(BF)
+    lanes = jnp.arange(128, dtype=jnp.int32)
+    place = (lanes[None, :] == part * local_exp + jnp.arange(local_exp, dtype=jnp.int32)[:, None])
+    d_gate = jnp.sum(jnp.where(place[None], d_gate[:, :, None], 0.0), axis=1)
+    dx_part = jnp.concatenate([dx_part, d_gate.astype(BF)], axis=1)
+    dx_sum = scatter_all(dx_part.reshape(chunk_shape + (width + 128,)), 2)
+    grad_widen = lax.dot_general(x_all, d_gu, (((0,), (0,)), ((), ())), preferred_element_type=F32)
+    grad_shrink = lax.dot_general(gated, dy_all, (((0,), (0,)), ((), ())), preferred_element_type=F32)
+    grad_widen = grad_widen.astype(BF).reshape(width, 2, local_exp // 2, 2, share).transpose(0, 2, 1, 3, 4)
+    return dx_sum, moe_part.reshape(chunk_shape + (width,)), grad_widen, grad_shrink
 
 
 def per_device(
@@ -467,16 +867,12 @@
     if xs == minor:
         two = keep_all[:, :, :, :, 1].transpose(0, 4, 2, 3, 1, 5, 6)
     keep_all = jnp.stack([one, two], axis=2).reshape(-1, experts)
-
-    widen = specialist_widen_matrix.reshape(local_exp, width, 2, groups, share)
-    widen = lax.dynamic_index_in_dim(widen, group, 3, keepdims=False)
-    widen = widen.transpose(1, 2, 0, 3).reshape(width, 2 * local_exp * share)
-    shrink = specialist_shrink_matrix.reshape(local_exp, groups, share, width)
-    shrink = lax.dynamic_index_in_dim(shrink, group, 1, keepdims=False).reshape(local_exp * share, width)
-
-    dy_all = gather_all(output_gradient, 0)
-    chunk_shape = dy_all.shape[:-1]
-    dy_all = dy_all.reshape(-1, width)
+    fused = xs == minor and share % 128 == 0 and local_exp % 2 == 0 and 2 * xs * minor * major * ROWS <= 512
+
+    if fused:
+        dy_all = lax.all_gather(output_gradient, ALL, axis=1, tiled=True)
+    else:
+        dy_all = gather_all(output_gradient, 0)
 
     skip = block_entry_states.astype(F32)
     inv_first = lax.rsqrt(jnp.mean(skip * skip, axis=-1, keepdims=True) + EPS)
@@ -510,32 +906,18 @@
     inv_second = lax.rsqrt(jnp.mean(hidden * hidden, axis=-1, keepdims=True) + EPS)
     hat_second = hidden * inv_second
     ffn_in = (hat_second * gains[1]).astype(BF)
-    x_all = gather_all(ffn_in, 1).reshape(-1, width)
-    router = jax.nn.softmax(jnp.dot(x_all, dispatcher_matrix, preferred_element_type=F32), axis=-1)
-    gate = lax.dynamic_slice_in_dim(router * keep_all, part * local_exp, local_exp, axis=1)
-    gate = jnp.repeat(gate, share, axis=1)
-    gate_up = jnp.dot(x_all, widen, preferred_element_type=F32)
-    g, u = gate_up[:, : local_exp * share], gate_up[:, local_exp * share:]
-    sigma = jax.nn.sigmoid(g)
-    act = g * sigma * u
-    gated = (gate * act).astype(BF)
-    moe_part = jnp.dot(gated, shrink, preferred_element_type=F32).astype(BF)
-    d_raw = lax.dot_general(dy_all, shrink, (((1,), (1,)), ((), ())), preferred_element_type=F32)
-    d_gate = jnp.sum((act * d_raw).reshape(-1, local_exp, share), axis=-1)
-    d_act = gate * d_raw
-    d_gu = jnp.concatenate([d_act * u * sigma * (1.0 + g * (1.0 - sigma)), d_act * (g * sigma)], axis=1).astype(BF)
-    dx_part = lax.dot_general(d_gu, widen, (((1,), (1,)), ((), ())), preferred_element_type=F32).astype(BF)
-    lanes = jnp.arange(128, dtype=jnp.int32)
-    place = (lanes[None, :] == part * local_exp + jnp.arange(local_exp, dtype=jnp.int32)[:, None])
-    d_gate = jnp.sum(jnp.where(place[None], d_gate[:, :, None], 0.0), axis=1)
-    dx_part = jnp.concatenate([dx_part, d_gate.astype(BF)], axis=1)
-    dx_sum = scatter_all(dx_part.reshape(chunk_shape + (width + 128,)), 2).astype(F32)
-    dx_sum = dx_sum.reshape(micro, local_rows, width + 128)
-    grad_widen = lax.dot_general(x_all, d_gu, (((0,), (0,)), ((), ())), preferred_element_type=F32)
-    grad_shrink = lax.dot_general(gated, dy_all, (((0,), (0,)), ((), ())), preferred_element_type=F32)
-    grad_widen = grad_widen.astype(BF).reshape(groups, width // groups, 2, local_exp, share)
-    grad_widen = lax.all_to_all(grad_widen, "grp", 0, 0, tiled=True)
-    grad_widen = grad_widen.transpose(3, 1, 2, 0, 4).reshape(local_exp, width // groups, 2 * inner).astype(F32)
+    chunk_shape = (micro * local_rows // ROWS, 2, xs, minor, major, ROWS)
+    keep_all = keep_all.reshape(chunk_shape[0], -1, experts)
+    if fused:
+        dx_sum, moe_part, grad_widen, grad_shrink = experts_together(
+            ffn_in, dy_all, specialist_widen_matrix, specialist_shrink_matrix, dispatcher_matrix, keep_all.astype(BF), 1)
+    else:
+        dx_sum, moe_part, grad_widen, grad_shrink = experts_apart(
+            ffn_in, dy_all, keep_all, specialist_widen_matrix, specialist_shrink_matrix, dispatcher_matrix)
+    dx_sum = dx_sum.astype(F32).reshape(micro, local_rows, width + 128)
+    grad_widen = lax.all_to_all(grad_widen.reshape(groups, width // groups, -1), "grp", 0, 0, tiled=True)
+    grad_widen = grad_widen.reshape(groups, width // groups, local_exp // 2, 2, 2, share)
+    grad_widen = grad_widen.transpose(2, 4, 1, 3, 0, 5).reshape(local_exp, width // groups, 2 * inner).astype(F32)
     grad_shrink = grad_shrink.reshape(local_exp, share, width)
     moe = scatter_all(moe_part.reshape(chunk_shape + (width,)), 3).astype(F32).reshape(micro, local_rows, width)
     output = (hidden + moe).astype(BF)

time: 1310 us -> 1010 us (0.77)
  matrix products: 172 us -> 40.8 us
  Pallas kernels: 700 us -> 569 us
  waiting for transfers between devices: 23.8 us -> 112 us
  local copies, waits for them, and re-layouts: 225 us -> 149 us
  other arithmetic: 87.4 us -> 30.4 us
    dot_general x7 -> x0, matrix products: 132 us -> none  [the longest x1 25.3 us: per_device(): lax.dot_general(d_gu, widen, (((1,), (1,)), ((), ())), preferred_element_...]
    pallas_call x2 -> x1, Pallas kernels: 256 us -> 160 us  [scatter_all(): call(part)]
    all_gather x0 -> x1, waiting for transfers between devices: none -> 67.2 us  [per_device(): dy_all = lax.all_gather(output_gradient, ALL, axis=1, tiled=True)]
    unnamed x102 -> x99, local copies, waits for them, and re-layouts: 71.7 us -> 27.7 us
    pallas_call x2 -> x1, Pallas kernels: 252 us -> 217 us  [experts_together(): pl.pallas_call(functools.partial(experts_kernel, groups, parts, local_row...]
    concatenate x1 -> x0, local copies, waits for them, and re-layouts: 22.2 us -> none  [per_device(): dx_part = jnp.concatenate([dx_part, d_gate.astype(BF)], axis=1)]
    all_gather x1, waiting for transfers between devices: 0.02 us -> 20 us  [per_device(): branch = lax.all_gather(d_hidden.astype(BF), 'ep', axis=1, tiled=True)]
    concatenate x1 -> x0, other arithmetic: 19 us -> none  [per_device(): dx_part = jnp.concatenate([dx_part, d_gate.astype(BF)], axis=1)]
  transfers between devices with their start and end apart: 5 -> 6, of which waited for: 1 -> 3; matrix products, arithmetic and copies ran while one was open for 17% -> 10% of each run, Pallas kernels for 36% -> 35%
where the time goes in v2:
time: 1010 us; the launch traced here: 995 us
  Pallas kernels  569 us (56%)
  local copies, waits for them, and re-layouts  149 us (15%)
  waiting for transfers between devices  112 us (11%)
  blocking collectives  71.5 us (7%)
  matrix products  40.8 us (4%)
  other arithmetic  30.4 us (3%)
  between operations  16.4 us (2%)
    pallas_call x1, Pallas kernels, experts_together(): pl.pallas_call(functools.partial(experts_kernel, groups, parts, local_row...  217 us
    pallas_call x1, Pallas kernels, total_over_groups(): pl.pallas_call(functools.partial(total_kernel, groups, parts, spans), out...  192 us
    pallas_call x1, Pallas kernels, scatter_all(): call(part)  160 us
    all_gather x1, waiting for transfers between devices, per_device(): dy_all = lax.all_gather(output_gradient, ALL, axis=1, tiled=True)  67.2 us
    all_gather x1, blocking collectives, per_device(): lax.all_gather(keep.astype(BF), ALL, axis=1, tiled=True).astype(F32)  47.2 us
    convert_element_type x3, local copies, waits for them, and re-layouts, per_device(): grad_widen.transpose(2, 4, 1, 3, 0, 5)  32.7 us
    unnamed x99, local copies, waits for them, and re-layouts  27.7 us
    convert_element_type x1, local copies, waits for them, and re-layouts, per_device(): grad_qkv.astype(BF).reshape(spans, minor, major, -1, 3 * local_width)  27.3 us
  transfers between devices with their start and end apart: 6, of which 3 were waited for; matrix products, arithmetic and copies ran while one was open for 10% of the time, Pallas kernels for 35%

profile of v2, /device:TPU:0, one launch (start us, length us, event | category | flops | bytes accessed | tf_op | source)
XLA Modules:
  0.0 994.9 jit_solution(8232653048887753668)
XLA Ops:
  14.5 23.7 %all-gather.4.cloned.1.call-done = bf16[2,256,2048]{2,1,0:T(8,128)(2,1)} async-done(((bf16[2,64,2048]{2,1,0:T(8,128)(2,1)}), bf16[2,256,2048]{2,1,0:T(8,128)(2,1)}) %all-gather.4.cloned.1.call-update) | async-done | bytes 2097168 | tf_op jit(solution)/shard_map/all_gather | solution.py:881
  38.2 6.2 fusion.17
  47.3 5.9 psum.21
  73.8 47.2 %all_gather.14 = bf16[2,2048,16]{2,0,1:T(2,128)(2,1)S(1)} all-gather(bf16[2,64,16]{2,0,1:T(2,128)(2,1)S(1)} %copy.137), channel_id=1, replica_groups=mesh['grp'=8,'ep'=4] {'grp','ep'}, dimensions={1}, use_global_device_ids=true | all-gather | bytes 135168 | tf_op jit(solution)/shard_map/all_gather | solution.py:863
  127.7 67.2 %all-gather.6.cloned.1.call-done.dy = bf16[2,2048,2048]{2,1,0:T(8,128)(2,1)} async-done(((bf16[2,64,2048]{2,1,0:T(8,128)(2,1)}), bf16[2,2048,2048]{2,1,0:T(8,128)(2,1)}) %all-gather.6.cloned.1.call-update) | async-done | bytes 16777232 | tf_op jit(solution)/shard_map/all_gather | solution.py:873
  194.9 217.3 %shard_map.187 = (bf16[8,16,2176]{2,1,0:T(8,128)(2,1)}, bf16[8,512,2048]{2,1,0:T(8,128)(2,1)}, bf16[2048,1024]{1,0:T(8,128)(2,1)}, f32[512,2048]{1,0:T(8,128)}) custom-call(bf16[8,16,2048]{2,1,0:T(8,128)(2,1)} %bitcast.186, bf16[2,2048,2048]{2,1,0:T(8,128)(2,1)} %all-gather.6.cloned.1.call-done.dy, bf16[4,2048,2048]{2,1,0:T(8,128)(2,1)} %widen.1, ...), custom_call_target="tpu_custom_call" | custom-call | flops 77309411328 | bytes 83886080 | tf_op jit(solution)/shard_map/pallas_call | solution.py:742
  421.1 20.0 %all-gather.8.cloned.1.call-done = bf16[2,256,2048]{2,1,0:T(8,128)(2,1)} async-done(((bf16[2,64,2048]{2,1,0:T(8,128)(2,1)}), bf16[2,256,2048]{2,1,0:T(8,128)(2,1)}) %all-gather.8.cloned.1.call-update) | async-done | bytes 2097168 | tf_op jit(solution)/shard_map/all_gather | solution.py:935
  441.2 3.7 fusion.28
  461.8 3.9 multiply_reduce_fusion
  465.7 5.9 psum.22
  474.7 7.4 bitcast_convert_fusion.2
  482.2 5.7 all-to-all-start
  487.9 160.5 %shard_map.188 = bf16[8,16,2048]{2,1,0:T(8,128)(2,1)} custom-call(bf16[8,2,2,2,4,16,2048]{6,5,4,3,2,1,0:T(8,128)(2,1)} %bitcast.184), custom_call_target="tpu_custom_call" | custom-call | tf_op jit(solution)/shard_map/pallas_call | solution.py:346
  648.8 3.9 bitcast_convert_fusion
  652.7 27.3 %copy.154 = bf16[2048,3,512]{2,1,0:T(4,128)(2,1)} copy(bf16[2048,3,512]{2,0,1:T(8,128)(2,1)S(1)} %bitcast_convert_fusion) | data formatting | bytes 12582912 | tf_op jit(solution)/shard_map/convert_element_type | solution.py:968
  680.1 17.9 %reshape.242.refs_0_ = bf16[4,2,4,64,1536]{4,3,2,1,0:T(8,128)(2,1)} reshape(bf16[2048,3,512]{2,1,0:T(4,128)(2,1)} %copy.154) | data formatting | bytes 12582912 | tf_op jit(solution)/shard_map/reshape | solution.py:968
  698.1 3.6 bitcast_convert_fusion.1
  703.2 12.5 %all-reduce.4 = bf16[18,2048]{1,0:T(8,128)(2,1)S(1)} all-reduce(f32[18,2048]{1,0:T(8,128)S(1)} %pad_maximum_fusion.5), channel_id=1, replica_groups=mesh['grp'=8,'ep'=4] {'ep'}, use_global_device_ids=true, to_apply=%region_20.21 | all-reduce | flops 36864 | bytes 221184 | tf_op jit(solution)/shard_map/psum | solution.py:962
  717.5 191.7 %shard_map.189 = (bf16[4,2,4,64,1536]{4,3,2,1,0:T(8,128)(2,1)}, bf16[1,2,4,64,2048]{4,3,2,1,0:T(8,128)(2,1)S(1)}, bf16[1,2,4,16,384]{4,3,2,1,0:T(8,128)(2,1)S(1)}) custom-call(bf16[4,2,4,64,1536]{4,3,2,1,0:T(8,128)(2,1)} %reshape.242.refs_0_, bf16[1,2,4,64,2048]{4,3,2,1,0:T(8,128)(2,1)S(1)} %bitcast.175, ...), custom_call_target="tpu_custom_call" | custom-call | tf_op jit(solution)/shard_map/pallas_call | solution.py:418
  910.0 19.7 %reshape.253 = f32[2048,3,512]{2,1,0:T(4,128)} reshape(bf16[4,2,4,64,1536]{4,3,2,1,0:T(8,128)(2,1)} %get-tuple-element.19) | data formatting | bytes 18874368 | tf_op jit(solution)/shard_map/convert_element_type | solution.py:971
  929.7 14.6 %copy.156 = f32[2048,3,512]{2,0,1:T(8,128)} copy(f32[2048,3,512]{2,1,0:T(4,128)} %reshape.253) | data formatting | bytes 25165824
  948.3 11.8 %reshape.256 = f32[8,256,2,2,2,128]{5,4,3,2,1,0:T(2,128)} reshape(bf16[8,256,1024]{2,1,0:T(8,128)(2,1)} %all-to-all-done) | data formatting | bytes 12582912 | tf_op jit(solution)/shard_map/convert_element_type | solution.py:920
  960.1 11.5 %copy.189 = f32[8,256,2,2,2,128]{5,0,3,1,4,2:T(8,128)} copy(f32[8,256,2,2,2,128]{5,4,3,2,1,0:T(2,128)} %reshape.256) | data formatting | bytes 16777216 | tf_op jit(solution)/shard_map/convert_element_type | solution.py:920
  971.6 9.4 reshape.255
  (189 shorter events, 80.0 us)
Async XLA Ops:
  8.0 61.5 %copy-start = (bf16[512,2048]{1,0:T(8,128)(2,1)S(1)}, bf16[512,2048]{1,0:T(8,128)(2,1)}, u32[]{:S(2)}) copy-start(bf16[512,2048]{1,0:T(8,128)(2,1)} %param.19) | copy-start | bytes 6291460
  8.0 4.8 copy-start.41
  8.0 5.7 copy-start.40
  8.0 30.2 %all-gather.4.cloned.1.call-start = ((), (), s32[]{:S(2)}) async-start(), calls=%async_computation.3 | async-start | bytes 2621440 | tf_op jit(solution)/shard_map/all_gather | solution.py:881
  12.8 112.0 %reduce-scatter.3.cloned.1.call-start = ((), (), s32[]{:S(2)}) async-start(), calls=%async_computation.4 | async-start | bytes 2621440 | tf_op jit(solution)/shard_map/reduce_scatter | solution.py:900
  13.7 48.1 %copy-start.19 = (f32[256,128]{1,0:T(8,128)}, f32[256,128]{1,0:T(8,128)S(1)}, u32[]{:S(2)}) copy-start(f32[256,128]{1,0:T(8,128)S(1)} %pad_maximum_fusion.7) | copy-start | bytes 393220
  72.2 122.7 %all-gather.6.cloned.1.call-start = ((), (), s32[]{:S(2)}) async-start(), calls=%async_computation.5 | async-start | bytes 17301504 | tf_op jit(solution)/shard_map/all_gather | solution.py:873
  72.8 368.4 %all-gather.8.cloned.1.call-start = ((), (), s32[]{:S(2)}) async-start(), calls=%async_computation.6 | async-start | bytes 2621440 | tf_op jit(solution)/shard_map/all_gather | solution.py:935
  126.0 291.3 %copy-start.33 = (f32[2,64]{1,0:T(2,128)}, f32[2,64]{1,0:T(2,128)S(1)}, u32[]{:S(2)}) copy-start(f32[2,64]{1,0:T(2,128)S(1)} %add_rsqrt_fusion.1) | copy-start | bytes 1540
  127.3 67.6 %copy-start.11 = (bf16[2,64,2048]{2,1,0:T(8,128)(2,1)}, bf16[2,64,2048]{2,1,0:T(8,128)(2,1)S(1)}, u32[]{:S(2)}) copy-start(bf16[2,64,2048]{2,1,0:T(8,128)(2,1)S(1)} %multiply_convert_fusion.2) | copy-start | bytes 1572868
  414.4 3.9 copy-start.9
  419.6 282.1 %reduce-scatter.5.cloned.1.call-start = ((), (), s32[]{:S(2)}) async-start(), calls=%async_computation.7 | async-start | bytes 2621440 | tf_op jit(solution)/shard_map/reduce_scatter | solution.py:953
  421.1 25.7 %copy-start.38 = (f32[2,4,256]{2,1,0:T(4,128)S(1)}, f32[2,4,256]{2,1,0:T(4,128)}, u32[]{:S(2)}) copy-start(f32[2,4,256]{2,1,0:T(4,128)} %copy-done.37) | copy-start | bytes 24580
  482.2 466.1 %all-to-all-start = ((bf16[8,256,1024]{2,1,0:T(8,128)(2,1)}), bf16[8,256,1024]{2,1,0:T(8,128)(2,1)}, u32[]{:S(2)}, u32[]{:S(2)}) async-start(bf16[8,256,1024]{2,1,0:T(8,128)(2,1)} %bitcast.189), calls=%async_computation.2 | async-start | bytes 8388608 | tf_op jit(solution)/shard_map/all_to_all | solution.py:918
  487.9 160.5 %copy-start.12 = (bf16[2,64,2048]{2,1,0:T(8,128)(2,1)S(1)}, bf16[2,64,2048]{2,1,0:T(8,128)(2,1)}, u32[]{:S(2)}) copy-start(bf16[2,64,2048]{2,1,0:T(8,128)(2,1)} %copy-done.11) | copy-start | bytes 1572868
  487.9 160.9 %copy-start.22 = (bf16[2,2,256,512]{3,2,0,1:T(8,128)(2,1)S(1)}, bf16[2,2,256,512]{3,2,0,1:T(8,128)(2,1)}, u32[]{:S(2)}) copy-start(bf16[2,2,256,512]{3,2,0,1:T(8,128)(2,1)} %copy-done.21) | copy-start | bytes 3145732
  487.9 160.9 %copy-start.26 = (bf16[1,2,256,512]{3,2,0,1:T(8,128)(2,1)S(1)}, bf16[1,2,256,512]{3,2,0,1:T(8,128)(2,1)}, u32[]{:S(2)}) copy-start(bf16[1,2,256,512]{3,2,0,1:T(8,128)(2,1)} %copy.174) | copy-start | bytes 1572868
  487.9 160.9 %copy-start.43 = (bf16[2,256,2048]{2,1,0:T(8,128)(2,1)S(1)}, bf16[2,256,2048]{2,1,0:T(8,128)(2,1)}, u32[]{:S(2)}) copy-start(bf16[2,256,2048]{2,1,0:T(8,128)(2,1)} %all-gather.4.cloned.1.call-done) | copy-start | bytes 6291460
  680.1 18.0 %copy-start.44 = (bf16[2,256,2048]{2,1,0:T(8,128)(2,1)S(1)}, bf16[2,256,2048]{2,1,0:T(8,128)(2,1)}, u32[]{:S(2)}) copy-start(bf16[2,256,2048]{2,1,0:T(8,128)(2,1)} %all-gather.8.cloned.1.call-done) | copy-start | bytes 6291460
  698.0 5.1 copy-start.32
  971.6 9.4 copy-start.8
  971.6 9.4 copy-start.10
  971.6 9.4 copy-start.17
  971.6 9.4 copy-start.34
  (28 other events, 58.5 us)
Sparse Core Ops, SparseCore 0:
  12.9 25.2 all-gather.3
  72.3 36.8 reduce-scatter.2
  419.7 21.3 all-gather.7
  482.3 38.3 reduce-scatter.4
Sparse Core Ops, SparseCore 1:
  76.0 118.8 all-gather.5

commit v3 on v2

--- a/solution.py
+++ b/solution.py
@@ -346,7 +346,7 @@
     return jnp.concatenate([call(part[i:i + per]) for i in range(0, chunks, per)]) if per < chunks else call(part)
 
 
-def total_kernel(groups, parts, spans, *refs):
+def total_kernel(groups, parts, spans, far_first, *refs):
     count = len(spans)
     ins, outs = refs[:count], refs[count:2 * count]
     acc, land_y, land_z = refs[2 * count:3 * count], refs[3 * count:4 * count], refs[4 * count:5 * count]
@@ -355,9 +355,10 @@
     g = lax.axis_index("grp")
     short = Line(minor, lax.rem(g, minor), (1, 0))
     long = Line(major, lax.div(g, minor), (minor, 0))
-    y, z = short.place, long.place
     loads, chains, number = [], [], 0
     for j in range(count):
+        one, two = (long, short) if far_first[j] else (short, long)
+        y, z = one.place, two.place
         for k in range(spans[j]):
             load = pltpu.make_async_copy(ins[j].at[k], acc[j].at[k], local.at[number])
             load.start()
@@ -370,10 +371,10 @@
                 base[0] += leg_count(n)
                 return (lambda i: send.at[number, b + i]), (lambda i: recv.at[number, b + i])
 
-            down = reduce_hops(short, lambda i, j=j, k=k: acc[j].at[k, i], lambda i, j=j, k=k: land_y[j].at[k, i], add, *sems(minor))
-            down += reduce_hops(long, lambda i, j=j, k=k: acc[j].at[k, y, i], lambda i, j=j, k=k: land_z[j].at[k, i], add, *sems(major))
-            up = gather_hops(long, lambda i, j=j, k=k: outs[j].at[k, y, i], *sems(major))
-            up += gather_hops(short, lambda i, j=j, k=k: outs[j].at[k, i], *sems(minor))
+            down = reduce_hops(one, lambda i, j=j, k=k: acc[j].at[k, i], lambda i, j=j, k=k: land_y[j].at[k, i], add, *sems(one.size))
+            down += reduce_hops(two, lambda i, j=j, k=k, y=y: acc[j].at[k, y, i], lambda i, j=j, k=k: land_z[j].at[k, i], add, *sems(two.size))
+            up = gather_hops(two, lambda i, j=j, k=k, y=y: outs[j].at[k, y, i], *sems(two.size))
+            up += gather_hops(one, lambda i, j=j, k=k: outs[j].at[k, i], *sems(one.size))
             chains.append((load, down, store, up))
             number += 1
     greet([short, long])
@@ -406,17 +407,18 @@
     flow(whole)
 
 
-def total_over_groups(arrays, spans, collective_id):
+def total_over_groups(arrays, far_first, collective_id):
     groups, parts = lax.axis_size("grp"), lax.axis_size("ep")
     major, minor, _ = mesh_sizes(groups, parts)
     legs = 2 * (leg_count(minor) + leg_count(major))
+    spans = tuple(a.shape[0] for a in arrays)
     total = sum(spans)
     any_spec = pl.BlockSpec(memory_space=pl.ANY)
     scratch = [pltpu.VMEM(a.shape, BF) for a in arrays]
-    scratch += [pltpu.VMEM((a.shape[0], leg_count(minor)) + a.shape[2:], BF) for a in arrays]
-    scratch += [pltpu.VMEM((a.shape[0], leg_count(major)) + a.shape[3:], BF) for a in arrays]
+    scratch += [pltpu.VMEM((a.shape[0], leg_count(a.shape[1])) + a.shape[2:], BF) for a in arrays]
+    scratch += [pltpu.VMEM((a.shape[0], leg_count(a.shape[2])) + a.shape[3:], BF) for a in arrays]
     return pl.pallas_call(
-        functools.partial(total_kernel, groups, parts, spans),
+        functools.partial(total_kernel, groups, parts, spans, far_first),
         out_shape=[jax.ShapeDtypeStruct(a.shape, BF) for a in arrays],
         in_specs=[any_spec] * len(arrays),
         out_specs=[any_spec] * len(arrays),
@@ -466,7 +468,7 @@
 
 def experts_kernel(
     groups, parts, local_rows, ring, acc_ring, experts,
-    x, dy, widen, shrink, dispatch, keep,
+    x, dy, widen, shrink, dispatch,
     summed, moe, grad_widen, grad_shrink,
     xs, dys, wide, down, sum_wide, sum_down, stage, acc, other, land_c, land_p, land_q, land_z,
     hid, raw, gated, d_gu, gate, d_gate,
@@ -498,20 +500,10 @@
     for copy in loads:
         copy.start()
 
-    def dy_start(k):
-        m, r = lax.div(k, cuts), lax.rem(k, cuts)
-        for cc in range(2):
-            for pp in range(pn):
-                for qq in range(qn):
-                    for zz in range(zn):
-                        xx, yy = (pp, qq) if (cc == 0 or pn != qn) else (qq, pp)
-                        device = (zz * (groups // zn) + yy) * parts + xx * 2 + cc
-                        pltpu.make_async_copy(
-                            dy.at[m, pl.ds(pl.multiple_of(device * local_rows + r * ROWS, ROWS), ROWS), :],
-                            dys.at[lax.rem(k, 2), pl.ds((((cc * pn + pp) * qn + qq) * zn + zz) * ROWS, ROWS), :],
-                            dy_sem.at[lax.rem(k, 2)],
-                        ).start()
-
+    def dy_copy(k):
+        return pltpu.make_async_copy(dy.at[k], dys.at[lax.rem(k, 2)], dy_sem.at[lax.rem(k, 2)])
+
+    dy_start = lambda k: dy_copy(k).start()
     dy_start(0)
     greet_lines([core, first, second, long])
     sum_wide[...] = jnp.zeros_like(sum_wide)
@@ -578,7 +570,7 @@
             for copy in loads:
                 copy.wait()
 
-        pltpu.make_async_copy(moe.at[0], dyk, dy_sem.at[lax.rem(k, 2)]).wait()
+        dy_copy(k).wait()
 
         @pl.when(k + 1 < chunks)
         def _():
@@ -592,7 +584,7 @@
             logits = jnp.where(lane < experts, hid[here, :128], NEG)
             grown = jnp.exp(logits - jnp.max(logits, axis=-1, keepdims=True))
             probs = grown / jnp.sum(grown, axis=-1, keepdims=True)
-            gate[here, :] = probs * keep[k, here, :].astype(F32)
+            gate[here, :] = probs * dyk[here, width:].astype(F32)
             d_gate[here, :] = jnp.zeros((64, 128), F32)
 
         @pl.loop(0, pairs)
@@ -600,7 +592,7 @@
             cols = pl.ds(pl.multiple_of(j * 4 * share, 4 * share), 4 * share)
             some = pl.ds(pl.multiple_of(j * 2 * share, 2 * share), 2 * share)
             hid[...] = jnp.dot(buf[...], wide[:, cols], preferred_element_type=F32)
-            raw[...] = lax.dot_general(dyk[...], down[some, :], (((1,), (1,)), ((), ())), preferred_element_type=F32)
+            raw[...] = lax.dot_general(dyk[:, :width], down[some, :], (((1,), (1,)), ((), ())), preferred_element_type=F32)
 
             @pl.loop(0, rows // 32)
             def _(i):
@@ -720,10 +712,9 @@
     out_down.wait()
 
 
-def experts_together(x, dy, widen, shrink, dispatch, keep, collective_id):
-    experts = keep.shape[-1]
+def experts_together(x, dy, widen, shrink, dispatch, collective_id):
+    experts = dispatch.shape[1]
     dispatch = jnp.pad(dispatch, ((0, 0), (0, 128 - experts)))
-    keep = jnp.pad(keep, ((0, 0), (0, 0), (0, 128 - experts)))
     groups, parts = lax.axis_size("grp"), lax.axis_size("ep")
     major, minor, xn = mesh_sizes(groups, parts)
     micro, local_rows, width = x.shape
@@ -747,11 +738,11 @@
             jax.ShapeDtypeStruct((width, 2 * hidden), BF),
             jax.ShapeDtypeStruct((hidden, width), F32),
         ],
-        in_specs=[vmem, hbm, hbm, hbm, vmem, vmem],
+        in_specs=[vmem, hbm, hbm, hbm, vmem],
         out_specs=[vmem, hbm, hbm, hbm],
         scratch_shapes=[
             pltpu.VMEM((ring, rows, width), BF),
-            pltpu.VMEM((2, rows, width), BF),
+            pltpu.VMEM((2, rows, wide), BF),
             pltpu.VMEM((width, 2 * hidden), BF),
             pltpu.VMEM((hidden, width), BF),
             pltpu.VMEM((width, 2 * hidden), F32),
@@ -781,10 +772,10 @@
             collective_id=collective_id, has_side_effects=True, vmem_limit_bytes=60 * 2**20
         ),
         cost_estimate=pl.CostEstimate(flops=flops, bytes_accessed=80 * 2**20, transcendentals=chunks * rows * hidden),
-    )(x, dy, widen, shrink, dispatch, keep)
-
-
-def experts_apart(x, dy_all, keep_all, specialist_widen_matrix, specialist_shrink_matrix, dispatcher_matrix):
+    )(x, dy, widen, shrink, dispatch)
+
+
+def experts_apart(x, dy_all, specialist_widen_matrix, specialist_shrink_matrix, dispatcher_matrix):
     groups, parts = lax.axis_size("grp"), lax.axis_size("ep")
     group, part = lax.axis_index("grp"), lax.axis_index("ep")
     local_exp, inner, width = specialist_shrink_matrix.shape
@@ -796,8 +787,9 @@
     shrink = lax.dynamic_index_in_dim(shrink, group, 1, keepdims=False).reshape(local_exp * share, width)
     x_all = gather_all(x, 1)
     chunk_shape = x_all.shape[:-1]
-    x_all, dy_all = x_all.reshape(-1, width), dy_all.reshape(-1, width)
-    keep_all = keep_all.reshape(x_all.shape[0], -1)
+    x_all, dy_all = x_all.reshape(-1, width), dy_all.reshape(x_all.shape[0] * ROWS * math.prod(chunk_shape[1:-1]), -1)
+    keep_all = dy_all[:, width: width + dispatcher_matrix.shape[1]].astype(F32)
+    dy_all = dy_all[:, :width]
     router = jax.nn.softmax(jnp.dot(x_all, dispatcher_matrix, preferred_element_type=F32), axis=-1)
     gate = lax.dynamic_slice_in_dim(router * keep_all, part * local_exp, local_exp, axis=1)
     gate = jnp.repeat(gate, share, axis=1)
@@ -821,6 +813,595 @@
     grad_shrink = lax.dot_general(gated, dy_all, (((0,), (0,)), ((), ())), preferred_element_type=F32)
     grad_widen = grad_widen.astype(BF).reshape(width, 2, local_exp // 2, 2, share).transpose(0, 2, 1, 3, 4)
     return dx_sum, moe_part.reshape(chunk_shape + (width,)), grad_widen, grad_shrink
+
+
+def spread_kernel(share, x, out):
+    for i in range(x.shape[0]):
+        out[0, :, i * share: (i + 1) * share] = x[i].astype(F32)
+
+
+def spread(x, local_exp, share):
+    groups, rows, _ = x.shape
+    if share % 128:
+        x = x.reshape(groups, rows, local_exp // 2, 2, 2, share).transpose(2, 4, 1, 3, 0, 5)
+        return x.reshape(local_exp, rows, 2 * groups * share).astype(F32)
+    return pl.pallas_call(
+        functools.partial(spread_kernel, share),
+        grid=(local_exp, 2),
+        out_shape=jax.ShapeDtypeStruct((local_exp, rows, 2 * groups * share), F32),
+        in_specs=[pl.BlockSpec((groups, rows, share), lambda e, h: (0, 0, e // 2 * 4 + h * 2 + e % 2))],
+        out_specs=pl.BlockSpec((1, rows, groups * share), lambda e, h: (e, 0, h)),
+    )(x)
+
+
+class Backdrop:
+    LAG = 4
+
+    def __init__(self, groups, parts, part, out, acc, land_c, land_p, land_q, land_z, local, send, recv):
+        self.core, self.first, self.second, self.long = lines(groups, parts)
+        self.part, self.out, self.acc, self.lands = part, out, acc, (land_c, land_p, land_q, land_z)
+        self.local, self.send, self.recv = local, send, recv
+        self.chunks = part.shape[0]
+        pn, qn, zn = self.first.size, self.second.size, self.long.size
+        self.rz, self.rq, self.rp, self.rc = ROWS, ROWS * zn, ROWS * zn * qn, ROWS * zn * qn * pn
+
+    @staticmethod
+    def scratch(chunks, width):
+        major, minor, xn = mesh_sizes(lax.axis_size("grp"), lax.axis_size("ep"))
+        half = ROWS * major * minor * xn
+        legs = major + minor + xn - 2
+        return [
+            pltpu.VMEM((4, half, width), BF),
+            pltpu.VMEM((2, 1, half, width), BF),
+            pltpu.VMEM((2, xn - 1, half // xn, width), BF),
+            pltpu.VMEM((2, minor - 1, half // xn // minor, width), BF),
+            pltpu.VMEM((2, major - 1, ROWS, width), BF),
+            pltpu.SemaphoreType.DMA((chunks,)),
+            pltpu.SemaphoreType.DMA((chunks, legs)),
+            pltpu.SemaphoreType.DMA((chunks, legs)),
+        ]
+
+    def near(self):
+        return [self.core, self.first, self.second, self.long]
+
+    def buf(self, k):
+        return self.acc.at[lax.rem(k, 4)]
+
+    def own(self, k):
+        here = pl.ds(pl.multiple_of(self.core.place * self.rc, self.rc), self.rc)
+        return pltpu.make_async_copy(self.part.at[k, here, :], self.buf(k), self.local.at[k])
+
+    def hop(self, k, level):
+        c, p, q, z = self.core.place, self.first.place, self.second.place, self.long.place
+        pn, qn = self.first.size, self.second.size
+        at = lambda start, size: pl.ds(pl.multiple_of(start, ROWS), size)
+        line, offset, source = [
+            (self.core, 0, lambda i: self.part.at[k, at(i * self.rc, self.rc), :]),
+            (self.first, 1, lambda i: self.buf(k).at[at(i * self.rp, self.rp), :]),
+            (self.second, pn, lambda i: self.buf(k).at[at(p * self.rp + i * self.rq, self.rq), :]),
+            (self.long, pn + qn - 1, lambda i: self.buf(k).at[at(p * self.rp + q * self.rq + i * self.rz, self.rz), :]),
+        ][level]
+        land = self.lands[level]
+        return swap_legs(line, source, lambda j, i: land.at[lax.rem(k, 2), j],
+                         lambda j: self.send.at[k, offset + j], lambda j: self.recv.at[k, offset + j])
+
+    def end(self, k, level):
+        c, p, q, z = self.core.place, self.first.place, self.second.place, self.long.place
+        end_legs(self.hop(k, level))
+        if level == 0:
+            self.own(k).wait()
+        first = [0, p * self.rp, p * self.rp + q * self.rq, p * self.rp + q * self.rq + z * self.rz][level]
+        size = [self.rc, self.rp, self.rq, self.rz][level]
+        land = self.lands[level]
+        if level == 3:
+            total = self.buf(k)[pl.ds(pl.multiple_of(first, ROWS), size), :].astype(F32)
+            for j in range(land.shape[1]):
+                total = total + land[lax.rem(k, 2), j].astype(F32)
+            self.out[k] = total.astype(self.out.dtype)
+        else:
+            for j in range(land.shape[1]):
+                add_rows(self.buf(k), first, land.at[lax.rem(k, 2), j], size)
+            start_legs(self.hop(k, level + 1))
+
+    def begin(self, k):
+        self.own(k).start()
+        start_legs(self.hop(k, 0))
+
+    def step(self, t):
+        for level in (3, 2, 1, 0):
+            k = t - level - 1
+
+            @pl.when((k >= 0) & (k < self.chunks))
+            def _(k=k, level=level):
+                self.end(k, level)
+
+        @pl.when((t >= 0) & (t < self.chunks))
+        def _():
+            self.begin(t)
+
+
+class Sequence:
+    def __init__(self, parts, block, micro):
+        e = lax.axis_index("ep")
+        self.xn, self.block, self.micro, self.e = parts // 2, block, micro, e
+        self.x, self.c = lax.div(e, 2), lax.rem(e, 2)
+        self.line = Line(parts, e, (0, 1))
+        self.line_x = Line(self.xn, self.x, (0, 2))
+        self.line_c = Line(2, self.c, (0, 1))
+
+    def at(self, ref, m, x, c):
+        return ref.at[m, pl.ds(pl.multiple_of((x * 2 + c) * self.block, self.block), self.block), :]
+
+    def gather_x(self, ref, send, recv):
+        legs = []
+        for m in range(self.micro):
+            legs += swap_legs(
+                self.line_x, lambda i, m=m: self.at(ref, m, self.x, self.c), lambda j, i, m=m: self.at(ref, m, i, self.c),
+                lambda j, m=m: send.at[m, j], lambda j, m=m: recv.at[m, j])
+        return legs
+
+    def gather_c(self, ref, send, recv):
+        legs = []
+        for m in range(self.micro):
+            for x in range(self.xn):
+                legs += swap_legs(
+                    self.line_c, lambda i, m=m, x=x: self.at(ref, m, x, self.c), lambda j, i, m=m, x=x: self.at(ref, m, x, i),
+                    lambda j, m=m, x=x: send.at[m, self.xn - 1 + x], lambda j, m=m, x=x: recv.at[m, self.xn - 1 + x])
+        return legs
+
+    def reduce_c(self, ref, land, send, recv):
+        legs = []
+        for m in range(self.micro):
+            for x in range(self.xn):
+                legs += swap_legs(
+                    self.line_c, lambda i, m=m, x=x: self.at(ref, m, x, i), lambda j, i, m=m, x=x: land.at[m, x],
+                    lambda j, m=m, x=x: send.at[m, self.xn - 1 + x], lambda j, m=m, x=x: recv.at[m, self.xn - 1 + x])
+        return legs
+
+    def reduce_x(self, ref, land, send, recv):
+        legs = []
+        for m in range(self.micro):
+            legs += swap_legs(
+                self.line_x, lambda i, m=m: self.at(ref, m, i, self.c), lambda j, i, m=m: land.at[m, j],
+                lambda j, m=m: send.at[m, j], lambda j, m=m: recv.at[m, j])
+        return legs
+
+    def add_c(self, ref, land):
+        for m in range(self.micro):
+            for x in range(self.xn):
+                add_rows(ref.at[m], (x * 2 + self.c) * self.block, land.at[m, x], self.block)
+
+    def total_x(self, ref, land, out):
+        for m in range(self.micro):
+            @pl.loop(0, self.block // ROWS)
+            def _(i, m=m):
+                here = pl.ds(pl.multiple_of(i * ROWS, ROWS), ROWS)
+                total = ref[m, pl.ds(pl.multiple_of(self.e * self.block + i * ROWS, ROWS), ROWS), :].astype(F32)
+                for j in range(self.xn - 1):
+                    total = total + land[m, j, here, :].astype(F32)
+                out[m, here, :] = total
+
+
+def sum_over_parts(seq, columns, sent, got, send, recv):
+    flat = columns.T
+    sent[...] = flat[:8]
+    legs = swap_legs(seq.line, lambda i: sent, lambda j, i: got.at[j], lambda j: send.at[j], lambda j: recv.at[j])
+    start_legs(legs)
+    end_legs(legs)
+    total = sent[...]
+    for j in range(seq.line.size - 1):
+        total = total + got[j]
+    return jnp.concatenate([total] * 16, axis=0).T
+
+
+def back_kernel(
+    groups, parts, backed,
+    branch, merge, triple, queries, keys, values, mixed, probs, hat, inv, gains, cos, sin, part,
+    d_proj, d_in, grad_heads, grad_out, summed,
+    rows_all, merge_v, triple_v, q_v, k_v, v_v, mixed_v, probs_v, hat_v, d_mixed, d_qk, sums, partial, land_c, land_x, sent, got,
+    load, g_send, g_recv, s_send, s_recv, t_send, t_recv, *behind
+):
+    micro, block, width = branch.shape
+    seq = Sequence(parts, block, micro)
+    length = queries.shape[1]
+    tokens = micro * length
+    heads = queries.shape[2] // HD
+    scale = 1.0 / math.sqrt(HD)
+    loads = [pltpu.make_async_copy(a, b, load.at[i]) for i, (a, b) in enumerate((
+        (merge, merge_v), (mixed, mixed_v), (queries, q_v), (keys, k_v), (values, v_v), (probs, probs_v), (hat, hat_v), (triple, triple_v)))]
+    for copy in loads:
+        copy.start()
+    if backed:
+        back = Backdrop(groups, parts, part, summed, *behind)
+        greet_lines([seq.line] + back.near())
+        steps = back.chunks + back.LAG
+        step = back.step
+    else:
+        greet_lines([seq.line])
+        steps, step = 0, lambda t: None
+        summed[...] = jnp.zeros_like(summed)
+    for m in range(micro):
+        rows_all[m, pl.ds(pl.multiple_of(seq.e * block, block), block), :] = branch[m]
+    gather_x = seq.gather_x(rows_all, g_send, g_recv)
+    start_legs(gather_x)
+    step(0)
+    step(1)
+    end_legs(gather_x)
+    gather_c = seq.gather_c(rows_all, g_send, g_recv)
+    start_legs(gather_c)
+    step(2)
+    sums[...] = jnp.zeros_like(sums)
+    grad_heads[...] = jnp.zeros_like(grad_heads)
+    end_legs(gather_c)
+    for copy in loads[:2]:
+        copy.wait()
+    for m in range(micro):
+        d_mixed[m] = lax.dot_general(rows_all[m], merge_v[...], (((1,), (1,)), ((), ())), preferred_element_type=F32).astype(BF)
+
+    @pl.loop(0, width // 512)
+    def _(n):
+        cols = pl.ds(pl.multiple_of(n * 512, 512), 512)
+        total = lax.dot_general(mixed_v[0], rows_all[0, :, cols], (((0,), (0,)), ((), ())), preferred_element_type=F32)
+        for m in range(1, micro):
+            total = total + lax.dot_general(
+                mixed_v[m], rows_all[m, :, cols], (((0,), (0,)), ((), ())), preferred_element_type=F32)
+        grad_out[:, cols] = total.astype(BF)
+
+    for copy in loads[2:7]:
+        copy.wait()
+    lane = lax.broadcasted_iota(jnp.int32, (1, 128), 1)
+
+    def one_head(i):
+        m, h = lax.div(i, heads), lax.rem(i, heads)
+        cols = pl.ds(pl.multiple_of(h * HD, HD), HD)
+        here = pl.ds(pl.multiple_of(m * length, length), length)
+        d_m = d_mixed[m, :, cols]
+        weights = probs_v[m, h]
+        low = weights.astype(BF)
+        d_proj[2, here, cols] = lax.dot_general(low, d_m, (((0,), (0,)), ((), ())), preferred_element_type=F32).astype(BF)
+        d_w = lax.dot_general(d_m, v_v[m, :, cols], (((1,), (1,)), ((), ())), preferred_element_type=F32)
+        d_s = (weights * (d_w - jnp.sum(weights * d_w, axis=-1, keepdims=True))).astype(BF)
+        d_q = jnp.dot(d_s, k_v[m, :, cols], preferred_element_type=F32) * scale
+        d_k = lax.dot_general(d_s, q_v[m, :, cols], (((0,), (0,)), ((), ())), preferred_element_type=F32) * scale
+        marks = sums[here, :]
+        for c, d in enumerate((d_q, d_k)):
+            d = d * cos[...] - pltpu.roll(d, HD // 2, 1) * sin[...]
+            d_qk[c, here, cols] = d
+            product = d * hat_v[c, here, cols]
+            grad_heads[c: c + 1, cols] += jnp.sum(product, axis=0, keepdims=True)
+            marks = marks + jnp.where(lane == c, jnp.sum(product * gains[c: c + 1, cols], axis=-1, keepdims=True), 0.0)
+        sums[here, :] = marks
+
+    @pl.loop(0, micro * heads)
+    def _(i):
+        one_head(i)
+        step(i + 3)
+
+    done = 3 + micro * heads
+    sums[...] = sum_over_parts(seq, sums[...], sent, got, t_send, t_recv)
+
+    @pl.loop(0, tokens // 64)
+    def _(i):
+        here = pl.ds(pl.multiple_of(i * 64, 64), 64)
+        for c in range(2):
+            inner = sums[here, c: c + 1] * (1.0 / width)
+            d_proj[c, here, :] = (inv[here, c: c + 1] * (
+                d_qk[c, here, :] * gains[c: c + 1, :] - hat_v[c, here, :] * inner)).astype(BF)
+
+    loads[7].wait()
+
+    @pl.loop(0, width // 512)
+    def _(n):
+        cols = pl.ds(pl.multiple_of(n * 512, 512), 512)
+        for m in range(micro):
+            here = pl.ds(m * length, length)
+            total = lax.dot_general(d_proj[0, here, :], triple_v[0, cols, :], (((1,), (1,)), ((), ())), preferred_element_type=F32)
+            for c in (1, 2):
+                total = total + lax.dot_general(
+                    d_proj[c, here, :], triple_v[c, cols, :], (((1,), (1,)), ((), ())), preferred_element_type=F32)
+            partial[m, :, cols] = total.astype(BF)
+
+    reduce_c = seq.reduce_c(partial, land_c, s_send, s_recv)
+    start_legs(reduce_c)
+    end_legs(reduce_c)
+    seq.add_c(partial, land_c)
+    reduce_x = seq.reduce_x(partial, land_x, s_send, s_recv)
+    start_legs(reduce_x)
+    for t in range(done, max(done, steps - 1)):
+        step(t)
+    end_legs(reduce_x)
+    seq.total_x(partial, land_x, d_in)
+    if steps > done:
+        step(steps - 1)
+
+
+def attention_back(branch, merge, triple, queries, keys, values, mixed, probs, hat, inv, gains, cos, sin, part, collective_id):
+    groups, parts = lax.axis_size("grp"), lax.axis_size("ep")
+    micro, block, width = branch.shape
+    length, local_width = queries.shape[1:]
+    tokens = micro * length
+    backed = part is not None
+    behind = Backdrop.scratch(part.shape[0], width) if backed else []
+    summed = (part.shape[0], ROWS, width) if backed else (8, 128)
+    vmem = pl.BlockSpec(memory_space=pltpu.VMEM)
+    hbm = pl.BlockSpec(memory_space=pl.ANY)
+    xn = parts // 2
+    return pl.pallas_call(
+        functools.partial(back_kernel, groups, parts, backed),
+        out_shape=[
+            jax.ShapeDtypeStruct((3, tokens, local_width), BF),
+            jax.ShapeDtypeStruct((micro, block, width), F32),
+            jax.ShapeDtypeStruct((8, local_width), F32),
+            jax.ShapeDtypeStruct((local_width, width), BF),
+            jax.ShapeDtypeStruct(summed, BF if backed else F32),
+        ],
+        in_specs=[vmem] + [hbm] * 8 + [vmem] * 4 + [hbm],
+        out_specs=[vmem] * 5,
+        scratch_shapes=[
+            pltpu.VMEM((micro, length, width), BF),
+            pltpu.VMEM(merge.shape, BF),
+            pltpu.VMEM(triple.shape, BF),
+            pltpu.VMEM(queries.shape, BF),
+            pltpu.VMEM(queries.shape, BF),
+            pltpu.VMEM(queries.shape, BF),
+            pltpu.VMEM(queries.shape, BF),
+            pltpu.VMEM(probs.shape, F32),
+            pltpu.VMEM(hat.shape, F32),
+            pltpu.VMEM(queries.shape, BF),
+            pltpu.VMEM((2, tokens, local_width), F32),
+            pltpu.VMEM((tokens, 128), F32),
+            pltpu.VMEM((micro, length, width), BF),
+            pltpu.VMEM((micro, xn, block, width), BF),
+            pltpu.VMEM((micro, xn - 1, block, width), BF),
+            pltpu.VMEM((8, tokens), F32),
+            pltpu.VMEM((parts - 1, 8, tokens), F32),
+            pltpu.SemaphoreType.DMA((8,)),
+            pltpu.SemaphoreType.DMA((micro, 2 * xn - 1)),
+            pltpu.SemaphoreType.DMA((micro, 2 * xn - 1)),
+            pltpu.SemaphoreType.DMA((micro, 2 * xn - 1)),
+            pltpu.SemaphoreType.DMA((micro, 2 * xn - 1)),
+            pltpu.SemaphoreType.DMA((parts - 1,)),
+            pltpu.SemaphoreType.DMA((parts - 1,)),
+        ] + behind,
+        compiler_params=pltpu.CompilerParams(
+            collective_id=collective_id, has_side_effects=True, vmem_limit_bytes=58 * 2**20
+        ),
+        cost_estimate=pl.CostEstimate(flops=10**10, bytes_accessed=40 * 2**20, transcendentals=0),
+    )(branch, merge, triple, queries, keys, values, mixed, probs, hat, inv, gains, cos, sin,
+      part if backed else mixed)
+
+
+class BackGather:
+    LAG = 4
+
+    def __init__(self, groups, parts, own, out, local, send, recv):
+        self.core, self.first, self.second, self.long = lines(groups, parts)
+        self.own, self.out, self.local, self.send, self.recv = own, out, local, send, recv
+        self.chunks = own.shape[0]
+        pn, qn, zn = self.first.size, self.second.size, self.long.size
+        self.rz, self.rq, self.rp, self.rc = ROWS, ROWS * zn, ROWS * zn * qn, ROWS * zn * qn * pn
+
+    @staticmethod
+    def scratch(chunks):
+        major, minor, xn = mesh_sizes(lax.axis_size("grp"), lax.axis_size("ep"))
+        legs = major + minor + xn - 2
+        return [
+            pltpu.SemaphoreType.DMA((chunks,)),
+            pltpu.SemaphoreType.DMA((chunks, legs)),
+            pltpu.SemaphoreType.DMA((chunks, legs)),
+        ]
+
+    def near(self):
+        return [self.core, self.first, self.second, self.long]
+
+    def rows(self, k, start, size):
+        return self.out.at[k, pl.ds(pl.multiple_of(start, ROWS), size), :]
+
+    def mine(self, k):
+        c, p, q, z = self.core.place, self.first.place, self.second.place, self.long.place
+        return pltpu.make_async_copy(
+            self.own.at[k], self.rows(k, c * self.rc + p * self.rp + q * self.rq + z * self.rz, self.rz), self.local.at[k])
+
+    def hop(self, k, level):
+        c, p, q, z = self.core.place, self.first.place, self.second.place, self.long.place
+        pn, qn, zn = self.first.size, self.second.size, self.long.size
+        line, offset, at = [
+            (self.long, 0, lambda i: self.rows(k, c * self.rc + p * self.rp + q * self.rq + i * self.rz, self.rz)),
+            (self.second, zn - 1, lambda i: self.rows(k, c * self.rc + p * self.rp + i * self.rq, self.rq)),
+            (self.first, zn + qn - 2, lambda i: self.rows(k, c * self.rc + i * self.rp, self.rp)),
+            (self.core, zn + qn + pn - 3, lambda i: self.rows(k, i * self.rc, self.rc)),
+        ][level]
+        source = (lambda i: self.own.at[k]) if level == 0 else (lambda i: at(line.place))
+        return swap_legs(line, source, lambda j, i: at(i),
+                         lambda j: self.send.at[k, offset + j], lambda j: self.recv.at[k, offset + j])
+
+    def step(self, t):
+        for level in (3, 2, 1, 0):
+            k = t - level - 1
+
+            @pl.when((k >= 0) & (k < self.chunks))
+            def _(k=k, level=level):
+                end_legs(self.hop(k, level))
+                if level == 0:
+                    self.mine(k).wait()
+                if level < 3:
+                    start_legs(self.hop(k, level + 1))
+
+        @pl.when((t >= 0) & (t < self.chunks))
+        def _():
+            self.mine(t).start()
+            start_legs(self.hop(t, 0))
+
+
+def forward_kernel(
+    groups, parts, experts,
+    x, dy, routes, quota, gains, head_gains, cos, sin, docs_down, docs_across, triple, merge,
+    gathered, q_out, k_out, v_out, mixed, probs, hat, inv, hidden, ffn_in, dy_all,
+    dy_own, triple_v, merge_v, sums, partial, land_c, land_x, sent, got,
+    load, g_send, g_recv, s_send, s_recv, t_send, t_recv, *behind
+):
+    micro, block, width = x.shape
+    seq = Sequence(parts, block, micro)
+    length = gathered.shape[1]
+    tokens = micro * length
+    heads = q_out.shape[2] // HD
+    scale = 1.0 / math.sqrt(HD)
+    cuts = block // ROWS
+    loads = [pltpu.make_async_copy(triple, triple_v, load.at[0]), pltpu.make_async_copy(merge, merge_v, load.at[1])]
+    for copy in loads:
+        copy.start()
+    back = BackGather(groups, parts, dy_own, dy_all, *behind)
+    step, steps = back.step, back.chunks + back.LAG
+    lane = lax.broadcasted_iota(jnp.int32, (1, 128), 1)
+    earlier = (lax.broadcasted_iota(jnp.int32, (block, block), 1) < lax.broadcasted_iota(jnp.int32, (block, block), 0))
+    for m in range(micro):
+        @pl.loop(0, cuts)
+        def _(r, m=m):
+            here = pl.ds(pl.multiple_of(r * ROWS, ROWS), ROWS)
+            v = x[m, here, :].astype(F32)
+            v = v * lax.rsqrt(jnp.mean(v * v, axis=-1, keepdims=True) + EPS)
+            gathered[m, pl.ds(pl.multiple_of(seq.e * block + r * ROWS, ROWS), ROWS), :] = (v * gains[0:1, :]).astype(BF)
+    greet_lines([seq.line] + back.near())
+    gather_x = seq.gather_x(gathered, g_send, g_recv)
+    start_legs(gather_x)
+    for m in range(micro):
+        chosen = routes[m]
+        counts = jnp.zeros((block, 128), F32)
+        for j in range(TOP):
+            counts = counts + jnp.where(chosen[:, j: j + 1] == lane, 1.0, 0.0)
+        prior = jnp.dot(jnp.where(earlier, 1.0, 0.0).astype(BF), counts.astype(BF), preferred_element_type=F32)
+        keep = jnp.where((counts > 0.0) & (prior < quota[0:1, :]), 1.0, 0.0).astype(BF)
+        for r in range(cuts):
+            dy_own[m * cuts + r, :, :width] = dy[m, r * ROWS: (r + 1) * ROWS, :]
+            dy_own[m * cuts + r, :, width:] = keep[r * ROWS: (r + 1) * ROWS, :]
+    step(0)
+    end_legs(gather_x)
+    gather_c = seq.gather_c(gathered, g_send, g_recv)
+    start_legs(gather_c)
+    step(1)
+    loads[0].wait()
+    end_legs(gather_c)
+
+    @pl.loop(0, micro)
+    def _(m):
+        here = pl.ds(pl.multiple_of(m * length, length), length)
+        marks = jnp.zeros((length, 128), F32)
+        for c in range(2):
+            raw = jnp.dot(gathered[m], triple_v[c], preferred_element_type=F32)
+            hat[c, here, :] = raw
+            marks = marks + jnp.where(lane == c, jnp.sum(raw * raw, axis=-1, keepdims=True), 0.0)
+        sums[here, :] = marks
+        v_out[m] = jnp.dot(gathered[m], triple_v[2], preferred_element_type=F32).astype(BF)
+        step(m + 2)
+
+    done = micro + 2
+    inv[...] = lax.rsqrt(sum_over_parts(seq, sums[...], sent, got, t_send, t_recv) * (1.0 / width) + EPS)
+    loads[1].wait()
+
+    @pl.loop(0, micro * heads)
+    def _(i):
+        m, h = lax.div(i, heads), lax.rem(i, heads)
+        cols = pl.ds(pl.multiple_of(h * HD, HD), HD)
+        here = pl.ds(pl.multiple_of(m * length, length), length)
+        for c, to in enumerate((q_out, k_out)):
+            v = hat[c, here, cols] * inv[here, c: c + 1]
+            hat[c, here, cols] = v
+            v = v * head_gains[c: c + 1, cols]
+            to[m, :, cols] = (v * cos[...] + pltpu.roll(v, HD // 2, 1) * sin[...]).astype(BF)
+        scores = lax.dot_general(
+            q_out[m, :, cols], k_out[m, :, cols], (((1,), (1,)), ((), ())), preferred_element_type=F32) * scale
+        allowed = (docs_down[m] == docs_across[m]) & (
+            lax.broadcasted_iota(jnp.int32, (length, length), 1) <= lax.broadcasted_iota(jnp.int32, (length, length), 0))
+        scores = jnp.where(allowed, scores, NEG)
+        grown = jnp.exp(scores - jnp.max(scores, axis=-1, keepdims=True))
+        weights = grown / jnp.sum(grown, axis=-1, keepdims=True)
+        probs[m, h] = weights
+        mixed[m, :, cols] = jnp.dot(weights.astype(BF), v_out[m, :, cols], preferred_element_type=F32).astype(BF)
+
+        @pl.when(lax.rem(i, 2) == 1)
+        def _():
+            step(done + lax.div(i, 2))
+
+    done = done + micro * heads // 2
+
+    @pl.loop(0, width // 512)
+    def _(n):
+        cols = pl.ds(pl.multiple_of(n * 512, 512), 512)
+        for m in range(micro):
+            partial[m, :, cols] = jnp.dot(mixed[m], merge_v[:, cols], preferred_element_type=F32).astype(BF)
+
+    reduce_c = seq.reduce_c(partial, land_c, s_send, s_recv)
+    start_legs(reduce_c)
+    end_legs(reduce_c)
+    seq.add_c(partial, land_c)
+    reduce_x = seq.reduce_x(partial, land_x, s_send, s_recv)
+    start_legs(reduce_x)
+    step(done)
+    end_legs(reduce_x)
+    seq.total_x(partial, land_x, hidden)
+    for m in range(micro):
+        @pl.loop(0, cuts)
+        def _(r, m=m):
+            here = pl.ds(pl.multiple_of(r * ROWS, ROWS), ROWS)
+            v = hidden[m, here, :] + x[m, here, :].astype(F32)
+            hidden[m, here, :] = v
+            v = v * lax.rsqrt(jnp.mean(v * v, axis=-1, keepdims=True) + EPS)
+            ffn_in[m, here, :] = (v * gains[1:2, :]).astype(BF)
+    for t in range(done + 1, steps):
+        step(t)
+
+
+def attention_forward(x, dy, routes, quota, gains, head_gains, cos, sin, docs, triple, merge, experts, collective_id):
+    groups, parts = lax.axis_size("grp"), lax.axis_size("ep")
+    major, minor, xn = mesh_sizes(groups, parts)
+    micro, block, width = x.shape
+    length = docs.shape[1]
+    local_width = triple.shape[2]
+    heads = local_width // HD
+    tokens = micro * length
+    chunks = micro * block // ROWS
+    rows = 2 * xn * minor * major * ROWS
+    vmem = pl.BlockSpec(memory_space=pltpu.VMEM)
+    hbm = pl.BlockSpec(memory_space=pl.ANY)
+    low = jax.ShapeDtypeStruct((micro, length, local_width), BF)
+    quota = jnp.pad(quota.astype(F32), (0, 128 - experts)).reshape(1, 128)
+    return pl.pallas_call(
+        functools.partial(forward_kernel, groups, parts, experts),
+        out_shape=[
+            jax.ShapeDtypeStruct((micro, length, width), BF),
+            low, low, low, low,
+            jax.ShapeDtypeStruct((micro, heads, length, length), F32),
+            jax.ShapeDtypeStruct((2, tokens, local_width), F32),
+            jax.ShapeDtypeStruct((tokens, 128), F32),
+            jax.ShapeDtypeStruct((micro, block, width), F32),
+            jax.ShapeDtypeStruct((micro, block, width), BF),
+            jax.ShapeDtypeStruct((chunks, rows, width + 128), BF),
+        ],
+        in_specs=[vmem] * 10 + [hbm] * 2,
+        out_specs=[vmem] * 10 + [hbm],
+        scratch_shapes=[
+            pltpu.VMEM((chunks, ROWS, width + 128), BF),
+            pltpu.VMEM(triple.shape, BF),
+            pltpu.VMEM(merge.shape, BF),
+            pltpu.VMEM((tokens, 128), F32),
+            pltpu.VMEM((micro, length, width), BF),
+            pltpu.VMEM((micro, xn, block, width), BF),
+            pltpu.VMEM((micro, xn - 1, block, width), BF),
+            pltpu.VMEM((8, tokens), F32),
+            pltpu.VMEM((parts - 1, 8, tokens), F32),
+            pltpu.SemaphoreType.DMA((2,)),
+            pltpu.SemaphoreType.DMA((micro, 2 * xn - 1)),
+            pltpu.SemaphoreType.DMA((micro, 2 * xn - 1)),
+            pltpu.SemaphoreType.DMA((micro, 2 * xn - 1)),
+            pltpu.SemaphoreType.DMA((micro, 2 * xn - 1)),
+            pltpu.SemaphoreType.DMA((parts - 1,)),
+            pltpu.SemaphoreType.DMA((parts - 1,)),
+        ] + BackGather.scratch(chunks),
+        compiler_params=pltpu.CompilerParams(
+            collective_id=collective_id, has_side_effects=True, vmem_limit_bytes=56 * 2**20
+        ),
+        cost_estimate=pl.CostEstimate(flops=6 * 10**9, bytes_accessed=40 * 2**20, transcendentals=0),
+    )(x, dy, routes, quota, gains, head_gains, cos, sin, docs[:, :, None], docs[:, None, :], triple, merge)
 
 
 def per_device(
@@ -854,76 +1435,31 @@
     head_gains = probe_lookup_scalers.astype(F32)
     cos, sin = rope_tables(seq_len, HD)
     signed_sin = jnp.concatenate([-sin[:, : HD // 2], sin[:, HD // 2:]], axis=-1)
+    triple = triple_projection_matrix.transpose(1, 0, 2)
+    gathered, queries, keys, values, mixed, weights, qk_hat, qk_inv, hidden, ffn_in, dy_all = attention_forward(
+        block_entry_states, output_gradient, token_assignments, worker_quota_tallies, gains, head_gains, cos, signed_sin,
+        document_labels, triple, heads_merge_matrix, experts, 0)
+
+    fused = xs == minor and share % 128 == 0 and local_exp % 2 == 0 and 2 * xs * minor * major * ROWS <= 512
+    chunk_shape = (micro * local_rows // ROWS, 2, xs, minor, major, ROWS)
+    if fused:
+        dx_sum, moe_part, grad_widen, grad_shrink = experts_together(
+            ffn_in, dy_all, specialist_widen_matrix, specialist_shrink_matrix, dispatcher_matrix, 1)
+    else:
+        dx_sum, moe_part, grad_widen, grad_shrink = experts_apart(
+            ffn_in, dy_all, specialist_widen_matrix, specialist_shrink_matrix, dispatcher_matrix)
+    dx_sum = dx_sum.astype(F32).reshape(micro, local_rows, width + 128)
+    grad_widen = lax.all_to_all(grad_widen.reshape(groups, width // groups, -1), "grp", 0, 0, tiled=True)
+    grad_widen = spread(grad_widen, local_exp, share)
+    grad_shrink = grad_shrink.reshape(local_exp, share, width)
+
     expert_ids = jnp.arange(experts, dtype=jnp.int32)
-
-    hits = (token_assignments[..., None] == expert_ids).astype(jnp.int32)
-    counts = jnp.sum(hits, axis=2)
-    prior = jnp.cumsum(counts, axis=1) - counts
-    keep = jnp.where((counts > 0) & (prior < worker_quota_tallies), 1.0, 0.0).astype(F32)
-    keep_all = lax.all_gather(keep.astype(BF), ALL, axis=1, tiled=True).astype(F32)
-    keep_all = keep_all.reshape(micro, major, minor, xs, 2, local_rows // ROWS, ROWS, experts)
-    one = keep_all[:, :, :, :, 0].transpose(0, 4, 3, 2, 1, 5, 6)
-    two = keep_all[:, :, :, :, 1].transpose(0, 4, 3, 2, 1, 5, 6)
-    if xs == minor:
-        two = keep_all[:, :, :, :, 1].transpose(0, 4, 2, 3, 1, 5, 6)
-    keep_all = jnp.stack([one, two], axis=2).reshape(-1, experts)
-    fused = xs == minor and share % 128 == 0 and local_exp % 2 == 0 and 2 * xs * minor * major * ROWS <= 512
-
-    if fused:
-        dy_all = lax.all_gather(output_gradient, ALL, axis=1, tiled=True)
-    else:
-        dy_all = gather_all(output_gradient, 0)
-
-    skip = block_entry_states.astype(F32)
-    inv_first = lax.rsqrt(jnp.mean(skip * skip, axis=-1, keepdims=True) + EPS)
-    hat_first = skip * inv_first
-    attn_in = (hat_first * gains[0]).astype(BF)
-    gathered = lax.all_gather(attn_in, "ep", axis=1, tiled=True)
-    projected = jnp.einsum("mtd,dcf->cmtf", gathered, triple_projection_matrix, preferred_element_type=F32)
-    qk_raw = projected[:2]
-    squares = lax.psum(jnp.sum(qk_raw * qk_raw, axis=-1), "ep")
-    qk_inv = lax.rsqrt(squares / width + EPS)[..., None]
-    qk_hat = qk_raw * qk_inv
-    qk_n = (qk_hat * head_gains[:, None, None, :]).reshape(2, micro, seq_len, heads, HD).transpose(0, 1, 3, 2, 4)
-    qk = (qk_n * cos + swap_halves(qk_n) * signed_sin).astype(BF)
-    queries, keys = qk[0], qk[1]
-    values = projected[2].astype(BF).reshape(micro, seq_len, heads, HD).transpose(0, 2, 1, 3)
-    places = jnp.arange(seq_len, dtype=jnp.int32)
-    allowed = (document_labels[:, :, None] == document_labels[:, None, :]) & (places[None, :] <= places[:, None])
-    scores = jnp.einsum("mhsd,mhtd->mhst", queries, keys, preferred_element_type=F32) * scale
-    scores = jnp.where(allowed[:, None], scores, NEG)
-    exponent = jnp.exp(scores - jnp.max(scores, axis=-1, keepdims=True))
-    weights = exponent / jnp.sum(exponent, axis=-1, keepdims=True)
-    weights_low = weights.astype(BF)
-    mixed = jnp.einsum("mhst,mhtd->mshd", weights_low, values, preferred_element_type=F32)
-    mixed = mixed.astype(BF).reshape(micro, seq_len, local_width)
-    attention = lax.psum_scatter(
-        jnp.einsum("msf,fd->msd", mixed, heads_merge_matrix, preferred_element_type=F32).astype(BF),
-        "ep", scatter_dimension=1, tiled=True,
-    ).astype(F32)
-
-    hidden = skip + attention
+    counts = jnp.sum((token_assignments[..., None] == expert_ids).astype(jnp.int32), axis=2)
+    keep = (counts > 0) & (jnp.cumsum(counts, axis=1) - counts < worker_quota_tallies)
     inv_second = lax.rsqrt(jnp.mean(hidden * hidden, axis=-1, keepdims=True) + EPS)
     hat_second = hidden * inv_second
-    ffn_in = (hat_second * gains[1]).astype(BF)
-    chunk_shape = (micro * local_rows // ROWS, 2, xs, minor, major, ROWS)
-    keep_all = keep_all.reshape(chunk_shape[0], -1, experts)
-    if fused:
-        dx_sum, moe_part, grad_widen, grad_shrink = experts_together(
-            ffn_in, dy_all, specialist_widen_matrix, specialist_shrink_matrix, dispatcher_matrix, keep_all.astype(BF), 1)
-    else:
-        dx_sum, moe_part, grad_widen, grad_shrink = experts_apart(
-            ffn_in, dy_all, keep_all, specialist_widen_matrix, specialist_shrink_matrix, dispatcher_matrix)
-    dx_sum = dx_sum.astype(F32).reshape(micro, local_rows, width + 128)
-    grad_widen = lax.all_to_all(grad_widen.reshape(groups, width // groups, -1), "grp", 0, 0, tiled=True)
-    grad_widen = grad_widen.reshape(groups, width // groups, local_exp // 2, 2, 2, share)
-    grad_widen = grad_widen.transpose(2, 4, 1, 3, 0, 5).reshape(local_exp, width // groups, 2 * inner).astype(F32)
-    grad_shrink = grad_shrink.reshape(local_exp, share, width)
-    moe = scatter_all(moe_part.reshape(chunk_shape + (width,)), 3).astype(F32).reshape(micro, local_rows, width)
-    output = (hidden + moe).astype(BF)
-
     probs = jax.nn.softmax(jnp.einsum("mtd,de->mte", ffn_in, dispatcher_matrix, preferred_element_type=F32), axis=-1)
-    d_probs = dx_sum[..., width: width + experts] * keep
+    d_probs = jnp.where(keep, dx_sum[..., width: width + experts], 0.0)
     d_logits = probs * (d_probs - jnp.sum(probs * d_probs, axis=-1, keepdims=True))
     d_ffn = dx_sum[..., :width] + jnp.einsum("mte,de->mtd", d_logits, dispatcher_matrix.astype(F32), precision=HIGH)
     grad_router = jnp.einsum("mtd,mte->ed", ffn_in.astype(F32), d_logits, precision=HIGH)
@@ -932,28 +1468,17 @@
     d_hidden = adjoint + inv_second * (scaled - hat_second * jnp.mean(scaled * hat_second, axis=-1, keepdims=True))
     grad_second = jnp.sum(d_ffn * hat_second, axis=(0, 1))
 
-    branch = lax.all_gather(d_hidden.astype(BF), "ep", axis=1, tiled=True)
-    grad_out = jnp.einsum("msf,msd->fd", mixed, branch, preferred_element_type=F32)
-    d_mixed = jnp.einsum("msd,fd->msf", branch, heads_merge_matrix, preferred_element_type=F32).astype(BF)
-    d_mixed = d_mixed.reshape(micro, seq_len, heads, HD).transpose(0, 2, 1, 3)
-    d_weights = jnp.einsum("mhsd,mhtd->mhst", d_mixed, values, preferred_element_type=F32)
-    d_scores = (weights * (d_weights - jnp.sum(weights * d_weights, axis=-1, keepdims=True))).astype(BF)
-    d_values = jnp.einsum("mhst,mhsd->mthd", weights_low, d_mixed, preferred_element_type=F32)
-    d_queries = jnp.einsum("mhst,mhtd->mshd", d_scores, keys, preferred_element_type=F32) * scale
-    d_keys = jnp.einsum("mhst,mhsd->mthd", d_scores, queries, preferred_element_type=F32) * scale
-    d_qk = jnp.stack([d_queries, d_keys])
-    d_qk = d_qk * cos[:, None] - swap_halves(d_qk) * signed_sin[:, None]
-    d_qk = d_qk.reshape(2, micro, seq_len, local_width)
-    scaled = d_qk * head_gains[:, None, None, :]
-    inner_sums = lax.psum(jnp.sum(scaled * qk_hat, axis=-1), "ep")
-    d_qk_raw = qk_inv * (scaled - qk_hat * (inner_sums / width)[..., None])
-    grad_heads = jnp.sum(d_qk * qk_hat, axis=(1, 2))
-    d_proj = jnp.concatenate([d_qk_raw, d_values.reshape(1, micro, seq_len, local_width)]).astype(BF)
-    grad_qkv = jnp.einsum("mtd,cmtf->dcf", gathered, d_proj, preferred_element_type=F32)
-    d_attn_in = lax.psum_scatter(
-        jnp.einsum("cmtf,dcf->mtd", d_proj, triple_projection_matrix, preferred_element_type=F32).astype(BF),
-        "ep", scatter_dimension=1, tiled=True,
-    ).astype(F32)
+    d_proj, d_attn_in, grad_heads, grad_out, moe = attention_back(
+        d_hidden.astype(BF), heads_merge_matrix, triple, queries, keys, values, mixed, weights,
+        qk_hat, qk_inv, head_gains, cos, signed_sin, moe_part if fused else None, 5)
+    if not fused:
+        moe = scatter_all(moe_part.reshape(chunk_shape + (width,)), 3)
+    output = (hidden + moe.astype(F32).reshape(micro, local_rows, width)).astype(BF)
+    grad_heads = grad_heads[:2]
+    grad_qkv = jnp.einsum("td,ctf->cdf", gathered.reshape(-1, width), d_proj, preferred_element_type=F32).astype(BF)
+    skip = block_entry_states.astype(F32)
+    inv_first = lax.rsqrt(jnp.mean(skip * skip, axis=-1, keepdims=True) + EPS)
+    hat_first = skip * inv_first
     scaled = d_attn_in * gains[0]
     grad_input = d_hidden + inv_first * (scaled - hat_first * jnp.mean(scaled * hat_first, axis=-1, keepdims=True))
     grad_first = jnp.sum(d_attn_in * hat_first, axis=(0, 1))
@@ -964,12 +1489,14 @@
     small = major * minor * ROWS * 128
     misc_size = misc.shape[0]
     misc = jnp.pad(misc, (0, -misc_size % small)).reshape(1, minor, major, ROWS, -1).astype(BF)
-    spans = 4
-    qkv_cut = grad_qkv.astype(BF).reshape(spans, minor, major, -1, 3 * local_width)
-    out_cut = grad_out.astype(BF).reshape(1, minor, major, -1, width)
-    qkv_sum, out_sum, misc_sum = total_over_groups([qkv_cut, out_cut, misc], (spans, 1, 1), 4)
-    qkv_sum = qkv_sum.reshape(grad_qkv.shape).astype(F32)
-    out_sum = out_sum.reshape(grad_out.shape).astype(F32)
+    qkv_cut = grad_qkv.reshape(6, minor, major, -1, local_width)
+    out_low = grad_out
+    near = out_low[: local_width // 2].reshape(1, minor, major, -1, width)
+    far = out_low[local_width // 2:].reshape(1, major, minor, -1, width)
+    qkv_sum, near_sum, far_sum, misc_sum = total_over_groups(
+        [qkv_cut, near, far, misc], (False, False, True, False), 4)
+    qkv_sum = qkv_sum.reshape(3, width, local_width).astype(F32).transpose(1, 0, 2)
+    out_sum = jnp.concatenate([near_sum.reshape(-1, width), far_sum.reshape(-1, width)]).astype(F32)
     misc_sum = misc_sum.reshape(-1)[:misc_size].astype(F32)
     rows = misc_sum[: (2 + experts) * width].reshape(2 + experts, width)
     return (

time: 1010 us -> 790 us (0.78); the launches traced: 995 us -> 789 us
  Pallas kernels: 569 us -> 711 us
  local copies, waits for them, and re-layouts: 149 us -> 23.8 us
  waiting for transfers between devices: 112 us -> 0.01 us
  blocking collectives: 71.5 us -> 13.7 us
  matrix products: 40.8 us -> 9.98 us
  between operations: 16.4 us -> 0.96 us
    pallas_call x2 -> x4, Pallas kernels: 352 us -> 494 us  [the longest x1 181 us: total_over_groups(): pl.pallas_call(functools.partial(total_kernel, groups, parts, spans, far_...]
    all_gather x3 -> x0, waiting for transfers between devices: 111 us -> none  [the longest x1 67.2 us: per_device(): dy_all = lax.all_gather(output_gradient, ALL, axis=1, tiled=True)]
    convert_element_type x7 -> x1, local copies, waits for them, and re-layouts: 80.9 us -> 8.76 us  [per_device(): jnp.einsum('td,ctf->cdf', gathered.reshape(-1, width), d_proj, preferred_...]
    all_gather x1 -> x0, blocking collectives: 47.2 us -> none  [per_device(): lax.all_gather(keep.astype(BF), ALL, axis=1, tiled=True).astype(F32)]
    reshape x5 -> x1, local copies, waits for them, and re-layouts: 26.7 us -> 0.51 us  [attention_forward(): quota = jnp.pad(quota.astype(F32), (0, 128 - experts)).reshape(1, 128)]
    dot_general x11 -> x2, matrix products: 34 us -> 8.58 us  [the longest x1 8.25 us: per_device(): jnp.einsum('td,ctf->cdf', gathered.reshape(-1, width), d_proj, preferred_...]
    unnamed x99 -> x33, local copies, waits for them, and re-layouts: 27.7 us -> 8.99 us
    psum x2 -> x0, blocking collectives: 11.8 us -> none  [the longest x1 5.9 us: per_device(): inner_sums = lax.psum(jnp.sum(scaled * qk_hat, axis=-1), 'ep')]
  transfers between devices with their start and end apart: 6 -> 1, of which waited for: 3 -> 0; matrix products, arithmetic and copies ran while one was open for 10% -> 5% of each run, Pallas kernels for 35% -> 45%
where the time goes in v3:
time: 790 us; the launch traced here: 789 us
  Pallas kernels  711 us (90%)
  other arithmetic  25.3 us (3%)
  local copies, waits for them, and re-layouts  23.8 us (3%)
  blocking collectives  13.7 us (2%)
  matrix products  9.98 us (1%)
    pallas_call x1, Pallas kernels, experts_together(): pl.pallas_call(functools.partial(experts_kernel, groups, parts, local_row...  216 us
    pallas_call x1, Pallas kernels, total_over_groups(): pl.pallas_call(functools.partial(total_kernel, groups, parts, spans, far_...  181 us
    pallas_call x1, Pallas kernels, attention_back(): pl.pallas_call(functools.partial(back_kernel, groups, parts, backed), out...  175 us
    pallas_call x1, Pallas kernels, attention_forward(): pl.pallas_call(functools.partial(forward_kernel, groups, parts, experts),...  131 us
  transfers between devices with their start and end apart: 1, of which 0 were waited for; matrix products, arithmetic and copies ran while one was open for 5% of the time, Pallas kernels for 45%

profile of v3, /device:TPU:0, one launch (start us, length us, event | category | flops | bytes accessed | tf_op | source)
XLA Modules:
  0.0 789.4 jit_solution(17002519518777348240)
XLA Ops:
  0.7 1.2 fusion.12
  2.0 1.3 convert_element_type.56.head_gains.gains
  3.3 1.3 broadcast_in_dim.13.docs_across
  4.5 1.5 copy.50.docs_down
  6.1 1.4 copy.49.routes
  7.5 1.3 convert_element_type.55.gains
  10.0 1.1 copy.51
  12.8 131.0 %shard_map.187 = (bf16[2,256,2048]{2,1,0:T(8,128)(2,1)}, bf16[2,256,512]{2,1,0:T(8,128)(2,1)}, bf16[2,256,512]{2,1,0:T(8,128)(2,1)}, bf16[2,256,512]{2,1,0:T(8,1...) custom-call(bf16[2,64,2048]{2,1,0:T(8,128)(2,1)} %x.7, ...), custom_call_target="tpu_custom_call" | custom-call | flops 6000000000 | bytes 41943040 | tf_op jit(solution)/shard_map/pallas_call | solution.py:1368
  143.8 216.3 %shard_map.188 = (bf16[8,16,2176]{2,1,0:T(8,128)(2,1)}, bf16[8,512,2048]{2,1,0:T(8,128)(2,1)}, bf16[2048,1024]{1,0:T(8,128)(2,1)}, f32[512,2048]{1,0:T(8,128)}) custom-call(bf16[8,16,2048]{2,1,0:T(8,128)(2,1)} %bitcast.63, bf16[8,512,2176]{2,1,0:T(8,128)(2,1)} %get-tuple-element.35.dy, bf16[4,2048,2048]{2,1,0:T(8,128)(2,1)} %widen.1, ...), custom_call_target="tpu_custom_call" | custom-call | flops 77309411328 | bytes 83886080 | tf_op jit(solution)/shard_map/pallas_call | solution.py:733
  360.2 4.9 all-to-all-start
  365.9 1.1 bitcast_convert_fusion
  368.5 1.0 copy-done.1
  369.5 2.2 fusion.20.branch
  372.1 174.9 %shard_map.189 = (bf16[3,512,512]{2,1,0:T(8,128)(2,1)}, f32[2,64,2048]{2,1,0:T(8,128)}, f32[8,512]{1,0:T(8,128)}, bf16[512,2048]{1,0:T(8,128)(2,1)}, bf16[8,16,2048]{2,1,0:T(8,128)(2,1)}) custom-call(bf16[2,64,2048]{2,1,0:T(8,128)(2,1)} %fusion.20.branch, bf16[512,2048]{1,0:T(8,128)(2,1)} %merge.3, bf16[3,2048,512]{2,1,0:T(8,128)(2,1)} %bitcast.77, ...), custom_call_target="tpu_custom_call" | custom-call | flops 10000000000 | bytes 41943040 | tf_op jit(solution)/shard_map/pallas_call | solution.py:1129
  547.1 1.6 fusion.7
  548.7 13.7 %all-reduce.4 = bf16[18,2048]{1,0:T(8,128)(2,1)S(1)} all-reduce(f32[18,2048]{1,0:T(8,128)S(1)} %pad_maximum_fusion), channel_id=1, replica_groups=mesh['grp'=8,'ep'=4] {'ep'}, use_global_device_ids=true, to_apply=%region_11.12 | all-reduce | flops 36864 | bytes 221184 | tf_op jit(solution)/shard_map/psum | solution.py:1487
  563.3 8.2 %convert_bitcast_fusion.1 = bf16[3,2048,512]{1,2,0:T(8,128)(2,1)} fusion(bf16[3,512,512]{2,1,0:T(8,128)(2,1)} %get-tuple-element.47, bf16[512,2048,1]{1,0,2:T(8,128)(2,1)} %bitcast.78), kind=kOutput, calls=%fused_computation.1 | convolution fusion | flops 3224371200 | bytes 9961472 | tf_op jit(solution)/shard_map/td,ctf->cdf/dot_general | solution.py:1478
  571.6 8.8 %copy.58 = bf16[3,2048,512]{2,1,0:T(8,128)(2,1)} copy(bf16[3,2048,512]{1,2,0:T(8,128)(2,1)} %convert_bitcast_fusion.1) | data formatting | bytes 12582912 | tf_op jit(solution)/shard_map/convert_element_type | solution.py:1478
  580.5 180.8 %shard_map.190 = (bf16[6,2,4,128,512]{4,3,2,1,0:T(8,128)(2,1)}, bf16[1,2,4,32,2048]{4,3,2,1,0:T(8,128)(2,1)S(1)}, bf16[1,4,2,32,2048]{4,3,2,1,0:T(8,128)(2,1)S(1)}, bf16[1,2,4,16,384]{4,3,2,1,0:T(8,128)(2,1)S(1)}) custom-call(bf16[6,2,4,128,512]{4,3,2,1,0:T(8,128)(2,1)} %bitcast.59, bf16[1,2,4,32,2048]{4,3,2,1,0:T(8,128)(2,1)S(1)} %bitcast.56, ...), custom_call_target="tpu_custom_call" | custom-call | tf_op jit(solution)/shard_map/pallas_call | solution.py:420
  763.4 2.5 maximum_convert_fusion
  766.0 1.7 fusion.6
  767.7 9.4 %convert_bitcast_fusion = f32[2048,3,512]{2,0,1:T(8,128)} fusion(bf16[3,2048,512]{2,1,0:T(8,128)(2,1)} %bitcast.60), kind=kLoop, calls=%fused_computation | loop fusion | flops 3145728 | bytes 18874368 | tf_op jit(solution)/shard_map/transpose | solution.py:1498
  777.0 7.6 shard_map.191
  784.7 4.7 copy.67
  (66 shorter events, 8.8 us)
Async XLA Ops:
  360.1 5.0 copy-start.6
  360.1 5.0 copy-start.9
  360.1 5.3 copy-start.12
  360.1 5.3 copy-start.3
  360.1 5.5 copy-start.11
  360.2 7.0 copy-start
  360.2 416.9 %all-to-all-start = ((bf16[8,256,1024]{2,1,0:T(8,128)(2,1)}), bf16[8,256,1024]{2,1,0:T(8,128)(2,1)}, u32[]{:S(2)}, u32[]{:S(2)}) async-start(bf16[8,256,1024]{2,1,0:T(8,128)(2,1)} %bitcast.62), calls=%async_computation | async-start | bytes 8388608 | tf_op jit(solution)/shard_map/all_to_all | solution.py:1452
  365.1 2.3 copy-start.13
  368.5 1.0 copy-start.1
  571.6 8.8 %copy-start.7 = (bf16[512,2048]{1,0:T(8,128)(2,1)S(1)}, bf16[512,2048]{1,0:T(8,128)(2,1)}, u32[]{:S(2)}) copy-start(bf16[512,2048]{1,0:T(8,128)(2,1)} %get-tuple-element.49) | copy-start | bytes 6291460
  762.8 3.2 copy-start.2
  762.8 3.2 copy-start.4
  762.8 3.2 copy-start.5
  762.8 3.2 copy-start.8
  762.8 3.2 copy-start.10

commit v4 on v3

--- a/solution.py
+++ b/solution.py
@@ -3,6 +3,7 @@
 
 import jax
 import jax.numpy as jnp
+import numpy as np
 from jax import lax
 from jax.experimental import pallas as pl
 from jax.experimental.pallas import tpu as pltpu
@@ -21,21 +22,11 @@
 F32 = jnp.float32
 
 
-def apply_silu(v):
-    return v * jax.nn.sigmoid(v)
-
-
 def rope_tables(length, head_dim):
     half = head_dim // 2
-    freq = THETA ** (-jnp.arange(half, dtype=F32) * 2.0 / head_dim)
-    angle = jnp.arange(length, dtype=F32)[:, None] * freq[None, :]
-    angle = jnp.concatenate([angle, angle], axis=-1)
-    return (jnp.cos(angle), jnp.sin(angle))
-
-
-def swap_halves(v):
-    half = v.shape[-1] // 2
-    return jnp.concatenate([v[..., half:], v[..., :half]], axis=-1)
+    angle = np.arange(length)[:, None] * THETA ** (-np.arange(half) * 2.0 / head_dim)
+    cos, sin = np.cos(angle), np.sin(angle)
+    return np.concatenate([cos, cos], 1).astype(np.float32), np.concatenate([-sin, sin], 1).astype(np.float32)
 
 
 def mesh_sizes(groups, parts):
@@ -68,9 +59,13 @@
     return Line(2, core, (0, 1)), first, second, Line(major, lax.div(g, minor), (minor, 0))
 
 
-def greet(some):
+def greet(some, whole=()):
     barrier = pltpu.get_barrier_semaphore()
-    peers = 0
+    peers = sum(line.size - 1 for line in whole)
+    for line in whole:
+        for j in range(1, line.size):
+            to = lax.rem(line.place + j, line.size)
+            pl.semaphore_signal(barrier, inc=1, device_id=line.at(to - line.place), device_id_type=MESH)
     for line in some:
         if line.size == 2:
             pl.semaphore_signal(barrier, inc=1, device_id=line.at(1 - 2 * line.place), device_id_type=MESH)
@@ -346,23 +341,73 @@
     return jnp.concatenate([call(part[i:i + per]) for i in range(0, chunks, per)]) if per < chunks else call(part)
 
 
-def total_kernel(groups, parts, spans, far_first, *refs):
-    count = len(spans)
-    ins, outs = refs[:count], refs[count:2 * count]
-    acc, land_y, land_z = refs[2 * count:3 * count], refs[3 * count:4 * count], refs[4 * count:5 * count]
-    local, stored, send, recv = refs[5 * count:]
+class Begun:
+    def __init__(self, hop, before):
+        self.hop, self.before = hop, before
+
+    def start(self):
+        self.before()
+        self.hop.start()
+
+    def arrive(self):
+        self.hop.arrive()
+
+    def sent(self):
+        self.hop.sent()
+
+
+def total_kernel(groups, parts, far_first, rows_in, d_proj, out_near, out_far, shared, own, *refs):
+    count = len(far_first)
+    outs, acc, land_one, land_two = (refs[i * count: (i + 1) * count] for i in range(4))
+    rows_v, proj_v, shared_v, own_v, got, local, stored, send, recv, t_send, t_recv = refs[4 * count:]
     major, minor, _ = mesh_sizes(groups, parts)
-    g = lax.axis_index("grp")
+    g, e = lax.axis_index("grp"), lax.axis_index("ep")
     short = Line(minor, lax.rem(g, minor), (1, 0))
     long = Line(major, lax.div(g, minor), (minor, 0))
-    loads, chains, number = [], [], 0
+    whole = Line(parts, e, (0, 1))
+    width = rows_in.shape[1]
+    load = [pltpu.make_async_copy(a, b, local.at[i]) for i, (a, b) in enumerate((
+        (out_near, acc[0].at[0]), (out_far, acc[1].at[0]), (rows_in, rows_v), (d_proj, proj_v), (shared, shared_v), (own, own_v)))]
+    for copy in load:
+        copy.start()
+
+    def weights(k):
+        def act():
+            if k == 0:
+                load[2].wait()
+                load[3].wait()
+            halves = acc[2].shape[0] // 3
+            c, half = k // halves, k % halves
+            rows = math.prod(acc[2].shape[2:4])
+
+            @pl.loop(0, acc[2].shape[1])
+            def _(i):
+                cols = pl.ds(pl.multiple_of(half * (width // halves) + i * rows, rows), rows)
+                total = lax.dot_general(rows_v[:, cols], proj_v[c], (((0,), (0,)), ((), ())), preferred_element_type=F32)
+                acc[2][k, i] = total.astype(BF).reshape(acc[2].shape[2:])
+
+        return act
+
+    swap = swap_legs(whole, lambda i: shared_v, lambda j, i: got.at[j], lambda j: t_send.at[j], lambda j: t_recv.at[j])
+
+    def everyone():
+        end_legs(swap)
+        load[5].wait()
+
+        @pl.loop(0, major * minor)
+        def _(i):
+            where = (lax.div(i, major), lax.rem(i, major))
+            total = shared_v[where].astype(F32) + own_v[where].astype(F32)
+            for j in range(parts - 1):
+                total = total + got[(j,) + where].astype(F32)
+            acc[3][(0,) + where] = total.astype(BF)
+
+    before = {(0, 0): load[0].wait, (1, 0): load[1].wait, (3, 0): everyone}
+    chains, number = [], 0
     for j in range(count):
         one, two = (long, short) if far_first[j] else (short, long)
         y, z = one.place, two.place
-        for k in range(spans[j]):
-            load = pltpu.make_async_copy(ins[j].at[k], acc[j].at[k], local.at[number])
-            load.start()
-            loads.append(load)
+        for k in range(acc[j].shape[0]):
             store = pltpu.make_async_copy(acc[j].at[k, y, z], outs[j].at[k, y, z], stored.at[number])
             base = [0]
 
@@ -371,67 +416,66 @@
                 base[0] += leg_count(n)
                 return (lambda i: send.at[number, b + i]), (lambda i: recv.at[number, b + i])
 
-            down = reduce_hops(one, lambda i, j=j, k=k: acc[j].at[k, i], lambda i, j=j, k=k: land_y[j].at[k, i], add, *sems(one.size))
-            down += reduce_hops(two, lambda i, j=j, k=k, y=y: acc[j].at[k, y, i], lambda i, j=j, k=k: land_z[j].at[k, i], add, *sems(two.size))
+            down = reduce_hops(one, lambda i, j=j, k=k: acc[j].at[k, i], lambda i, j=j, k=k: land_one[j].at[k, i], add, *sems(one.size))
+            down += reduce_hops(two, lambda i, j=j, k=k, y=y: acc[j].at[k, y, i], lambda i, j=j, k=k: land_two[j].at[k, i], add, *sems(two.size))
             up = gather_hops(two, lambda i, j=j, k=k, y=y: outs[j].at[k, y, i], *sems(two.size))
             up += gather_hops(one, lambda i, j=j, k=k: outs[j].at[k, i], *sems(one.size))
-            chains.append((load, down, store, up))
+
+            def put(store=store):
+                store.start()
+                store.wait()
+
+            down[0] = Begun(down[0], before.get((j, k)) or weights(k))
+            up[0] = Begun(up[0], put)
+            chains.append(down + up)
             number += 1
-    greet([short, long])
-    whole = []
-    for load, down, store, up in chains:
-        hops = down + up
-        turn = len(down)
-
-        class Loaded:
-            def __init__(self, hop, before):
-                self.hop, self.before = hop, before
-
-            def start(self):
-                self.before()
-                self.hop.start()
-
-            def arrive(self):
-                self.hop.arrive()
-
-            def sent(self):
-                self.hop.sent()
-
-        def put(store=store):
-            store.start()
-            store.wait()
-
-        hops[0] = Loaded(hops[0], load.wait)
-        hops[turn] = Loaded(hops[turn], put)
-        whole.append(hops)
-    flow(whole)
-
-
-def total_over_groups(arrays, far_first, collective_id):
+    greet([short, long], [whole])
+    load[4].wait()
+    start_legs(swap)
+    flow(chains)
+
+
+def total_over_groups(gathered, d_proj, grad_out, shared, own, collective_id):
     groups, parts = lax.axis_size("grp"), lax.axis_size("ep")
     major, minor, _ = mesh_sizes(groups, parts)
+    tokens, width = gathered.shape
+    local_width = d_proj.shape[2]
+    half = grad_out.shape[0] // 2
+    shapes = [
+        (1, minor, major, half // groups, width),
+        (1, major, minor, half // groups, width),
+        (6, minor, major, 3 * width // 6 // groups, local_width),
+        (1,) + shared.shape,
+    ]
     legs = 2 * (leg_count(minor) + leg_count(major))
-    spans = tuple(a.shape[0] for a in arrays)
-    total = sum(spans)
-    any_spec = pl.BlockSpec(memory_space=pl.ANY)
-    scratch = [pltpu.VMEM(a.shape, BF) for a in arrays]
-    scratch += [pltpu.VMEM((a.shape[0], leg_count(a.shape[1])) + a.shape[2:], BF) for a in arrays]
-    scratch += [pltpu.VMEM((a.shape[0], leg_count(a.shape[2])) + a.shape[3:], BF) for a in arrays]
+    total = sum(a[0] for a in shapes)
+    hbm = pl.BlockSpec(memory_space=pl.ANY)
+    scratch = [pltpu.VMEM(a, BF) for a in shapes]
+    scratch += [pltpu.VMEM((a[0], leg_count(a[1])) + a[2:], BF) for a in shapes]
+    scratch += [pltpu.VMEM((a[0], leg_count(a[2])) + a[3:], BF) for a in shapes]
     return pl.pallas_call(
-        functools.partial(total_kernel, groups, parts, spans, far_first),
-        out_shape=[jax.ShapeDtypeStruct(a.shape, BF) for a in arrays],
-        in_specs=[any_spec] * len(arrays),
-        out_specs=[any_spec] * len(arrays),
+        functools.partial(total_kernel, groups, parts, (False, True, False, False)),
+        out_shape=[jax.ShapeDtypeStruct(a, BF) for a in shapes],
+        in_specs=[hbm] * 6,
+        out_specs=[hbm] * len(shapes),
         scratch_shapes=scratch + [
-            pltpu.SemaphoreType.DMA((total,)),
+            pltpu.VMEM(gathered.shape, BF),
+            pltpu.VMEM(d_proj.shape, BF),
+            pltpu.VMEM(shared.shape, BF),
+            pltpu.VMEM(shared.shape, BF),
+            pltpu.VMEM((parts - 1,) + shared.shape, BF),
+            pltpu.SemaphoreType.DMA((6,)),
             pltpu.SemaphoreType.DMA((total,)),
             pltpu.SemaphoreType.DMA((total, legs)),
             pltpu.SemaphoreType.DMA((total, legs)),
+            pltpu.SemaphoreType.DMA((parts - 1,)),
+            pltpu.SemaphoreType.DMA((parts - 1,)),
         ],
         compiler_params=pltpu.CompilerParams(
             collective_id=collective_id, has_side_effects=True, vmem_limit_bytes=48 * 2**20
         ),
-    )(*arrays)
+        cost_estimate=pl.CostEstimate(flops=6 * tokens * width * local_width, bytes_accessed=40 * 2**20, transcendentals=0),
+    )(gathered, d_proj, grad_out[:half].reshape(shapes[0][1:]), grad_out[half:].reshape(shapes[1][1:]), shared, own)
 
 
 def swap_legs(line, source, target, send, recv):
@@ -458,6 +502,27 @@
         out().wait_send()
 
 
+def add_and_send(acc, first, land, rows, line, send):
+    def add(place, count):
+        @pl.loop(0, count * rows // line.size // ROWS)
+        def _(i):
+            offset = place * (rows // line.size) + i * ROWS
+            here = pl.ds(pl.multiple_of(first + offset, ROWS), ROWS)
+            there = pl.ds(pl.multiple_of(offset, ROWS), ROWS)
+            total = acc[here, :].astype(F32)
+            for j in range(land.shape[0]):
+                total = total + land[j, there, :].astype(F32)
+            acc[here, :] = total.astype(acc.dtype)
+
+    if line.size == 2:
+        add(1 - line.place, 1)
+        send()
+        add(line.place, 1)
+    else:
+        add(0, line.size)
+        send()
+
+
 def add_rows(acc, first, land, rows):
     @pl.loop(0, rows // ROWS)
     def _(i):
@@ -468,16 +533,16 @@
 
 def experts_kernel(
     groups, parts, local_rows, ring, acc_ring, experts,
-    x, dy, widen, shrink, dispatch,
+    x, dy, widen, shrink,
     summed, moe, grad_widen, grad_shrink,
     xs, dys, wide, down, sum_wide, sum_down, stage, acc, other, land_c, land_p, land_q, land_z,
-    hid, raw, gated, d_gu, gate, d_gate,
+    hid, raw, gated, d_gu, gate, product, marks,
     load, dy_sem, stage_sem, g_send, g_recv, s_send, s_recv,
 ):
     core, first, second, long = lines(groups, parts)
     c, p, q, z = core.place, first.place, second.place, long.place
     pn, qn, zn = first.size, second.size, long.size
-    chunks, _, width = x.shape
+    chunks, width = x.shape[0], shrink.shape[2]
     local_exp, inner = shrink.shape[0], shrink.shape[1]
     share = inner // groups
     group, part = lax.axis_index("grp"), lax.axis_index("ep")
@@ -506,8 +571,6 @@
     dy_start = lambda k: dy_copy(k).start()
     dy_start(0)
     greet_lines([core, first, second, long])
-    sum_wide[...] = jnp.zeros_like(sum_wide)
-    sum_down[...] = jnp.zeros_like(sum_down)
 
     def rows_at(start, size):
         return pl.ds(pl.multiple_of(start, ROWS), size)
@@ -560,7 +623,7 @@
         def _():
             act(k)
 
-    lane = lax.broadcasted_iota(jnp.int32, (1, 128), 1)
+    tiles = width // 512
 
     def compute(k):
         buf, dyk = xs.at[lax.rem(k, ring)], dys.at[lax.rem(k, 2)]
@@ -576,62 +639,52 @@
         def _():
             dy_start(k + 1)
 
-        hid[:, :128] = jnp.dot(buf[...], dispatch[...], preferred_element_type=F32)
-
-        @pl.loop(0, rows // 64)
-        def _(i):
-            here = pl.ds(pl.multiple_of(i * 64, 64), 64)
-            logits = jnp.where(lane < experts, hid[here, :128], NEG)
-            grown = jnp.exp(logits - jnp.max(logits, axis=-1, keepdims=True))
-            probs = grown / jnp.sum(grown, axis=-1, keepdims=True)
-            gate[here, :] = probs * dyk[here, width:].astype(F32)
-            d_gate[here, :] = jnp.zeros((64, 128), F32)
-
         @pl.loop(0, pairs)
         def _(j):
             cols = pl.ds(pl.multiple_of(j * 4 * share, 4 * share), 4 * share)
             some = pl.ds(pl.multiple_of(j * 2 * share, 2 * share), 2 * share)
-            hid[...] = jnp.dot(buf[...], wide[:, cols], preferred_element_type=F32)
-            raw[...] = lax.dot_general(dyk[:, :width], down[some, :], (((1,), (1,)), ((), ())), preferred_element_type=F32)
+            to_up = pl.ds(pl.multiple_of(j * 4 * share + 2 * share, share), 2 * share)
+            to_gate = pl.ds(pl.multiple_of(j * 4 * share, share), 2 * share)
+            hid[...] = jnp.dot(buf[:, :width], wide[:, cols], preferred_element_type=F32)
+            raw[...] = lax.dot_general(dyk[...], down[some, :], (((1,), (1,)), ((), ())), preferred_element_type=F32)
+            gate[...] = jnp.dot(buf[:, width:], marks[:, some], preferred_element_type=F32)
 
             @pl.loop(0, rows // 32)
             def _(i):
                 here = pl.ds(pl.multiple_of(i * 32, 32), 32)
-                gates = gate[here, :]
-                marks = d_gate[here, :]
-                for e in range(2):
-                    mark = lane == base + 2 * j + e
-                    weight = jnp.sum(jnp.where(mark, gates, 0.0), axis=-1, keepdims=True)
-                    g = hid[here, e * share: (e + 1) * share]
-                    u = hid[here, (2 + e) * share: (3 + e) * share]
-                    d = raw[here, e * share: (e + 1) * share]
-                    sigma = jax.nn.sigmoid(g)
-                    swish = g * sigma
-                    act = swish * u
-                    marks = marks + jnp.where(mark, jnp.sum(act * d, axis=-1, keepdims=True), 0.0)
-                    d = d * weight
-                    gated[here, pl.ds(pl.multiple_of(j * 2 * share + e * share, share), share)] = (act * weight).astype(BF)
-                    d_gu[here, pl.ds(pl.multiple_of(j * 4 * share + e * share, share), share)] = (
-                        d * u * (sigma + swish * (1.0 - sigma))).astype(BF)
-                    d_gu[here, pl.ds(pl.multiple_of(j * 4 * share + (2 + e) * share, share), share)] = (d * swish).astype(BF)
-                d_gate[here, :] = marks
-
-        tiles = width // 512
-
-        def input_grads(half, to):
-            here = pl.ds(pl.multiple_of(half * rc, rc), rc)
-
-            @pl.loop(0, tiles)
-            def _(n):
-                cols = pl.ds(pl.multiple_of(n * 512, 512), 512)
-                to[:, cols] = lax.dot_general(
-                    d_gu[here, :], wide[cols, :], (((1,), (1,)), ((), ())), preferred_element_type=F32).astype(BF)
-
-            to[:, width:] = d_gate[here, :].astype(BF)
-
-        input_grads(1 - c, other)
+                g, u = hid[here, : 2 * share], hid[here, 2 * share:]
+                d, weight = raw[here, :], gate[here, :]
+                sigma = 0.5 * jnp.tanh(0.5 * g) + 0.5
+                swish = g * sigma
+                act = swish * u
+                product[here, some] = (act * d).astype(BF)
+                gated[here, some] = (act * weight).astype(BF)
+                d = d * weight
+                d_gu[here, to_gate] = (d * u * (sigma + swish * (1.0 - sigma))).astype(BF)
+                d_gu[here, to_up] = (d * swish).astype(BF)
+
+        mine = acc.at[lax.rem(k, acc_ring)]
+
+        def split(cols, total):
+            @pl.when(c == 0)
+            def _():
+                mine[:, cols] = total[:rc].astype(BF)
+                other[:, cols] = total[rc:].astype(BF)
+
+            @pl.when(c == 1)
+            def _():
+                other[:, cols] = total[:rc].astype(BF)
+                mine[:, cols] = total[rc:].astype(BF)
+
+        @pl.loop(0, tiles)
+        def _(n):
+            cols = pl.ds(pl.multiple_of(n * 512, 512), 512)
+            split(cols, lax.dot_general(
+                d_gu[...], wide[cols, :], (((1,), (1,)), ((), ())), preferred_element_type=F32))
+
+        split(pl.ds(width, 128), lax.dot_general(
+            product[...], marks[...], (((1,), (1,)), ((), ())), preferred_element_type=F32))
         start_legs(s_core(k))
-        input_grads(c, acc.at[lax.rem(k, acc_ring)])
         slot = lax.rem(k, 2)
 
         @pl.when(k >= 2)
@@ -659,24 +712,27 @@
 
     def end_second(k):
         end_legs(s_second(k))
-        for j in range(qn - 1):
-            add_rows(acc.at[lax.rem(k, acc_ring)], p * rp + q * rq, land_q.at[lax.rem(k, 2), j], rq)
-        start_legs(s_long(k))
+        add_and_send(acc.at[lax.rem(k, acc_ring)], p * rp + q * rq, land_q.at[lax.rem(k, 2)], rq, long, lambda: start_legs(s_long(k)))
 
     def end_first(k):
         end_legs(s_first(k))
-        for j in range(pn - 1):
-            add_rows(acc.at[lax.rem(k, acc_ring)], p * rp, land_p.at[lax.rem(k, 2), j], rp)
-        start_legs(s_second(k))
+        add_and_send(acc.at[lax.rem(k, acc_ring)], p * rp, land_p.at[lax.rem(k, 2)], rp, second, lambda: start_legs(s_second(k)))
 
     def end_core(k):
         end_legs(s_core(k))
-        add_rows(acc.at[lax.rem(k, acc_ring)], 0, land_c.at[lax.rem(k, 2), 0], rc)
-        start_legs(s_first(k))
+        add_and_send(acc.at[lax.rem(k, acc_ring)], 0, land_c.at[lax.rem(k, 2)], rc, first, lambda: start_legs(s_first(k)))
 
     def begin(k):
         xs[lax.rem(k, ring), rows_at(c * rc + p * rp + q * rq + z * rz, rz), :] = x[k]
         start_legs(g_long(k))
+
+        @pl.when(k == 0)
+        def _():
+            sum_wide[...] = jnp.zeros_like(sum_wide)
+            sum_down[...] = jnp.zeros_like(sum_down)
+            lanes = lax.broadcasted_iota(jnp.int32, marks.shape, 0)
+            owner = base + lax.div(lax.broadcasted_iota(jnp.int32, marks.shape, 1), share)
+            marks[...] = jnp.where((lanes == owner) | (lanes == owner + experts), 1.0, 0.0).astype(BF)
 
     def then(one, two):
         def act(k):
@@ -685,46 +741,60 @@
 
         return act
 
+    def wide_out(i):
+        here = pl.ds(pl.multiple_of(i * rows, rows), rows)
+        return pltpu.make_async_copy(d_gu, grad_widen.at[here, :], load.at[1])
+
+    out_down = pltpu.make_async_copy(sum_down, grad_shrink, load.at[0])
+
+    def store(i):
+        @pl.when(i == 0)
+        def _():
+            out_down.start()
+
+        @pl.when(i > 0)
+        def _():
+            wide_out(i - 1).wait()
+
+        d_gu[...] = sum_wide[pl.ds(pl.multiple_of(i * rows, rows), rows), :].astype(BF)
+        wide_out(i).start()
+
     @pl.loop(0, chunks + 8)
     def _(t):
-        after(t, 8, end_long)
-        after(t, 7, end_second)
-        after(t, 6, end_first)
-        after(t, 5, end_core)
         after(t, 4, lambda k: end_legs(g_core(k)))
         after(t, 3, then(g_first, g_core))
         after(t, 2, then(g_second, g_first))
         after(t, 1, then(g_long, g_second))
         after(t, 0, begin)
+        after(t, 8, end_long)
+        after(t, 7, end_second)
+        after(t, 6, end_first)
+        after(t, 5, end_core)
         after(t, 4, compute)
 
-    out_down = pltpu.make_async_copy(sum_down, grad_shrink, load.at[0])
-    out_down.start()
+        @pl.when((t >= chunks + 4) & (t < chunks + 4 + width // rows))
+        def _():
+            store(t - chunks - 4)
+
+    for i in range(4, width // rows):
+        store(i)
     for k in range(chunks - 2, chunks):
         pltpu.make_async_copy(stage.at[k % 2], moe.at[k], stage_sem.at[k % 2]).wait()
-    for i in range(width // rows):
-        here = pl.ds(i * rows, rows)
-        if i:
-            pltpu.make_async_copy(d_gu, grad_widen.at[here, :], load.at[1]).wait()
-        d_gu[...] = sum_wide[here, :].astype(BF)
-        pltpu.make_async_copy(d_gu, grad_widen.at[here, :], load.at[1]).start()
-    pltpu.make_async_copy(d_gu, grad_widen.at[pl.ds(0, rows), :], load.at[1]).wait()
+    wide_out(width // rows - 1).wait()
     out_down.wait()
 
 
-def experts_together(x, dy, widen, shrink, dispatch, collective_id):
-    experts = dispatch.shape[1]
-    dispatch = jnp.pad(dispatch, ((0, 0), (0, 128 - experts)))
+def experts_together(x, dy, widen, shrink, experts, collective_id):
     groups, parts = lax.axis_size("grp"), lax.axis_size("ep")
     major, minor, xn = mesh_sizes(groups, parts)
-    micro, local_rows, width = x.shape
-    x = x.reshape(-1, ROWS, width)
+    micro, local_rows, wide = x.shape
+    x = x.reshape(-1, ROWS, wide)
     chunks = x.shape[0]
-    local_exp, inner = shrink.shape[:2]
+    local_exp, inner, width = shrink.shape
     share = inner // groups
     hidden = local_exp * share
     half = ROWS * major * minor * xn
-    rows, wide = 2 * half, width + 128
+    rows = 2 * half
     ring, acc_ring = min(chunks, 6), 4
     legs = major + minor + xn - 2
     vmem = pl.BlockSpec(memory_space=pltpu.VMEM)
@@ -738,11 +808,11 @@
             jax.ShapeDtypeStruct((width, 2 * hidden), BF),
             jax.ShapeDtypeStruct((hidden, width), F32),
         ],
-        in_specs=[vmem, hbm, hbm, hbm, vmem],
+        in_specs=[vmem, hbm, hbm, hbm],
         out_specs=[vmem, hbm, hbm, hbm],
         scratch_shapes=[
-            pltpu.VMEM((ring, rows, width), BF),
-            pltpu.VMEM((2, rows, wide), BF),
+            pltpu.VMEM((ring, rows, wide), BF),
+            pltpu.VMEM((2, rows, width), BF),
             pltpu.VMEM((width, 2 * hidden), BF),
             pltpu.VMEM((hidden, width), BF),
             pltpu.VMEM((width, 2 * hidden), F32),
@@ -758,8 +828,9 @@
             pltpu.VMEM((rows, 2 * share), F32),
             pltpu.VMEM((rows, hidden), BF),
             pltpu.VMEM((rows, 2 * hidden), BF),
-            pltpu.VMEM((rows, 128), F32),
-            pltpu.VMEM((rows, 128), F32),
+            pltpu.VMEM((rows, 2 * share), F32),
+            pltpu.VMEM((rows, hidden), BF),
+            pltpu.VMEM((128, hidden), BF),
             pltpu.SemaphoreType.DMA((3 * local_exp,)),
             pltpu.SemaphoreType.DMA((2,)),
             pltpu.SemaphoreType.DMA((2,)),
@@ -772,10 +843,10 @@
             collective_id=collective_id, has_side_effects=True, vmem_limit_bytes=60 * 2**20
         ),
         cost_estimate=pl.CostEstimate(flops=flops, bytes_accessed=80 * 2**20, transcendentals=chunks * rows * hidden),
-    )(x, dy, widen, shrink, dispatch)
-
-
-def experts_apart(x, dy_all, specialist_widen_matrix, specialist_shrink_matrix, dispatcher_matrix):
+    )(x, dy, widen, shrink)
+
+
+def experts_apart(x, dy_all, specialist_widen_matrix, specialist_shrink_matrix, experts):
     groups, parts = lax.axis_size("grp"), lax.axis_size("ep")
     group, part = lax.axis_index("grp"), lax.axis_index("ep")
     local_exp, inner, width = specialist_shrink_matrix.shape
@@ -787,11 +858,10 @@
     shrink = lax.dynamic_index_in_dim(shrink, group, 1, keepdims=False).reshape(local_exp * share, width)
     x_all = gather_all(x, 1)
     chunk_shape = x_all.shape[:-1]
-    x_all, dy_all = x_all.reshape(-1, width), dy_all.reshape(x_all.shape[0] * ROWS * math.prod(chunk_shape[1:-1]), -1)
-    keep_all = dy_all[:, width: width + dispatcher_matrix.shape[1]].astype(F32)
-    dy_all = dy_all[:, :width]
-    router = jax.nn.softmax(jnp.dot(x_all, dispatcher_matrix, preferred_element_type=F32), axis=-1)
-    gate = lax.dynamic_slice_in_dim(router * keep_all, part * local_exp, local_exp, axis=1)
+    x_all, dy_all = x_all.reshape(-1, width + 128), dy_all.reshape(-1, width)
+    gate = x_all[:, width: width + experts].astype(F32) + x_all[:, width + experts: width + 2 * experts].astype(F32)
+    x_all = x_all[:, :width]
+    gate = lax.dynamic_slice_in_dim(gate, part * local_exp, local_exp, axis=1)
     gate = jnp.repeat(gate, share, axis=1)
     gate_up = jnp.dot(x_all, widen, preferred_element_type=F32)
     g, u = gate_up[:, : local_exp * share], gate_up[:, local_exp * share:]
@@ -835,7 +905,7 @@
 
 
 class Backdrop:
-    LAG = 4
+    LAG = 8
 
     def __init__(self, groups, parts, part, out, acc, land_c, land_p, land_q, land_z, local, send, recv):
         self.core, self.first, self.second, self.long = lines(groups, parts)
@@ -851,11 +921,11 @@
         half = ROWS * major * minor * xn
         legs = major + minor + xn - 2
         return [
-            pltpu.VMEM((4, half, width), BF),
-            pltpu.VMEM((2, 1, half, width), BF),
-            pltpu.VMEM((2, xn - 1, half // xn, width), BF),
-            pltpu.VMEM((2, minor - 1, half // xn // minor, width), BF),
-            pltpu.VMEM((2, major - 1, ROWS, width), BF),
+            pltpu.VMEM((8, half, width), BF),
+            pltpu.VMEM((4, 1, half, width), BF),
+            pltpu.VMEM((4, xn - 1, half // xn, width), BF),
+            pltpu.VMEM((4, minor - 1, half // xn // minor, width), BF),
+            pltpu.VMEM((4, major - 1, ROWS, width), BF),
             pltpu.SemaphoreType.DMA((chunks,)),
             pltpu.SemaphoreType.DMA((chunks, legs)),
             pltpu.SemaphoreType.DMA((chunks, legs)),
@@ -865,7 +935,7 @@
         return [self.core, self.first, self.second, self.long]
 
     def buf(self, k):
-        return self.acc.at[lax.rem(k, 4)]
+        return self.acc.at[lax.rem(k, 8)]
 
     def own(self, k):
         here = pl.ds(pl.multiple_of(self.core.place * self.rc, self.rc), self.rc)
@@ -882,7 +952,7 @@
             (self.long, pn + qn - 1, lambda i: self.buf(k).at[at(p * self.rp + q * self.rq + i * self.rz, self.rz), :]),
         ][level]
         land = self.lands[level]
-        return swap_legs(line, source, lambda j, i: land.at[lax.rem(k, 2), j],
+        return swap_legs(line, source, lambda j, i: land.at[lax.rem(k, 4), j],
                          lambda j: self.send.at[k, offset + j], lambda j: self.recv.at[k, offset + j])
 
     def end(self, k, level):
@@ -896,20 +966,19 @@
         if level == 3:
             total = self.buf(k)[pl.ds(pl.multiple_of(first, ROWS), size), :].astype(F32)
             for j in range(land.shape[1]):
-                total = total + land[lax.rem(k, 2), j].astype(F32)
+                total = total + land[lax.rem(k, 4), j].astype(F32)
             self.out[k] = total.astype(self.out.dtype)
         else:
-            for j in range(land.shape[1]):
-                add_rows(self.buf(k), first, land.at[lax.rem(k, 2), j], size)
-            start_legs(self.hop(k, level + 1))
+            add_and_send(self.buf(k), first, land.at[lax.rem(k, 4)], size, (self.first, self.second, self.long)[level],
+                         lambda: start_legs(self.hop(k, level + 1)))
 
     def begin(self, k):
+        start_legs(self.hop(k, 0))
         self.own(k).start()
-        start_legs(self.hop(k, 0))
 
     def step(self, t):
         for level in (3, 2, 1, 0):
-            k = t - level - 1
+            k = t - 2 * level - 2
 
             @pl.when((k >= 0) & (k < self.chunks))
             def _(k=k, level=level):
@@ -982,11 +1051,12 @@
                 out[m, here, :] = total
 
 
-def sum_over_parts(seq, columns, sent, got, send, recv):
+def sum_over_parts(seq, columns, sent, got, send, recv, meanwhile):
     flat = columns.T
     sent[...] = flat[:8]
     legs = swap_legs(seq.line, lambda i: sent, lambda j, i: got.at[j], lambda j: send.at[j], lambda j: recv.at[j])
     start_legs(legs)
+    meanwhile()
     end_legs(legs)
     total = sent[...]
     for j in range(seq.line.size - 1):
@@ -1026,10 +1096,11 @@
     start_legs(gather_x)
     step(0)
     step(1)
+    step(2)
     end_legs(gather_x)
     gather_c = seq.gather_c(rows_all, g_send, g_recv)
     start_legs(gather_c)
-    step(2)
+    step(3)
     sums[...] = jnp.zeros_like(sums)
     grad_heads[...] = jnp.zeros_like(grad_heads)
     end_legs(gather_c)
@@ -1037,6 +1108,7 @@
         copy.wait()
     for m in range(micro):
         d_mixed[m] = lax.dot_general(rows_all[m], merge_v[...], (((1,), (1,)), ((), ())), preferred_element_type=F32).astype(BF)
+    step(4)
 
     @pl.loop(0, width // 512)
     def _(n):
@@ -1047,6 +1119,7 @@
                 mixed_v[m], rows_all[m, :, cols], (((0,), (0,)), ((), ())), preferred_element_type=F32)
         grad_out[:, cols] = total.astype(BF)
 
+    step(5)
     for copy in loads[2:7]:
         copy.wait()
     lane = lax.broadcasted_iota(jnp.int32, (1, 128), 1)
@@ -1075,10 +1148,10 @@
     @pl.loop(0, micro * heads)
     def _(i):
         one_head(i)
-        step(i + 3)
-
-    done = 3 + micro * heads
-    sums[...] = sum_over_parts(seq, sums[...], sent, got, t_send, t_recv)
+        step(i + 6)
+
+    done = 7 + micro * heads
+    sums[...] = sum_over_parts(seq, sums[...], sent, got, t_send, t_recv, lambda: step(done - 1))
 
     @pl.loop(0, tokens // 64)
     def _(i):
@@ -1103,16 +1176,16 @@
 
     reduce_c = seq.reduce_c(partial, land_c, s_send, s_recv)
     start_legs(reduce_c)
+    step(done)
     end_legs(reduce_c)
     seq.add_c(partial, land_c)
     reduce_x = seq.reduce_x(partial, land_x, s_send, s_recv)
     start_legs(reduce_x)
-    for t in range(done, max(done, steps - 1)):
-        step(t)
+    step(done + 1)
     end_legs(reduce_x)
     seq.total_x(partial, land_x, d_in)
-    if steps > done:
-        step(steps - 1)
+    for t in range(done + 2, steps):
+        step(t)
 
 
 def attention_back(branch, merge, triple, queries, keys, values, mixed, probs, hat, inv, gains, cos, sin, part, collective_id):
@@ -1172,7 +1245,7 @@
 
 
 class BackGather:
-    LAG = 4
+    LAG = 8
 
     def __init__(self, groups, parts, own, out, local, send, recv):
         self.core, self.first, self.second, self.long = lines(groups, parts)
@@ -1217,7 +1290,7 @@
 
     def step(self, t):
         for level in (3, 2, 1, 0):
-            k = t - level - 1
+            k = t - 2 * level - 2
 
             @pl.when((k >= 0) & (k < self.chunks))
             def _(k=k, level=level):
@@ -1235,9 +1308,9 @@
 
 def forward_kernel(
     groups, parts, experts,
-    x, dy, routes, quota, gains, head_gains, cos, sin, docs_down, docs_across, triple, merge,
-    gathered, q_out, k_out, v_out, mixed, probs, hat, inv, hidden, ffn_in, dy_all,
-    dy_own, triple_v, merge_v, sums, partial, land_c, land_x, sent, got,
+    x, dy, routes, quota, gains, head_gains, cos, sin, docs_down, docs_across, dispatch, triple, merge,
+    gathered, q_out, k_out, v_out, mixed, probs, hat, inv, hidden, ffn_in, router, dy_all,
+    kept, triple_v, merge_v, sums, partial, land_c, land_x, sent, got,
     load, g_send, g_recv, s_send, s_recv, t_send, t_recv, *behind
 ):
     micro, block, width = x.shape
@@ -1250,7 +1323,7 @@
     loads = [pltpu.make_async_copy(triple, triple_v, load.at[0]), pltpu.make_async_copy(merge, merge_v, load.at[1])]
     for copy in loads:
         copy.start()
-    back = BackGather(groups, parts, dy_own, dy_all, *behind)
+    back = BackGather(groups, parts, dy, dy_all, *behind)
     step, steps = back.step, back.chunks + back.LAG
     lane = lax.broadcasted_iota(jnp.int32, (1, 128), 1)
     earlier = (lax.broadcasted_iota(jnp.int32, (block, block), 1) < lax.broadcasted_iota(jnp.int32, (block, block), 0))
@@ -1264,21 +1337,20 @@
     greet_lines([seq.line] + back.near())
     gather_x = seq.gather_x(gathered, g_send, g_recv)
     start_legs(gather_x)
+    step(0)
     for m in range(micro):
         chosen = routes[m]
         counts = jnp.zeros((block, 128), F32)
         for j in range(TOP):
             counts = counts + jnp.where(chosen[:, j: j + 1] == lane, 1.0, 0.0)
         prior = jnp.dot(jnp.where(earlier, 1.0, 0.0).astype(BF), counts.astype(BF), preferred_element_type=F32)
-        keep = jnp.where((counts > 0.0) & (prior < quota[0:1, :]), 1.0, 0.0).astype(BF)
-        for r in range(cuts):
-            dy_own[m * cuts + r, :, :width] = dy[m, r * ROWS: (r + 1) * ROWS, :]
-            dy_own[m * cuts + r, :, width:] = keep[r * ROWS: (r + 1) * ROWS, :]
-    step(0)
+        kept[m] = jnp.where((counts > 0.0) & (prior < quota[0:1, :]), 1.0, 0.0)
+    step(1)
+    step(2)
     end_legs(gather_x)
     gather_c = seq.gather_c(gathered, g_send, g_recv)
     start_legs(gather_c)
-    step(1)
+    step(3)
     loads[0].wait()
     end_legs(gather_c)
 
@@ -1292,10 +1364,11 @@
             marks = marks + jnp.where(lane == c, jnp.sum(raw * raw, axis=-1, keepdims=True), 0.0)
         sums[here, :] = marks
         v_out[m] = jnp.dot(gathered[m], triple_v[2], preferred_element_type=F32).astype(BF)
-        step(m + 2)
-
-    done = micro + 2
-    inv[...] = lax.rsqrt(sum_over_parts(seq, sums[...], sent, got, t_send, t_recv) * (1.0 / width) + EPS)
+        step(m + 4)
+
+    done = micro + 5
+    squares = sum_over_parts(seq, sums[...], sent, got, t_send, t_recv, lambda: step(done - 1))
+    inv[...] = lax.rsqrt(squares * (1.0 / width) + EPS)
     loads[1].wait()
 
     @pl.loop(0, micro * heads)
@@ -1317,12 +1390,9 @@
         weights = grown / jnp.sum(grown, axis=-1, keepdims=True)
         probs[m, h] = weights
         mixed[m, :, cols] = jnp.dot(weights.astype(BF), v_out[m, :, cols], preferred_element_type=F32).astype(BF)
-
-        @pl.when(lax.rem(i, 2) == 1)
-        def _():
-            step(done + lax.div(i, 2))
-
-    done = done + micro * heads // 2
+        step(done + i)
+
+    done = done + micro * heads
 
     @pl.loop(0, width // 512)
     def _(n):
@@ -1332,11 +1402,12 @@
 
     reduce_c = seq.reduce_c(partial, land_c, s_send, s_recv)
     start_legs(reduce_c)
+    step(done)
     end_legs(reduce_c)
     seq.add_c(partial, land_c)
     reduce_x = seq.reduce_x(partial, land_x, s_send, s_recv)
     start_legs(reduce_x)
-    step(done)
+    step(done + 1)
     end_legs(reduce_x)
     seq.total_x(partial, land_x, hidden)
     for m in range(micro):
@@ -1346,12 +1417,20 @@
             v = hidden[m, here, :] + x[m, here, :].astype(F32)
             hidden[m, here, :] = v
             v = v * lax.rsqrt(jnp.mean(v * v, axis=-1, keepdims=True) + EPS)
-            ffn_in[m, here, :] = (v * gains[1:2, :]).astype(BF)
-    for t in range(done + 1, steps):
+            ffn_in[m, here, :width] = (v * gains[1:2, :]).astype(BF)
+        logits = jnp.dot(ffn_in[m, :, :width], dispatch[...], preferred_element_type=F32)
+        logits = jnp.where(lane < experts, logits, NEG)
+        grown = jnp.exp(logits - jnp.max(logits, axis=-1, keepdims=True))
+        grown = grown / jnp.sum(grown, axis=-1, keepdims=True)
+        gate = grown * kept[m]
+        router[m] = grown + pltpu.roll(kept[m], experts, 1)
+        head = gate.astype(BF).astype(F32)
+        ffn_in[m, :, width:] = (head + pltpu.roll(gate - head, experts, 1)).astype(BF)
+    for t in range(done + 2, steps):
         step(t)
 
 
-def attention_forward(x, dy, routes, quota, gains, head_gains, cos, sin, docs, triple, merge, experts, collective_id):
+def attention_forward(x, dy, routes, quota, gains, head_gains, cos, sin, docs, dispatch, triple, merge, collective_id):
     groups, parts = lax.axis_size("grp"), lax.axis_size("ep")
     major, minor, xn = mesh_sizes(groups, parts)
     micro, block, width = x.shape
@@ -1364,6 +1443,8 @@
     vmem = pl.BlockSpec(memory_space=pltpu.VMEM)
     hbm = pl.BlockSpec(memory_space=pl.ANY)
     low = jax.ShapeDtypeStruct((micro, length, local_width), BF)
+    experts = dispatch.shape[1]
+    dispatch = jnp.pad(dispatch, ((0, 0), (0, 128 - experts)))
     quota = jnp.pad(quota.astype(F32), (0, 128 - experts)).reshape(1, 128)
     return pl.pallas_call(
         functools.partial(forward_kernel, groups, parts, experts),
@@ -1374,13 +1455,14 @@
             jax.ShapeDtypeStruct((2, tokens, local_width), F32),
             jax.ShapeDtypeStruct((tokens, 128), F32),
             jax.ShapeDtypeStruct((micro, block, width), F32),
-            jax.ShapeDtypeStruct((micro, block, width), BF),
-            jax.ShapeDtypeStruct((chunks, rows, width + 128), BF),
+            jax.ShapeDtypeStruct((micro, block, width + 128), BF),
+            jax.ShapeDtypeStruct((micro, block, 128), F32),
+            jax.ShapeDtypeStruct((chunks, rows, width), BF),
         ],
-        in_specs=[vmem] * 10 + [hbm] * 2,
-        out_specs=[vmem] * 10 + [hbm],
+        in_specs=[vmem] * 11 + [hbm] * 2,
+        out_specs=[vmem] * 11 + [hbm],
         scratch_shapes=[
-            pltpu.VMEM((chunks, ROWS, width + 128), BF),
+            pltpu.VMEM((micro, block, 128), F32),
             pltpu.VMEM(triple.shape, BF),
             pltpu.VMEM(merge.shape, BF),
             pltpu.VMEM((tokens, 128), F32),
@@ -1401,7 +1483,8 @@
             collective_id=collective_id, has_side_effects=True, vmem_limit_bytes=56 * 2**20
         ),
         cost_estimate=pl.CostEstimate(flops=6 * 10**9, bytes_accessed=40 * 2**20, transcendentals=0),
-    )(x, dy, routes, quota, gains, head_gains, cos, sin, docs[:, :, None], docs[:, None, :], triple, merge)
+    )(x, dy.reshape(chunks, ROWS, width), routes, quota, gains, head_gains, cos, sin, docs[:, :, None], docs[:, None, :],
+      dispatch, triple, merge)
 
 
 def per_device(
@@ -1433,33 +1516,30 @@
     scale = 1.0 / math.sqrt(HD)
     gains = rescale_factors_both.astype(F32)
     head_gains = probe_lookup_scalers.astype(F32)
-    cos, sin = rope_tables(seq_len, HD)
-    signed_sin = jnp.concatenate([-sin[:, : HD // 2], sin[:, HD // 2:]], axis=-1)
+    cos, signed_sin = rope_tables(seq_len, HD)
     triple = triple_projection_matrix.transpose(1, 0, 2)
-    gathered, queries, keys, values, mixed, weights, qk_hat, qk_inv, hidden, ffn_in, dy_all = attention_forward(
+    gathered, queries, keys, values, mixed, weights, qk_hat, qk_inv, hidden, ffn_ext, probs, dy_all = attention_forward(
         block_entry_states, output_gradient, token_assignments, worker_quota_tallies, gains, head_gains, cos, signed_sin,
-        document_labels, triple, heads_merge_matrix, experts, 0)
+        document_labels, dispatcher_matrix, triple, heads_merge_matrix, 0)
+    ffn_in = ffn_ext[..., :width]
 
     fused = xs == minor and share % 128 == 0 and local_exp % 2 == 0 and 2 * xs * minor * major * ROWS <= 512
     chunk_shape = (micro * local_rows // ROWS, 2, xs, minor, major, ROWS)
     if fused:
         dx_sum, moe_part, grad_widen, grad_shrink = experts_together(
-            ffn_in, dy_all, specialist_widen_matrix, specialist_shrink_matrix, dispatcher_matrix, 1)
+            ffn_ext, dy_all, specialist_widen_matrix, specialist_shrink_matrix, experts, 1)
     else:
         dx_sum, moe_part, grad_widen, grad_shrink = experts_apart(
-            ffn_in, dy_all, specialist_widen_matrix, specialist_shrink_matrix, dispatcher_matrix)
+            ffn_ext, dy_all, specialist_widen_matrix, specialist_shrink_matrix, experts)
     dx_sum = dx_sum.astype(F32).reshape(micro, local_rows, width + 128)
     grad_widen = lax.all_to_all(grad_widen.reshape(groups, width // groups, -1), "grp", 0, 0, tiled=True)
     grad_widen = spread(grad_widen, local_exp, share)
     grad_shrink = grad_shrink.reshape(local_exp, share, width)
 
-    expert_ids = jnp.arange(experts, dtype=jnp.int32)
-    counts = jnp.sum((token_assignments[..., None] == expert_ids).astype(jnp.int32), axis=2)
-    keep = (counts > 0) & (jnp.cumsum(counts, axis=1) - counts < worker_quota_tallies)
     inv_second = lax.rsqrt(jnp.mean(hidden * hidden, axis=-1, keepdims=True) + EPS)
     hat_second = hidden * inv_second
-    probs = jax.nn.softmax(jnp.einsum("mtd,de->mte", ffn_in, dispatcher_matrix, preferred_element_type=F32), axis=-1)
-    d_probs = jnp.where(keep, dx_sum[..., width: width + experts], 0.0)
+    probs, keep = probs[..., :experts], probs[..., experts: 2 * experts]
+    d_probs = dx_sum[..., width: width + experts] * keep
     d_logits = probs * (d_probs - jnp.sum(probs * d_probs, axis=-1, keepdims=True))
     d_ffn = dx_sum[..., :width] + jnp.einsum("mte,de->mtd", d_logits, dispatcher_matrix.astype(F32), precision=HIGH)
     grad_router = jnp.einsum("mtd,mte->ed", ffn_in.astype(F32), d_logits, precision=HIGH)
@@ -1474,8 +1554,6 @@
     if not fused:
         moe = scatter_all(moe_part.reshape(chunk_shape + (width,)), 3)
     output = (hidden + moe.astype(F32).reshape(micro, local_rows, width)).astype(BF)
-    grad_heads = grad_heads[:2]
-    grad_qkv = jnp.einsum("td,ctf->cdf", gathered.reshape(-1, width), d_proj, preferred_element_type=F32).astype(BF)
     skip = block_entry_states.astype(F32)
     inv_first = lax.rsqrt(jnp.mean(skip * skip, axis=-1, keepdims=True) + EPS)
     hat_first = skip * inv_first
@@ -1483,21 +1561,18 @@
     grad_input = d_hidden + inv_first * (scaled - hat_first * jnp.mean(scaled * hat_first, axis=-1, keepdims=True))
     grad_first = jnp.sum(d_attn_in * hat_first, axis=(0, 1))
 
-    misc = jnp.concatenate([grad_first[None], grad_second[None], grad_router])
-    misc = lax.psum(misc, "ep").reshape(-1)
-    misc = jnp.concatenate([misc, grad_heads.reshape(-1)])
-    small = major * minor * ROWS * 128
-    misc_size = misc.shape[0]
-    misc = jnp.pad(misc, (0, -misc_size % small)).reshape(1, minor, major, ROWS, -1).astype(BF)
-    qkv_cut = grad_qkv.reshape(6, minor, major, -1, local_width)
-    out_low = grad_out
-    near = out_low[: local_width // 2].reshape(1, minor, major, -1, width)
-    far = out_low[local_width // 2:].reshape(1, major, minor, -1, width)
-    qkv_sum, near_sum, far_sum, misc_sum = total_over_groups(
-        [qkv_cut, near, far, misc], (False, False, True, False), 4)
+    shared = jnp.concatenate([grad_first[None], grad_second[None], grad_router]).reshape(-1).astype(BF)
+    own = grad_heads[:2].reshape(-1).astype(BF)
+    gap, size = shared.shape[0], shared.shape[0] + own.shape[0]
+    block = (minor, major, ROWS, -(-size // (groups * ROWS * 128)) * 128)
+    room = math.prod(block)
+    shared = jnp.pad(shared, (0, room - gap)).reshape(block)
+    own = jnp.pad(own, (gap, room - size)).reshape(block)
+    near_sum, far_sum, qkv_sum, misc_sum = total_over_groups(
+        gathered.reshape(-1, width), d_proj, grad_out, shared, own, 4)
     qkv_sum = qkv_sum.reshape(3, width, local_width).astype(F32).transpose(1, 0, 2)
     out_sum = jnp.concatenate([near_sum.reshape(-1, width), far_sum.reshape(-1, width)]).astype(F32)
-    misc_sum = misc_sum.reshape(-1)[:misc_size].astype(F32)
+    misc_sum = misc_sum.reshape(-1)[:size].astype(F32)
     rows = misc_sum[: (2 + experts) * width].reshape(2 + experts, width)
     return (
         output,

time: 790 us -> 712 us (0.901)
  Pallas kernels: 711 us -> 660 us
  blocking collectives: 13.7 us -> 0 us
  matrix products: 9.98 us -> 1.39 us
    pallas_call x1, Pallas kernels: 216 us -> 192 us  [experts_together(): pl.pallas_call(functools.partial(experts_kernel, groups, parts, local_row...]
    pallas_call x1, Pallas kernels: 175 us -> 151 us  [attention_back(): pl.pallas_call(functools.partial(back_kernel, groups, parts, backed), out...]
    pallas_call x1, Pallas kernels: 131 us -> 116 us  [attention_forward(): pl.pallas_call(functools.partial(forward_kernel, groups, parts, experts),...]
    psum x1 -> x0, blocking collectives: 13.7 us -> none  [per_device(): misc = lax.psum(misc, 'ep').reshape(-1)]
    pallas_call x1, Pallas kernels: 181 us -> 194 us  [total_over_groups(): pl.pallas_call(functools.partial(total_kernel, groups, parts, (False, Tru...]
    convert_element_type x2 -> x1, local copies, waits for them, and re-layouts: 8.81 us -> 0.05 us  [per_device(): jnp.concatenate([grad_first[None], grad_second[None], grad_router])]
    dot_general x2 -> x0, matrix products: 8.58 us -> none  [the longest x1 8.25 us: per_device(): jnp.einsum('td,ctf->cdf', gathered.reshape(-1, width), d_proj, preferred_...]
  transfers between devices with their start and end apart: 1 -> 1, of which waited for: 0 -> 0; matrix products, arithmetic and copies ran while one was open for 5% -> 4% of each run, Pallas kernels for 45% -> 49%
where the time goes in v4:
time: 712 us; the launch traced here: 708 us
  Pallas kernels  660 us (93%)
  other arithmetic  22.3 us (3%)
  local copies, waits for them, and re-layouts  18.5 us (3%)
    pallas_call x1, Pallas kernels, total_over_groups(): pl.pallas_call(functools.partial(total_kernel, groups, parts, (False, Tru...  194 us
    pallas_call x1, Pallas kernels, experts_together(): pl.pallas_call(functools.partial(experts_kernel, groups, parts, local_row...  192 us
    pallas_call x1, Pallas kernels, attention_back(): pl.pallas_call(functools.partial(back_kernel, groups, parts, backed), out...  151 us
    pallas_call x1, Pallas kernels, attention_forward(): pl.pallas_call(functools.partial(forward_kernel, groups, parts, experts),...  116 us
  transfers between devices with their start and end apart: 1, of which 0 were waited for; matrix products, arithmetic and copies ran while one was open for 4% of the time, Pallas kernels for 49%

profile of v4, /device:TPU:0, one launch (start us, length us, event | category | flops | bytes accessed | tf_op | source)
XLA Modules:
  0.0 708.5 jit_solution(2801329542741862374)
XLA Ops:
  0.6 1.3 convert_element_type.54.head_gains.gains
  1.9 1.1 copy.27
  3.0 1.3 broadcast_in_dim.20.docs_across
  4.3 1.5 copy.29.docs_down
  5.8 1.4 copy.28.routes
  7.3 1.3 convert_element_type.53.gains
  9.7 0.9 pad.17.dispatch
  10.6 116.2 %shard_map.205 = (bf16[2,256,2048]{2,1,0:T(8,128)(2,1)}, bf16[2,256,512]{2,1,0:T(8,128)(2,1)}, bf16[2,256,512]{2,1,0:T(8,128)(2,1)}, bf16[2,256,512]{2,1,0:T(8,1...) custom-call(bf16[2,64,2048]{2,1,0:T(8,128)(2,1)} %x.9, ...), custom_call_target="tpu_custom_call" | custom-call | flops 6000000000 | bytes 41943040 | tf_op jit(solution)/shard_map/pallas_call | solution.py:1449
  126.9 191.6 %shard_map.206 = (bf16[8,16,2176]{2,1,0:T(8,128)(2,1)}, bf16[8,512,2048]{2,1,0:T(8,128)(2,1)}, bf16[2048,1024]{1,0:T(8,128)(2,1)}, f32[512,2048]{1,0:T(8,128)}) custom-call(bf16[8,16,2176]{2,1,0:T(8,128)(2,1)} %bitcast.53, bf16[8,512,2048]{2,1,0:T(8,128)(2,1)} %get-tuple-element.36.dy, bf16[4,2048,2048]{2,1,0:T(8,128)(2,1)} %widen.1, ...), custom_call_target="tpu_custom_call" | custom-call | flops 77309411328 | bytes 83886080 | tf_op jit(solution)/shard_map/pallas_call | solution.py:803
  318.5 5.3 all-to-all-start
  324.5 1.0 multiply_reduce_fusion
  325.5 1.0 copy-done.2
  326.5 1.1 fusion.14.branch
  327.6 151.0 %shard_map.207 = (bf16[3,512,512]{2,1,0:T(8,128)(2,1)}, f32[2,64,2048]{2,1,0:T(8,128)}, f32[8,512]{1,0:T(8,128)}, bf16[512,2048]{1,0:T(8,128)(2,1)}, bf16[8,16,2048]{2,1,0:T(8,128)(2,1)}) custom-call(bf16[2,64,2048]{2,1,0:T(8,128)(2,1)} %fusion.14.branch, bf16[512,2048]{1,0:T(8,128)(2,1)} %merge.3, bf16[3,2048,512]{2,1,0:T(8,128)(2,1)} %bitcast.63, ...), custom_call_target="tpu_custom_call" | custom-call | flops 10000000000 | bytes 41943040 | tf_op jit(solution)/shard_map/pallas_call | solution.py:1202
  478.6 2.2 fusion.8
  482.3 1.9 fusion.15
  484.3 193.6 %shard_map.208 = (bf16[1,2,4,32,2048]{4,3,2,1,0:T(8,128)(2,1)S(1)}, bf16[1,4,2,32,2048]{4,3,2,1,0:T(8,128)(2,1)S(1)}, bf16[6,2,4,128,512]{4,3,2,1,0:T(8,128)(2,1)}, bf16[1,2,4,16,384]{4,3,2,1,0:T(8,128)(2,1)S(1)}) custom-call(bf16[512,2048]{1,0:T(8,128)(2,1)} %bitcast.64, bf16[3,512,512]{2,1,0:T(8,128)(2,1)S(1)} %copy-done, ...), custom_call_target="tpu_custom_call" | custom-call | flops 3221225472 | bytes 41943040 | tf_op jit(solution)/shard_map/pallas_call | solution.py:456
  678.9 1.6 slice.81
  681.1 0.8 broadcast_multiply_fusion
  682.5 2.5 maximum_convert_fusion
  685.1 1.7 fusion.7
  686.8 9.4 %convert_bitcast_fusion = f32[2048,3,512]{2,0,1:T(8,128)} fusion(bf16[3,2048,512]{2,1,0:T(8,128)(2,1)} %bitcast.47), kind=kLoop, calls=%fused_computation | loop fusion | flops 3145728 | bytes 18874368 | tf_op jit(solution)/shard_map/transpose | solution.py:1573
  696.2 7.6 %shard_map.209 = f32[4,256,2048]{2,1,0:T(8,128)} custom-call(bf16[8,256,1024]{2,1,0:T(8,128)(2,1)} %all-to-all-done.x), custom_call_target="tpu_custom_call" | custom-call | tf_op jit(solution)/shard_map/pallas_call | solution.py:898
  703.8 4.7 copy.36
  (69 shorter events, 5.5 us)
Async XLA Ops:
  318.5 5.4 copy-start.4
  318.5 5.6 copy-start.14
  318.5 5.6 copy-start.10
  318.5 5.7 copy-start.1
  318.5 5.8 copy-start.9
  318.5 6.0 copy-start.13
  318.5 377.6 %all-to-all-start = ((bf16[8,256,1024]{2,1,0:T(8,128)(2,1)}), bf16[8,256,1024]{2,1,0:T(8,128)(2,1)}, u32[]{:S(2)}, u32[]{:S(2)}) async-start(bf16[8,256,1024]{2,1,0:T(8,128)(2,1)} %bitcast.49), calls=%async_computation | async-start | bytes 8388608 | tf_op jit(solution)/shard_map/all_to_all | solution.py:1535
  323.8 2.6 copy-start.7
  324.5 154.1 %copy-start.15 = (f32[2,64]{1,0:T(2,128)}, f32[2,64]{1,0:T(2,128)S(1)}, u32[]{:S(2)}) copy-start(f32[2,64]{1,0:T(2,128)S(1)} %get-tuple-element.71) | copy-start | bytes 1540
  324.5 154.1 %copy-start.19 = (f32[2,64]{1,0:T(2,128)}, f32[2,64]{1,0:T(2,128)S(1)}, u32[]{:S(2)}) copy-start(f32[2,64]{1,0:T(2,128)S(1)} %get-tuple-element.70) | copy-start | bytes 1540
  325.5 1.0 copy-start.2
  325.5 2.1 copy-start.17
  327.6 153.2 %copy-start.12 = (bf16[2,64,2176]{2,1,0:T(8,128)(2,1)S(1)}, bf16[2,64,2176]{2,1,0:T(8,128)(2,1)}, u32[]{:S(2)}) copy-start(bf16[2,64,2176]{2,1,0:T(8,128)(2,1)} %get-tuple-element.35) | copy-start | bytes 1671172
  482.3 2.0 copy-start
  678.0 7.1 %copy-start.16 = (f32[2,64]{1,0:T(2,128)S(1)}, f32[2,64]{1,0:T(2,128)}, u32[]{:S(2)}) copy-start(f32[2,64]{1,0:T(2,128)} %copy-done.15) | copy-start | bytes 1540
  678.0 7.1 copy-start.18
  678.0 7.1 copy-start.20
  681.1 4.0 copy-start.3
  681.1 4.0 copy-start.5
  681.1 4.0 copy-start.6
  681.1 4.0 copy-start.8
  681.1 4.0 copy-start.11

commit v5 on v4

--- a/solution.py
+++ b/solution.py
@@ -190,11 +190,13 @@
     return 1 if n == 2 else 2 * (n - 1)
 
 
-def flow(chains):
+def flow(chains, pace=1):
     depth, count = max(len(c) for c in chains), len(chains)
-    for t in range(count + depth):
+    for t in range(count + pace * depth):
         for k in range(count):
-            i = t - k
+            i, rest = divmod(t - k, pace)
+            if rest:
+                continue
             if 1 <= i <= len(chains[k]):
                 chains[k][i - 1].arrive()
             if 0 <= i < len(chains[k]):
@@ -356,10 +358,10 @@
         self.hop.sent()
 
 
-def total_kernel(groups, parts, far_first, rows_in, d_proj, out_near, out_far, shared, own, *refs):
-    count = len(far_first)
-    outs, acc, land_one, land_two = (refs[i * count: (i + 1) * count] for i in range(4))
-    rows_v, proj_v, shared_v, own_v, got, local, stored, send, recv, t_send, t_recv = refs[4 * count:]
+def total_kernel(groups, parts, plan, rows_in, d_proj, grad_out, shared, own, *refs):
+    count = 3
+    outs, acc, land = (refs[i * count: (i + 1) * count] for i in range(3))
+    rows_v, proj_v, shared_v, own_v, got, local, stored, send, recv, t_send, t_recv = refs[3 * count:]
     major, minor, _ = mesh_sizes(groups, parts)
     g, e = lax.axis_index("grp"), lax.axis_index("ep")
     short = Line(minor, lax.rem(g, minor), (1, 0))
@@ -367,24 +369,25 @@
     whole = Line(parts, e, (0, 1))
     width = rows_in.shape[1]
     load = [pltpu.make_async_copy(a, b, local.at[i]) for i, (a, b) in enumerate((
-        (out_near, acc[0].at[0]), (out_far, acc[1].at[0]), (rows_in, rows_v), (d_proj, proj_v), (shared, shared_v), (own, own_v)))]
+        (grad_out, acc[0]), (rows_in, rows_v), (d_proj, proj_v), (shared, shared_v), (own, own_v)))]
     for copy in load:
         copy.start()
 
     def weights(k):
         def act():
             if k == 0:
+                load[1].wait()
                 load[2].wait()
-                load[3].wait()
-            halves = acc[2].shape[0] // 3
-            c, half = k // halves, k % halves
-            rows = math.prod(acc[2].shape[2:4])
-
-            @pl.loop(0, acc[2].shape[1])
+            cuts = acc[1].shape[0] // 3
+            c, cut = k // cuts, k % cuts
+            blocks = max(1, 256 // acc[1].shape[2])
+            rows = blocks * acc[1].shape[2]
+
+            @pl.loop(0, groups // blocks)
             def _(i):
-                cols = pl.ds(pl.multiple_of(half * (width // halves) + i * rows, rows), rows)
+                cols = pl.ds(pl.multiple_of(cut * (width // cuts) + i * rows, 128), rows)
                 total = lax.dot_general(rows_v[:, cols], proj_v[c], (((0,), (0,)), ((), ())), preferred_element_type=F32)
-                acc[2][k, i] = total.astype(BF).reshape(acc[2].shape[2:])
+                acc[1][k, pl.ds(i * blocks, blocks)] = total.astype(BF).reshape((blocks,) + acc[1].shape[2:])
 
         return act
 
@@ -392,47 +395,53 @@
 
     def everyone():
         end_legs(swap)
-        load[5].wait()
-
-        @pl.loop(0, major * minor)
+        load[4].wait()
+
+        @pl.loop(0, groups)
         def _(i):
-            where = (lax.div(i, major), lax.rem(i, major))
-            total = shared_v[where].astype(F32) + own_v[where].astype(F32)
+            total = shared_v[i].astype(F32) + own_v[i].astype(F32)
             for j in range(parts - 1):
-                total = total + got[(j,) + where].astype(F32)
-            acc[3][(0,) + where] = total.astype(BF)
-
-    before = {(0, 0): load[0].wait, (1, 0): load[1].wait, (3, 0): everyone}
-    chains, number = [], 0
-    for j in range(count):
-        one, two = (long, short) if far_first[j] else (short, long)
+                total = total + got[j, i].astype(F32)
+            acc[2][0, i] = total.astype(BF)
+
+    before = {(0, 0): load[0].wait, (2, 0): everyone}
+    chains = []
+    for number, (j, k, far) in enumerate(plan):
+        one, two = (long, short) if far else (short, long)
         y, z = one.place, two.place
-        for k in range(acc[j].shape[0]):
-            store = pltpu.make_async_copy(acc[j].at[k, y, z], outs[j].at[k, y, z], stored.at[number])
-            base = [0]
-
-            def sems(n, number=number, base=base):
-                b = base[0]
-                base[0] += leg_count(n)
-                return (lambda i: send.at[number, b + i]), (lambda i: recv.at[number, b + i])
-
-            down = reduce_hops(one, lambda i, j=j, k=k: acc[j].at[k, i], lambda i, j=j, k=k: land_one[j].at[k, i], add, *sems(one.size))
-            down += reduce_hops(two, lambda i, j=j, k=k, y=y: acc[j].at[k, y, i], lambda i, j=j, k=k: land_two[j].at[k, i], add, *sems(two.size))
-            up = gather_hops(two, lambda i, j=j, k=k, y=y: outs[j].at[k, y, i], *sems(two.size))
-            up += gather_hops(one, lambda i, j=j, k=k: outs[j].at[k, i], *sems(one.size))
-
-            def put(store=store):
-                store.start()
-                store.wait()
-
-            down[0] = Begun(down[0], before.get((j, k)) or weights(k))
-            up[0] = Begun(up[0], put)
-            chains.append(down + up)
-            number += 1
+        n = two.size
+
+        def level_one(ref, k, n=n):
+            return lambda i: ref.at[k, pl.ds(i * n, n)]
+
+        def level_two(ref, k, y=y, n=n):
+            return lambda i: ref.at[k, y * n + i]
+
+        store = pltpu.make_async_copy(acc[j].at[k, y * n + z], outs[j].at[k, y * n + z], stored.at[number])
+        base = [0]
+
+        def sems(size, number=number, base=base):
+            b = base[0]
+            base[0] += leg_count(size)
+            return (lambda i: send.at[number, b + i]), (lambda i: recv.at[number, b + i])
+
+        first_land = leg_count(one.size) * n
+        down = reduce_hops(one, level_one(acc[j], k), lambda i, j=j, k=k, n=n: land[j].at[k, pl.ds(i * n, n)], add, *sems(one.size))
+        down += reduce_hops(two, level_two(acc[j], k), lambda i, j=j, k=k, f=first_land: land[j].at[k, f + i], add, *sems(two.size))
+        up = gather_hops(two, level_two(outs[j], k), *sems(two.size))
+        up += gather_hops(one, level_one(outs[j], k), *sems(one.size))
+
+        def put(store=store):
+            store.start()
+            store.wait()
+
+        down[0] = Begun(down[0], before.get((j, k)) or (weights(k) if j == 1 else lambda: None))
+        up[0] = Begun(up[0], put)
+        chains.append(down + up)
     greet([short, long], [whole])
-    load[4].wait()
+    load[3].wait()
     start_legs(swap)
-    flow(chains)
+    flow(chains, 2)
 
 
 def total_over_groups(gathered, d_proj, grad_out, shared, own, collective_id):
@@ -440,23 +449,24 @@
     major, minor, _ = mesh_sizes(groups, parts)
     tokens, width = gathered.shape
     local_width = d_proj.shape[2]
-    half = grad_out.shape[0] // 2
+    few = max(n for n in (4, 2, 1) if n == 1 or grad_out.shape[0] % (n * groups * ROWS) == 0)
+    many = max(n for n in (12, 6, 3) if n == 3 or 3 * width % (n * groups * ROWS) == 0)
     shapes = [
-        (1, minor, major, half // groups, width),
-        (1, major, minor, half // groups, width),
-        (6, minor, major, 3 * width // 6 // groups, local_width),
+        (few, groups, grad_out.shape[0] // few // groups, width),
+        (many, groups, 3 * width // many // groups, local_width),
         (1,) + shared.shape,
     ]
+    plan = [(0, k, k % 4 == 1) for k in range(few)] + [(1, k, k % 4 == 1) for k in range(many)] + [(2, 0, False)]
+    blocks = max(leg_count(a) * b + leg_count(b) for a, b in ((minor, major), (major, minor)))
     legs = 2 * (leg_count(minor) + leg_count(major))
-    total = sum(a[0] for a in shapes)
+    total = len(plan)
     hbm = pl.BlockSpec(memory_space=pl.ANY)
     scratch = [pltpu.VMEM(a, BF) for a in shapes]
-    scratch += [pltpu.VMEM((a[0], leg_count(a[1])) + a[2:], BF) for a in shapes]
-    scratch += [pltpu.VMEM((a[0], leg_count(a[2])) + a[3:], BF) for a in shapes]
+    scratch += [pltpu.VMEM((a[0], blocks) + a[2:], BF) for a in shapes]
     return pl.pallas_call(
-        functools.partial(total_kernel, groups, parts, (False, True, False, False)),
+        functools.partial(total_kernel, groups, parts, plan),
         out_shape=[jax.ShapeDtypeStruct(a, BF) for a in shapes],
-        in_specs=[hbm] * 6,
+        in_specs=[hbm] * 5,
         out_specs=[hbm] * len(shapes),
         scratch_shapes=scratch + [
             pltpu.VMEM(gathered.shape, BF),
@@ -464,7 +474,7 @@
             pltpu.VMEM(shared.shape, BF),
             pltpu.VMEM(shared.shape, BF),
             pltpu.VMEM((parts - 1,) + shared.shape, BF),
-            pltpu.SemaphoreType.DMA((6,)),
+            pltpu.SemaphoreType.DMA((5,)),
             pltpu.SemaphoreType.DMA((total,)),
             pltpu.SemaphoreType.DMA((total, legs)),
             pltpu.SemaphoreType.DMA((total, legs)),
@@ -475,7 +485,7 @@
             collective_id=collective_id, has_side_effects=True, vmem_limit_bytes=48 * 2**20
         ),
         cost_estimate=pl.CostEstimate(flops=6 * tokens * width * local_width, bytes_accessed=40 * 2**20, transcendentals=0),
-    )(gathered, d_proj, grad_out[:half].reshape(shapes[0][1:]), grad_out[half:].reshape(shapes[1][1:]), shared, own)
+    )(gathered, d_proj, grad_out.reshape(shapes[0]), shared, own)
 
 
 def swap_legs(line, source, target, send, recv):
@@ -885,27 +895,38 @@
     return dx_sum, moe_part.reshape(chunk_shape + (width,)), grad_widen, grad_shrink
 
 
-def spread_kernel(share, x, out):
-    for i in range(x.shape[0]):
-        out[0, :, i * share: (i + 1) * share] = x[i].astype(F32)
-
-
-def spread(x, local_exp, share):
-    groups, rows, _ = x.shape
+def finish_kernel(share, qkv, out, wide, shrink, qkv_to, out_to, wide_to, shrink_to):
+    qkv_to[...] = qkv[...].astype(F32)
+    out_to[...] = out[...].astype(F32)
+    shrink_to[...] = shrink[...]
+    for i in range(wide.shape[0]):
+        wide_to[0, :, i * share: (i + 1) * share] = wide[i].astype(F32)
+
+
+def finish(qkv, out, wide, shrink, local_exp, share):
+    groups, rows, _ = wide.shape
+    whole = (local_exp, rows, 2 * groups * share)
     if share % 128:
-        x = x.reshape(groups, rows, local_exp // 2, 2, 2, share).transpose(2, 4, 1, 3, 0, 5)
-        return x.reshape(local_exp, rows, 2 * groups * share).astype(F32)
+        wide = wide.reshape(groups, rows, local_exp // 2, 2, 2, share).transpose(2, 4, 1, 3, 0, 5)
+        return qkv.astype(F32), out.astype(F32), wide.reshape(whole).astype(F32), shrink
+    steps = 2 * local_exp
+    cut = lambda a: pl.BlockSpec((a.shape[0] // (2 * steps), a.shape[1]), lambda i, j: (2 * i + j, 0))
+    outs = [jax.ShapeDtypeStruct(a.shape, F32) for a in (qkv, out)] + [
+        jax.ShapeDtypeStruct(whole, F32), jax.ShapeDtypeStruct(shrink.shape, F32)]
     return pl.pallas_call(
-        functools.partial(spread_kernel, share),
-        grid=(local_exp, 2),
-        out_shape=jax.ShapeDtypeStruct((local_exp, rows, 2 * groups * share), F32),
-        in_specs=[pl.BlockSpec((groups, rows, share), lambda e, h: (0, 0, e // 2 * 4 + h * 2 + e % 2))],
-        out_specs=pl.BlockSpec((1, rows, groups * share), lambda e, h: (e, 0, h)),
-    )(x)
+        functools.partial(finish_kernel, share),
+        grid=(steps, 2),
+        out_shape=outs,
+        in_specs=[cut(qkv), cut(out),
+                  pl.BlockSpec((groups, rows // 2, share), lambda i, j: (0, j, i // 4 * 4 + i % 2 * 2 + i // 2 % 2)), cut(shrink)],
+        out_specs=[cut(qkv), cut(out),
+                   pl.BlockSpec((1, rows // 2, groups * share), lambda i, j: (i // 2, j, i % 2)), cut(shrink)],
+        compiler_params=pltpu.CompilerParams(vmem_limit_bytes=40 * 2**20),
+    )(qkv, out, wide, shrink)
 
 
 class Backdrop:
-    LAG = 8
+    PACE = 2
 
     def __init__(self, groups, parts, part, out, acc, land_c, land_p, land_q, land_z, local, send, recv):
         self.core, self.first, self.second, self.long = lines(groups, parts)
@@ -914,18 +935,20 @@
         self.chunks = part.shape[0]
         pn, qn, zn = self.first.size, self.second.size, self.long.size
         self.rz, self.rq, self.rp, self.rc = ROWS, ROWS * zn, ROWS * zn * qn, ROWS * zn * qn * pn
+        self.levels = 3 + hop_count(zn)
+        self.lag = self.PACE * self.levels
 
     @staticmethod
     def scratch(chunks, width):
         major, minor, xn = mesh_sizes(lax.axis_size("grp"), lax.axis_size("ep"))
         half = ROWS * major * minor * xn
-        legs = major + minor + xn - 2
+        legs = minor + xn - 1 + leg_count(major)
         return [
-            pltpu.VMEM((8, half, width), BF),
+            pltpu.VMEM((min(chunks, 12), half, width), BF),
             pltpu.VMEM((4, 1, half, width), BF),
             pltpu.VMEM((4, xn - 1, half // xn, width), BF),
             pltpu.VMEM((4, minor - 1, half // xn // minor, width), BF),
-            pltpu.VMEM((4, major - 1, ROWS, width), BF),
+            pltpu.VMEM((chunks, leg_count(major), ROWS, width), BF),
             pltpu.SemaphoreType.DMA((chunks,)),
             pltpu.SemaphoreType.DMA((chunks, legs)),
             pltpu.SemaphoreType.DMA((chunks, legs)),
@@ -935,7 +958,7 @@
         return [self.core, self.first, self.second, self.long]
 
     def buf(self, k):
-        return self.acc.at[lax.rem(k, 8)]
+        return self.acc.at[lax.rem(k, self.acc.shape[0])]
 
     def own(self, k):
         here = pl.ds(pl.multiple_of(self.core.place * self.rc, self.rc), self.rc)
@@ -949,36 +972,48 @@
             (self.core, 0, lambda i: self.part.at[k, at(i * self.rc, self.rc), :]),
             (self.first, 1, lambda i: self.buf(k).at[at(i * self.rp, self.rp), :]),
             (self.second, pn, lambda i: self.buf(k).at[at(p * self.rp + i * self.rq, self.rq), :]),
-            (self.long, pn + qn - 1, lambda i: self.buf(k).at[at(p * self.rp + q * self.rq + i * self.rz, self.rz), :]),
         ][level]
         land = self.lands[level]
         return swap_legs(line, source, lambda j, i: land.at[lax.rem(k, 4), j],
                          lambda j: self.send.at[k, offset + j], lambda j: self.recv.at[k, offset + j])
 
+    def long_hop(self, k, number):
+        base = self.first.place * self.rp + self.second.place * self.rq
+        offset = self.first.size + self.second.size - 1
+        at = lambda i: self.buf(k).at[pl.ds(pl.multiple_of(base + i * self.rz, ROWS), self.rz), :]
+        land = self.lands[3].at[k]
+        return reduce_hops(self.long, at, lambda i: land.at[i], add,
+                           lambda i: self.send.at[k, offset + i], lambda i: self.recv.at[k, offset + i])[number]
+
     def end(self, k, level):
-        c, p, q, z = self.core.place, self.first.place, self.second.place, self.long.place
+        p, q, z = self.first.place, self.second.place, self.long.place
+        if level >= 3:
+            hop = self.long_hop(k, level - 3)
+            hop.arrive()
+            hop.sent()
+            if level + 1 < self.levels:
+                self.long_hop(k, level - 2).start()
+            else:
+                here = pl.ds(pl.multiple_of(p * self.rp + q * self.rq + z * self.rz, ROWS), ROWS)
+                self.out[k] = self.buf(k)[here, :]
+            return
         end_legs(self.hop(k, level))
         if level == 0:
             self.own(k).wait()
-        first = [0, p * self.rp, p * self.rp + q * self.rq, p * self.rp + q * self.rq + z * self.rz][level]
-        size = [self.rc, self.rp, self.rq, self.rz][level]
+        first = [0, p * self.rp, p * self.rp + q * self.rq][level]
+        size = [self.rc, self.rp, self.rq][level]
         land = self.lands[level]
-        if level == 3:
-            total = self.buf(k)[pl.ds(pl.multiple_of(first, ROWS), size), :].astype(F32)
-            for j in range(land.shape[1]):
-                total = total + land[lax.rem(k, 4), j].astype(F32)
-            self.out[k] = total.astype(self.out.dtype)
-        else:
-            add_and_send(self.buf(k), first, land.at[lax.rem(k, 4)], size, (self.first, self.second, self.long)[level],
-                         lambda: start_legs(self.hop(k, level + 1)))
+        line = (self.first, self.second, self.long)[level]
+        then = (lambda: start_legs(self.hop(k, level + 1))) if level < 2 else self.long_hop(k, 0).start
+        add_and_send(self.buf(k), first, land.at[lax.rem(k, 4)], size, line, then)
 
     def begin(self, k):
         start_legs(self.hop(k, 0))
         self.own(k).start()
 
     def step(self, t):
-        for level in (3, 2, 1, 0):
-            k = t - 2 * level - 2
+        for level in reversed(range(self.levels)):
+            k = t - self.PACE * (level + 1)
 
             @pl.when((k >= 0) & (k < self.chunks))
             def _(k=k, level=level):
@@ -1066,10 +1101,10 @@
 
 def back_kernel(
     groups, parts, backed,
-    branch, merge, triple, queries, keys, values, mixed, probs, hat, inv, gains, cos, sin, part,
-    d_proj, d_in, grad_heads, grad_out, summed,
-    rows_all, merge_v, triple_v, q_v, k_v, v_v, mixed_v, probs_v, hat_v, d_mixed, d_qk, sums, partial, land_c, land_x, sent, got,
-    load, g_send, g_recv, s_send, s_recv, t_send, t_recv, *behind
+    branch, merge, triple, queries, keys, values, mixed, probs, hat, inv, gains_in, cos, sin, wide, part,
+    d_proj, d_in, grad_heads, grad_out, wide_all, summed,
+    gains, rows_all, merge_v, triple_v, q_v, k_v, v_v, mixed_v, probs_v, hat_v, d_mixed, d_qk, sums, partial, land_c, land_x, sent, got,
+    load, g_send, g_recv, s_send, s_recv, t_send, t_recv, w_send, w_recv, *behind
 ):
     micro, block, width = branch.shape
     seq = Sequence(parts, block, micro)
@@ -1081,19 +1116,26 @@
         (merge, merge_v), (mixed, mixed_v), (queries, q_v), (keys, k_v), (values, v_v), (probs, probs_v), (hat, hat_v), (triple, triple_v)))]
     for copy in loads:
         copy.start()
+    gains[...] = gains_in[...].astype(F32)
+    over = Line(groups, lax.axis_index("grp"), (1, 0))
     if backed:
         back = Backdrop(groups, parts, part, summed, *behind)
-        greet_lines([seq.line] + back.near())
-        steps = back.chunks + back.LAG
+        greet_lines([seq.line, over] + back.near())
+        steps = back.chunks + back.lag
         step = back.step
     else:
-        greet_lines([seq.line])
+        greet_lines([seq.line, over])
         steps, step = 0, lambda t: None
         summed[...] = jnp.zeros_like(summed)
     for m in range(micro):
         rows_all[m, pl.ds(pl.multiple_of(seq.e * block, block), block), :] = branch[m]
     gather_x = seq.gather_x(rows_all, g_send, g_recv)
     start_legs(gather_x)
+    g = over.place
+    own_wide = pltpu.make_async_copy(wide.at[g], wide_all.at[g], load.at[8])
+    own_wide.start()
+    turn = swap_legs(over, lambda i: wide.at[i], lambda j, i: wide_all.at[i], lambda j: w_send.at[j], lambda j: w_recv.at[j])
+    start_legs(turn)
     step(0)
     step(1)
     step(2)
@@ -1186,9 +1228,11 @@
     seq.total_x(partial, land_x, d_in)
     for t in range(done + 2, steps):
         step(t)
-
-
-def attention_back(branch, merge, triple, queries, keys, values, mixed, probs, hat, inv, gains, cos, sin, part, collective_id):
+    end_legs(turn)
+    own_wide.wait()
+
+
+def attention_back(branch, merge, triple, queries, keys, values, mixed, probs, hat, inv, gains, cos, sin, wide, part, collective_id):
     groups, parts = lax.axis_size("grp"), lax.axis_size("ep")
     micro, block, width = branch.shape
     length, local_width = queries.shape[1:]
@@ -1206,11 +1250,13 @@
             jax.ShapeDtypeStruct((micro, block, width), F32),
             jax.ShapeDtypeStruct((8, local_width), F32),
             jax.ShapeDtypeStruct((local_width, width), BF),
+            jax.ShapeDtypeStruct(wide.shape, BF),
             jax.ShapeDtypeStruct(summed, BF if backed else F32),
         ],
-        in_specs=[vmem] + [hbm] * 8 + [vmem] * 4 + [hbm],
-        out_specs=[vmem] * 5,
+        in_specs=[vmem] + [hbm] * 8 + [vmem] * 4 + [hbm] * 2,
+        out_specs=[vmem] * 4 + [hbm, vmem],
         scratch_shapes=[
+            pltpu.VMEM(gains.shape, F32),
             pltpu.VMEM((micro, length, width), BF),
             pltpu.VMEM(merge.shape, BF),
             pltpu.VMEM(triple.shape, BF),
@@ -1228,24 +1274,27 @@
             pltpu.VMEM((micro, xn - 1, block, width), BF),
             pltpu.VMEM((8, tokens), F32),
             pltpu.VMEM((parts - 1, 8, tokens), F32),
-            pltpu.SemaphoreType.DMA((8,)),
+            pltpu.SemaphoreType.DMA((9,)),
             pltpu.SemaphoreType.DMA((micro, 2 * xn - 1)),
             pltpu.SemaphoreType.DMA((micro, 2 * xn - 1)),
             pltpu.SemaphoreType.DMA((micro, 2 * xn - 1)),
             pltpu.SemaphoreType.DMA((micro, 2 * xn - 1)),
             pltpu.SemaphoreType.DMA((parts - 1,)),
             pltpu.SemaphoreType.DMA((parts - 1,)),
+            pltpu.SemaphoreType.DMA((groups - 1,)),
+            pltpu.SemaphoreType.DMA((groups - 1,)),
         ] + behind,
         compiler_params=pltpu.CompilerParams(
             collective_id=collective_id, has_side_effects=True, vmem_limit_bytes=58 * 2**20
         ),
         cost_estimate=pl.CostEstimate(flops=10**10, bytes_accessed=40 * 2**20, transcendentals=0),
-    )(branch, merge, triple, queries, keys, values, mixed, probs, hat, inv, gains, cos, sin,
+    )(branch, merge, triple, queries, keys, values, mixed, probs, hat, inv, gains, cos, sin, wide,
       part if backed else mixed)
 
 
 class BackGather:
-    LAG = 8
+    PACE = 3
+    LAG = 4 * PACE
 
     def __init__(self, groups, parts, own, out, local, send, recv):
         self.core, self.first, self.second, self.long = lines(groups, parts)
@@ -1290,7 +1339,7 @@
 
     def step(self, t):
         for level in (3, 2, 1, 0):
-            k = t - 2 * level - 2
+            k = t - self.PACE * (level + 1)
 
             @pl.when((k >= 0) & (k < self.chunks))
             def _(k=k, level=level):
@@ -1308,9 +1357,9 @@
 
 def forward_kernel(
     groups, parts, experts,
-    x, dy, routes, quota, gains, head_gains, cos, sin, docs_down, docs_across, dispatch, triple, merge,
+    x, dy, routes, quota, gains_in, head_gains_in, cos, sin, docs, dispatch_in, triple, merge,
     gathered, q_out, k_out, v_out, mixed, probs, hat, inv, hidden, ffn_in, router, dy_all,
-    kept, triple_v, merge_v, sums, partial, land_c, land_x, sent, got,
+    kept, gains, head_gains, docs_down, dispatch, triple_v, merge_v, sums, partial, land_c, land_x, sent, got,
     load, g_send, g_recv, s_send, s_recv, t_send, t_recv, *behind
 ):
     micro, block, width = x.shape
@@ -1325,6 +1374,8 @@
         copy.start()
     back = BackGather(groups, parts, dy, dy_all, *behind)
     step, steps = back.step, back.chunks + back.LAG
+    gains[...] = gains_in[...].astype(F32)
+    head_gains[...] = head_gains_in[...].astype(F32)
     lane = lax.broadcasted_iota(jnp.int32, (1, 128), 1)
     earlier = (lax.broadcasted_iota(jnp.int32, (block, block), 1) < lax.broadcasted_iota(jnp.int32, (block, block), 0))
     for m in range(micro):
@@ -1338,13 +1389,17 @@
     gather_x = seq.gather_x(gathered, g_send, g_recv)
     start_legs(gather_x)
     step(0)
+    limits = jnp.concatenate([quota[...], jnp.zeros((1, 128 - experts), jnp.int32)], axis=1).astype(F32)
+    dispatch[...] = jnp.zeros_like(dispatch)
+    dispatch[:experts, :] = dispatch_in[...]
     for m in range(micro):
-        chosen = routes[m]
-        counts = jnp.zeros((block, 128), F32)
+        chosen = jnp.zeros((128, block), F32)
         for j in range(TOP):
-            counts = counts + jnp.where(chosen[:, j: j + 1] == lane, 1.0, 0.0)
+            chosen = chosen + jnp.where(routes[m, j: j + 1, :] == lax.broadcasted_iota(jnp.int32, (128, 1), 0), 1.0, 0.0)
+        counts = chosen.T
         prior = jnp.dot(jnp.where(earlier, 1.0, 0.0).astype(BF), counts.astype(BF), preferred_element_type=F32)
-        kept[m] = jnp.where((counts > 0.0) & (prior < quota[0:1, :]), 1.0, 0.0)
+        kept[m] = jnp.where((counts > 0.0) & (prior < limits), 1.0, 0.0)
+        docs_down[m] = jnp.broadcast_to(docs[m: m + 1, :], (128, length)).astype(F32).T
     step(1)
     step(2)
     end_legs(gather_x)
@@ -1383,7 +1438,7 @@
             to[m, :, cols] = (v * cos[...] + pltpu.roll(v, HD // 2, 1) * sin[...]).astype(BF)
         scores = lax.dot_general(
             q_out[m, :, cols], k_out[m, :, cols], (((1,), (1,)), ((), ())), preferred_element_type=F32) * scale
-        allowed = (docs_down[m] == docs_across[m]) & (
+        allowed = (docs_down[m][:, :1] == docs[pl.ds(m, 1), :].astype(F32)) & (
             lax.broadcasted_iota(jnp.int32, (length, length), 1) <= lax.broadcasted_iota(jnp.int32, (length, length), 0))
         scores = jnp.where(allowed, scores, NEG)
         grown = jnp.exp(scores - jnp.max(scores, axis=-1, keepdims=True))
@@ -1418,7 +1473,8 @@
             hidden[m, here, :] = v
             v = v * lax.rsqrt(jnp.mean(v * v, axis=-1, keepdims=True) + EPS)
             ffn_in[m, here, :width] = (v * gains[1:2, :]).astype(BF)
-        logits = jnp.dot(ffn_in[m, :, :width], dispatch[...], preferred_element_type=F32)
+        logits = lax.dot_general(
+            ffn_in[m, :, :width], dispatch[...], (((1,), (1,)), ((), ())), preferred_element_type=F32)
         logits = jnp.where(lane < experts, logits, NEG)
         grown = jnp.exp(logits - jnp.max(logits, axis=-1, keepdims=True))
         grown = grown / jnp.sum(grown, axis=-1, keepdims=True)
@@ -1444,8 +1500,6 @@
     hbm = pl.BlockSpec(memory_space=pl.ANY)
     low = jax.ShapeDtypeStruct((micro, length, local_width), BF)
     experts = dispatch.shape[1]
-    dispatch = jnp.pad(dispatch, ((0, 0), (0, 128 - experts)))
-    quota = jnp.pad(quota.astype(F32), (0, 128 - experts)).reshape(1, 128)
     return pl.pallas_call(
         functools.partial(forward_kernel, groups, parts, experts),
         out_shape=[
@@ -1459,10 +1513,14 @@
             jax.ShapeDtypeStruct((micro, block, 128), F32),
             jax.ShapeDtypeStruct((chunks, rows, width), BF),
         ],
-        in_specs=[vmem] * 11 + [hbm] * 2,
+        in_specs=[vmem] * 10 + [hbm] * 2,
         out_specs=[vmem] * 11 + [hbm],
         scratch_shapes=[
             pltpu.VMEM((micro, block, 128), F32),
+            pltpu.VMEM(gains.shape, F32),
+            pltpu.VMEM(head_gains.shape, F32),
+            pltpu.VMEM((micro, length, 128), F32),
+            pltpu.VMEM((128, width), BF),
             pltpu.VMEM(triple.shape, BF),
             pltpu.VMEM(merge.shape, BF),
             pltpu.VMEM((tokens, 128), F32),
@@ -1483,8 +1541,8 @@
             collective_id=collective_id, has_side_effects=True, vmem_limit_bytes=56 * 2**20
         ),
         cost_estimate=pl.CostEstimate(flops=6 * 10**9, bytes_accessed=40 * 2**20, transcendentals=0),
-    )(x, dy.reshape(chunks, ROWS, width), routes, quota, gains, head_gains, cos, sin, docs[:, :, None], docs[:, None, :],
-      dispatch, triple, merge)
+    )(x, dy.reshape(chunks, ROWS, width), routes.transpose(0, 2, 1), quota.reshape(1, -1), gains, head_gains, cos, sin, docs,
+      dispatch.T, triple, merge)
 
 
 def per_device(
@@ -1515,11 +1573,11 @@
     heads = local_width // HD
     scale = 1.0 / math.sqrt(HD)
     gains = rescale_factors_both.astype(F32)
-    head_gains = probe_lookup_scalers.astype(F32)
     cos, signed_sin = rope_tables(seq_len, HD)
     triple = triple_projection_matrix.transpose(1, 0, 2)
     gathered, queries, keys, values, mixed, weights, qk_hat, qk_inv, hidden, ffn_ext, probs, dy_all = attention_forward(
-        block_entry_states, output_gradient, token_assignments, worker_quota_tallies, gains, head_gains, cos, signed_sin,
+        block_entry_states, output_gradient, token_assignments, worker_quota_tallies, rescale_factors_both,
+        probe_lookup_scalers, cos, signed_sin,
         document_labels, dispatcher_matrix, triple, heads_merge_matrix, 0)
     ffn_in = ffn_ext[..., :width]
 
@@ -1532,9 +1590,7 @@
         dx_sum, moe_part, grad_widen, grad_shrink = experts_apart(
             ffn_ext, dy_all, specialist_widen_matrix, specialist_shrink_matrix, experts)
     dx_sum = dx_sum.astype(F32).reshape(micro, local_rows, width + 128)
-    grad_widen = lax.all_to_all(grad_widen.reshape(groups, width // groups, -1), "grp", 0, 0, tiled=True)
-    grad_widen = spread(grad_widen, local_exp, share)
-    grad_shrink = grad_shrink.reshape(local_exp, share, width)
+    grad_widen = grad_widen.reshape(groups, width // groups, -1)
 
     inv_second = lax.rsqrt(jnp.mean(hidden * hidden, axis=-1, keepdims=True) + EPS)
     hat_second = hidden * inv_second
@@ -1548,9 +1604,10 @@
     d_hidden = adjoint + inv_second * (scaled - hat_second * jnp.mean(scaled * hat_second, axis=-1, keepdims=True))
     grad_second = jnp.sum(d_ffn * hat_second, axis=(0, 1))
 
-    d_proj, d_attn_in, grad_heads, grad_out, moe = attention_back(
+    d_proj, d_attn_in, grad_heads, grad_out, grad_widen, moe = attention_back(
         d_hidden.astype(BF), heads_merge_matrix, triple, queries, keys, values, mixed, weights,
-        qk_hat, qk_inv, head_gains, cos, signed_sin, moe_part if fused else None, 5)
+        qk_hat, qk_inv, probe_lookup_scalers, cos, signed_sin, grad_widen,
+        moe_part if fused else None, 5)
     if not fused:
         moe = scatter_all(moe_part.reshape(chunk_shape + (width,)), 3)
     output = (hidden + moe.astype(F32).reshape(micro, local_rows, width)).astype(BF)
@@ -1564,14 +1621,16 @@
     shared = jnp.concatenate([grad_first[None], grad_second[None], grad_router]).reshape(-1).astype(BF)
     own = grad_heads[:2].reshape(-1).astype(BF)
     gap, size = shared.shape[0], shared.shape[0] + own.shape[0]
-    block = (minor, major, ROWS, -(-size // (groups * ROWS * 128)) * 128)
+    block = (groups, ROWS, -(-size // (groups * ROWS * 128)) * 128)
     room = math.prod(block)
     shared = jnp.pad(shared, (0, room - gap)).reshape(block)
     own = jnp.pad(own, (gap, room - size)).reshape(block)
-    near_sum, far_sum, qkv_sum, misc_sum = total_over_groups(
+    out_sum, qkv_sum, misc_sum = total_over_groups(
         gathered.reshape(-1, width), d_proj, grad_out, shared, own, 4)
-    qkv_sum = qkv_sum.reshape(3, width, local_width).astype(F32).transpose(1, 0, 2)
-    out_sum = jnp.concatenate([near_sum.reshape(-1, width), far_sum.reshape(-1, width)]).astype(F32)
+    qkv_sum, out_sum, grad_widen, grad_shrink = finish(
+        qkv_sum.reshape(-1, local_width), out_sum.reshape(-1, width), grad_widen, grad_shrink, local_exp, share)
+    qkv_sum = qkv_sum.reshape(3, width, local_width).transpose(1, 0, 2)
+    grad_shrink = grad_shrink.reshape(local_exp, share, width)
     misc_sum = misc_sum.reshape(-1)[:size].astype(F32)
     rows = misc_sum[: (2 + experts) * width].reshape(2 + experts, width)
     return (

time: 712 us -> 655 us (0.920)
  Pallas kernels: 660 us -> 637 us
  local copies, waits for them, and re-layouts: 18.5 us -> 4.05 us
  other arithmetic: 22.3 us -> 9.58 us
    pallas_call x2, Pallas kernels: 201 us -> 177 us  [the longest x1 162 us: total_over_groups(): pl.pallas_call(functools.partial(total_kernel, groups, parts, plan), out_...]
    transpose x1 -> x0, other arithmetic: 9.37 us -> none  [per_device(): qkv_sum.reshape(3, width, local_width).astype(F32).transpose(1, 0, 2)]
  transfers between devices with their start and end apart: 1 -> 0, of which waited for: 0 -> 0; matrix products, arithmetic and copies ran while one was open for 4% -> 0% of each run, Pallas kernels for 49% -> 0%
where the time goes in v5:
time: 655 us; the launch traced here: 653 us
  Pallas kernels  637 us (97%)
  other arithmetic  9.58 us (1%)
    pallas_call x1, Pallas kernels, experts_together(): pl.pallas_call(functools.partial(experts_kernel, groups, parts, local_row...  194 us
    pallas_call x1, Pallas kernels, total_over_groups(): pl.pallas_call(functools.partial(total_kernel, groups, parts, plan), out_...  162 us
    pallas_call x1, Pallas kernels, attention_back(): pl.pallas_call(functools.partial(back_kernel, groups, parts, backed), out...  155 us
    pallas_call x1, Pallas kernels, attention_forward(): pl.pallas_call(functools.partial(forward_kernel, groups, parts, experts),...  111 us
    pallas_call x1, Pallas kernels, finish(): pl.pallas_call(functools.partial(finish_kernel, share), grid=(steps, 2),...  15.3 us

profile of v5, /device:TPU:0, one launch (start us, length us, event | category | flops | bytes accessed | tf_op | source)
XLA Modules:
  0.0 652.9 jit_solution(5140355248931020222)
XLA Ops:
  0.6 110.6 %shard_map.205 = (bf16[2,256,2048]{2,1,0:T(8,128)(2,1)}, bf16[2,256,512]{2,1,0:T(8,128)(2,1)}, bf16[2,256,512]{2,1,0:T(8,128)(2,1)}, bf16[2,256,512]{2,1,0:T(8,1...) custom-call(bf16[2,64,2048]{2,1,0:T(8,128)(2,1)} %x.5, ...), custom_call_target="tpu_custom_call" | custom-call | flops 6000000000 | bytes 41943040 | tf_op jit(solution)/shard_map/pallas_call | solution.py:1503
  111.3 194.5 %shard_map.206 = (bf16[8,16,2176]{2,1,0:T(8,128)(2,1)}, bf16[8,512,2048]{2,1,0:T(8,128)(2,1)}, bf16[2048,1024]{1,0:T(8,128)(2,1)}, f32[512,2048]{1,0:T(8,128)}) custom-call(bf16[8,16,2176]{2,1,0:T(8,128)(2,1)} %bitcast.47, bf16[8,512,2048]{2,1,0:T(8,128)(2,1)} %get-tuple-element.40.dy, bf16[4,2048,2048]{2,1,0:T(8,128)(2,1)} %widen.1, ...), custom_call_target="tpu_custom_call" | custom-call | flops 77309411328 | bytes 83886080 | tf_op jit(solution)/shard_map/pallas_call | solution.py:813
  305.8 1.2 bitcast_convert_fusion
  307.1 0.2 multiply_reduce_fusion.3
  307.3 0.2 multiply_reduce_fusion.2
  307.4 0.2 fusion.9
  307.7 1.0 multiply_reduce_fusion
  308.7 1.2 fusion.14.branch
  309.8 154.6 %shard_map.207 = (bf16[3,512,512]{2,1,0:T(8,128)(2,1)}, f32[2,64,2048]{2,1,0:T(8,128)}, f32[8,512]{1,0:T(8,128)}, bf16[512,2048]{1,0:T(8,128)(2,1)}, bf16[8,256,...) custom-call(bf16[2,64,2048]{2,1,0:T(8,128)(2,1)} %fusion.14.branch, bf16[512,2048]{1,0:T(8,128)(2,1)} %merge.3, ...), custom_call_target="tpu_custom_call" | custom-call | flops 10000000000 | bytes 41943040 | tf_op jit(solution)/shard_map/pallas_call | solution.py:1246
  464.5 2.3 fusion.8
  466.8 0.4 fusion
  467.2 0.1 pad_maximum_fusion
  467.4 0.1 reshape.121.shared
  467.4 0.7 fusion.13
  468.3 1.6 copy-done.2
  469.8 161.9 %shard_map.208 = (bf16[4,8,16,2048]{3,2,1,0:T(8,128)(2,1)S(1)}, bf16[12,8,64,512]{3,2,1,0:T(8,128)(2,1)}, bf16[1,8,16,384]{3,2,1,0:T(8,128)(2,1)S(1)}) custom-call(bf16[512,2048]{1,0:T(8,128)(2,1)S(1)} %bitcast.42, bf16[3,512,512]{2,1,0:T(8,128)(2,1)S(1)} %copy-done.3, bf16[4,8,16,2048]{3,2,1,0:T(8,128)(2,1)} %bitcast.63, ...), custom_call_target="tpu_custom_call" | custom-call | flops 3221225472 | bytes 41943040 | tf_op jit(solution)/shard_map/pallas_call | solution.py:466
  631.8 15.3 %shard_map.209 = (f32[6144,512]{1,0:T(8,128)}, f32[512,2048]{1,0:T(8,128)}, f32[4,256,2048]{2,1,0:T(8,128)}, f32[512,2048]{1,0:T(8,128)}) custom-call(bf16[6144,512]{1,0:T(8,128)(2,1)} %bitcast.43, bf16[512,2048]{1,0:T(8,128)(2,1)S(1)} %bitcast.41, bf16[8,256,1024]{2,1,0:T(8,128)(2,1)S(1)} %copy-done.1, f32[512,2048]{1,0:T(8,128)S(1)} %copy-done), custom_call_target="tpu_custom_call" | custom-call | tf_op jit(solution)/shard_map/pallas_call | solution.py:916
  647.1 0.1 reshape.123
  647.2 0.7 slice.73
  647.8 0.6 slice.68
  648.5 0.1 slice.69
  648.6 0.6 slice_convert_fusion.2
  649.2 0.7 broadcast_multiply_fusion
  649.9 3.0 fusion.7
  (42 shorter events, 0.3 us)
Async XLA Ops:
  111.3 195.8 %copy-start.11 = (f32[2,64,128]{2,1,0:T(8,128)S(1)}, f32[2,64,128]{2,1,0:T(8,128)}, u32[]{:S(2)}) copy-start(f32[2,64,128]{2,1,0:T(8,128)} %get-tuple-element.42) | copy-start | bytes 196612
  305.8 1.5 copy-start.4
  305.8 1.6 copy-start.8
  305.8 1.8 copy-start.14
  305.8 1.8 copy-start.13
  307.1 1.6 copy-start.9
  308.6 1.2 copy-start.6
  309.8 157.0 %copy-start.12 = (bf16[2,64,2176]{2,1,0:T(8,128)(2,1)S(1)}, bf16[2,64,2176]{2,1,0:T(8,128)(2,1)}, u32[]{:S(2)}) copy-start(bf16[2,64,2176]{2,1,0:T(8,128)(2,1)} %get-tuple-element.39) | copy-start | bytes 1671172
  464.5 3.8 copy-start.3
  468.2 1.6 copy-start.2
  469.8 161.9 %copy-start = (f32[512,2048]{1,0:T(8,128)S(1)}, f32[512,2048]{1,0:T(8,128)}, u32[]{:S(2)}) copy-start(f32[512,2048]{1,0:T(8,128)} %get-tuple-element.62.shrink) | copy-start | bytes 12582916
  469.8 161.9 %copy-start.1 = (bf16[8,256,1024]{2,1,0:T(8,128)(2,1)S(1)}, bf16[8,256,1024]{2,1,0:T(8,128)(2,1)}, u32[]{:S(2)}) copy-start(bf16[8,256,1024]{2,1,0:T(8,128)(2,1)} %get-tuple-element.61.wide) | copy-start | bytes 12582916
  631.7 18.1 %copy-start.5 = (f32[2,64,2048]{2,1,0:T(8,128)S(1)}, f32[2,64,2048]{2,1,0:T(8,128)}, u32[]{:S(2)}) copy-start(f32[2,64,2048]{2,1,0:T(8,128)} %get-tuple-element.38) | copy-start | bytes 3145732
  631.8 18.1 %copy-start.7 = (f32[2,64,2048]{2,1,0:T(8,128)S(1)}, f32[2,64,2048]{2,1,0:T(8,128)}, u32[]{:S(2)}) copy-start(f32[2,64,2048]{2,1,0:T(8,128)} %copy-done.6) | copy-start | bytes 3145732
  631.8 18.1 %copy-start.10 = (bf16[2,64,2048]{2,1,0:T(8,128)(2,1)S(1)}, bf16[2,64,2048]{2,1,0:T(8,128)(2,1)}, u32[]{:S(2)}) copy-start(bf16[2,64,2048]{2,1,0:T(8,128)(2,1)} %param.25) | copy-start | bytes 1572868

commit v6 on v5

--- a/solution.py
+++ b/solution.py
@@ -56,7 +56,7 @@
     else:
         first = Line(xs, x_pos, (0, 2))
         second = Line(minor, minor_pos, (1, 0))
-    return Line(2, core, (0, 1)), first, second, Line(major, lax.div(g, minor), (minor, 0))
+    return Line(2, core, (0, 1)), first, Line(major, lax.div(g, minor), (minor, 0)), second
 
 
 def greet(some, whole=()):
@@ -121,13 +121,41 @@
     def sent(self):
         self._each(0, lambda leg: leg[2]().wait_send())
 
-
-def gather_hops(line, at, send, recv):
+    def finish(self):
+        self.arrive()
+        self.sent()
+
+
+def spread_hops(core, first, third, fourth, at, own, send, recv):
+    c, p, z, q = core.place, first.place, third.place, fourth.place
+    r4 = ROWS
+    r3 = r4 * fourth.size
+    r2 = r3 * third.size
+    rc = r2 * first.size
+    base = [0]
+
+    def sems(n):
+        b = base[0]
+        base[0] += n
+        return (lambda i: send(b + i)), (lambda i: recv(b + i))
+
+    def swap(line, place, first_source=None):
+        source = first_source or (lambda i: place(line.place))
+        return Swap(line, source, lambda j, i: place(i), *sems(line.size - 1))
+
+    hops = [swap(fourth, lambda i: at(c * rc + p * r2 + z * r3 + i * r4, r4), lambda i: own)]
+    hops += gather_hops(third, lambda i: at(c * rc + p * r2 + i * r3, r3), *sems(leg_count(third.size)))
+    hops.append(swap(first, lambda i: at(c * rc + i * r2, r2)))
+    hops.append(swap(core, lambda i: at(i * rc, rc)))
+    return hops
+
+
+def gather_hops(line, at, send, recv, own=None):
     n, a = line.size, line.place
     if n == 2:
         mine, theirs, peer = at(a), at(1 - a), line.at(1 - 2 * a)
         return [
-            Hop([(None, None, lambda: remote(mine, mine, send(0), recv(0), peer),
+            Hop([(None, None, lambda: remote(mine if own is None else own, mine, send(0), recv(0), peer),
                   lambda: remote(theirs, theirs, send(0), recv(0), peer), None)])
         ]
     hops = []
@@ -142,7 +170,8 @@
             out, into = jnp.clip(out, 0, n - 1), jnp.clip(into, 0, n - 1)
             legs.append((
                 sends, gets,
-                lambda out=out, way=way, k=k: remote(at(out), at(out), send(k), recv(k), line.at(way)),
+                lambda out=out, way=way, k=k, s=s: remote(
+                    own if s == 1 and own is not None else at(out), at(out), send(k), recv(k), line.at(way)),
                 lambda into=into, way=way, k=k: remote(at(into), at(into), send(k), recv(k), line.at(-way)),
                 None,
             ))
@@ -260,7 +289,7 @@
     chunks = x.shape[0]
     return pl.pallas_call(
         functools.partial(gather_kernel, groups, parts),
-        out_shape=jax.ShapeDtypeStruct((chunks, 2, xs, minor, major, ROWS, width), x.dtype),
+        out_shape=jax.ShapeDtypeStruct((chunks, 2, xs, major, minor, ROWS, width), x.dtype),
         in_specs=[pl.BlockSpec(memory_space=pl.ANY)],
         out_specs=pl.BlockSpec(memory_space=pl.ANY),
         scratch_shapes=[
@@ -317,7 +346,7 @@
     legs = sum(leg_count(n) for n in (2, xs, minor, major))
     chunks, width = part.shape[0], part.shape[-1]
     unit = 2 * ROWS * width
-    need = unit * (2 * xs * minor * major + leg_count(xs) * minor * major + leg_count(minor) * major + leg_count(major) + 2)
+    need = unit * (2 * xs * minor * major + leg_count(xs) * minor * major + leg_count(major) * minor + leg_count(minor) + 2)
     per = chunks
     while per > 1 and per * need > 44 * 2**20:
         per //= 2
@@ -327,11 +356,11 @@
         in_specs=[pl.BlockSpec(memory_space=pl.ANY)],
         out_specs=pl.BlockSpec(memory_space=pltpu.VMEM),
         scratch_shapes=[
-            pltpu.VMEM((per, xs, minor, major, ROWS, width), BF),
-            pltpu.VMEM((per, xs, minor, major, ROWS, width), BF),
-            pltpu.VMEM((per, leg_count(xs), minor, major, ROWS, width), BF),
-            pltpu.VMEM((per, leg_count(minor), major, ROWS, width), BF),
-            pltpu.VMEM((per, leg_count(major), ROWS, width), BF),
+            pltpu.VMEM((per, xs, major, minor, ROWS, width), BF),
+            pltpu.VMEM((per, xs, major, minor, ROWS, width), BF),
+            pltpu.VMEM((per, leg_count(xs), major, minor, ROWS, width), BF),
+            pltpu.VMEM((per, leg_count(major), minor, ROWS, width), BF),
+            pltpu.VMEM((per, leg_count(minor), ROWS, width), BF),
             pltpu.SemaphoreType.DMA((per,)),
             pltpu.SemaphoreType.DMA((per, legs)),
             pltpu.SemaphoreType.DMA((per, legs)),
@@ -428,15 +457,13 @@
         first_land = leg_count(one.size) * n
         down = reduce_hops(one, level_one(acc[j], k), lambda i, j=j, k=k, n=n: land[j].at[k, pl.ds(i * n, n)], add, *sems(one.size))
         down += reduce_hops(two, level_two(acc[j], k), lambda i, j=j, k=k, f=first_land: land[j].at[k, f + i], add, *sems(two.size))
-        up = gather_hops(two, level_two(outs[j], k), *sems(two.size))
+        up = gather_hops(two, level_two(outs[j], k), *sems(two.size), own=acc[j].at[k, y * n + z])
+        turn = len(up)
         up += gather_hops(one, level_one(outs[j], k), *sems(one.size))
 
-        def put(store=store):
-            store.start()
-            store.wait()
-
         down[0] = Begun(down[0], before.get((j, k)) or (weights(k) if j == 1 else lambda: None))
-        up[0] = Begun(up[0], put)
+        up[0] = Begun(up[0], store.start)
+        up[turn] = Begun(up[turn], store.wait)
         chains.append(down + up)
     greet([short, long], [whole])
     load[3].wait()
@@ -512,25 +539,15 @@
         out().wait_send()
 
 
-def add_and_send(acc, first, land, rows, line, send):
-    def add(place, count):
-        @pl.loop(0, count * rows // line.size // ROWS)
-        def _(i):
-            offset = place * (rows // line.size) + i * ROWS
-            here = pl.ds(pl.multiple_of(first + offset, ROWS), ROWS)
-            there = pl.ds(pl.multiple_of(offset, ROWS), ROWS)
-            total = acc[here, :].astype(F32)
-            for j in range(land.shape[0]):
-                total = total + land[j, there, :].astype(F32)
-            acc[here, :] = total.astype(acc.dtype)
-
-    if line.size == 2:
-        add(1 - line.place, 1)
-        send()
-        add(line.place, 1)
-    else:
-        add(0, line.size)
-        send()
+class Swap:
+    def __init__(self, *how):
+        self.legs = swap_legs(*how)
+
+    def start(self):
+        start_legs(self.legs)
+
+    def finish(self):
+        end_legs(self.legs)
 
 
 def add_rows(acc, first, land, rows):
@@ -542,22 +559,23 @@
 
 
 def experts_kernel(
-    groups, parts, local_rows, ring, acc_ring, experts,
+    groups, parts, local_rows, acc_ring, experts,
     x, dy, widen, shrink,
     summed, moe, grad_widen, grad_shrink,
     xs, dys, wide, down, sum_wide, sum_down, stage, acc, other, land_c, land_p, land_q, land_z,
     hid, raw, gated, d_gu, gate, product, marks,
     load, dy_sem, stage_sem, g_send, g_recv, s_send, s_recv,
 ):
-    core, first, second, long = lines(groups, parts)
-    c, p, q, z = core.place, first.place, second.place, long.place
-    pn, qn, zn = first.size, second.size, long.size
+    core, first, third, fourth = lines(groups, parts)
+    c, p, z, q = core.place, first.place, third.place, fourth.place
+    pn, zn, qn = first.size, third.size, fourth.size
     chunks, width = x.shape[0], shrink.shape[2]
     local_exp, inner = shrink.shape[0], shrink.shape[1]
     share = inner // groups
     group, part = lax.axis_index("grp"), lax.axis_index("ep")
-    rz, rq, rp, rc = ROWS, ROWS * zn, ROWS * zn * qn, ROWS * zn * qn * pn
+    rq, rz, rp, rc = ROWS, ROWS * qn, ROWS * qn * zn, ROWS * qn * zn * pn
     rows = 2 * rc
+    levels = 3 + hop_count(zn)
     cuts = local_rows // ROWS
     base = part * local_exp
     pairs = local_exp // 2
@@ -580,51 +598,51 @@
 
     dy_start = lambda k: dy_copy(k).start()
     dy_start(0)
-    greet_lines([core, first, second, long])
+    greet_lines([core, first, third, fourth])
 
     def rows_at(start, size):
         return pl.ds(pl.multiple_of(start, ROWS), size)
 
-    def g_long(k):
-        buf = xs.at[lax.rem(k, ring)]
-        return swap_legs(
-            long, lambda i: x.at[k], lambda j, i: buf.at[rows_at(c * rc + p * rp + q * rq + i * rz, rz), :],
-            lambda j: g_send.at[k, j], lambda j: g_recv.at[k, j])
-
-    def g_line(k, line, at, offset):
-        return swap_legs(line, lambda i: at(line.place), lambda j, i: at(i),
-                         lambda j: g_send.at[k, offset + j], lambda j: g_recv.at[k, offset + j])
-
-    def g_second(k):
-        buf = xs.at[lax.rem(k, ring)]
-        return g_line(k, second, lambda i: buf.at[rows_at(c * rc + p * rp + i * rq, rq), :], zn - 1)
-
-    def g_first(k):
-        buf = xs.at[lax.rem(k, ring)]
-        return g_line(k, first, lambda i: buf.at[rows_at(c * rc + i * rp, rp), :], zn + qn - 2)
-
-    def g_core(k):
-        buf = xs.at[lax.rem(k, ring)]
-        return g_line(k, core, lambda i: buf.at[rows_at(i * rc, rc), :], zn + qn + pn - 3)
+    def g_hop(k, level):
+        buf = xs.at[k]
+        return spread_hops(core, first, third, fourth, lambda start, size: buf.at[rows_at(start, size), :], x.at[k],
+                           lambda i: g_send.at[k, i], lambda i: g_recv.at[k, i])[level]
 
     def s_line(k, line, at, land, offset):
-        return swap_legs(line, at, lambda j, i: land.at[lax.rem(k, 2), j],
-                         lambda j: s_send.at[k, offset + j], lambda j: s_recv.at[k, offset + j])
-
-    def s_core(k):
-        return s_line(k, core, lambda i: other, land_c, 0)
-
-    def s_first(k):
-        buf = acc.at[lax.rem(k, acc_ring)]
-        return s_line(k, first, lambda i: buf.at[rows_at(i * rp, rp), :], land_p, 1)
-
-    def s_second(k):
-        buf = acc.at[lax.rem(k, acc_ring)]
-        return s_line(k, second, lambda i: buf.at[rows_at(p * rp + i * rq, rq), :], land_q, pn)
-
-    def s_long(k):
-        buf = acc.at[lax.rem(k, acc_ring)]
-        return s_line(k, long, lambda i: buf.at[rows_at(p * rp + q * rq + i * rz, rz), :], land_z, pn + qn - 1)
+        return Swap(line, at, lambda j, i: land.at[lax.rem(k, 2), j],
+                    lambda j: s_send.at[k, offset + j], lambda j: s_recv.at[k, offset + j])
+
+    def mine(k):
+        return acc.at[lax.rem(k, acc_ring)]
+
+    def s_hop(k, level):
+        if level == 0:
+            return s_line(k, core, lambda i: other, land_c, 0)
+        if level == 1:
+            return s_line(k, first, lambda i: mine(k).at[i], land_p, 1)
+        if level == 2:
+            return s_line(k, fourth, lambda i: mine(k).at[p, :, i], land_q, pn)
+        return s_line(k, third, lambda i: mine(k).at[p, i, q], land_z, pn + qn - 1)
+
+    def s_end(k, level):
+        s_hop(k, level).finish()
+        slot = lax.rem(k, 2)
+        if level == 3:
+            total = mine(k)[p, z, q].astype(F32)
+            for j in range(zn - 1):
+                total = total + land_z[slot, j].astype(F32)
+            summed[k] = total.astype(BF)
+            return
+        if level == 0 and pn == 2:
+            add(mine(k).at[1 - p], land_c.at[slot, 0, 1 - p])
+            s_hop(k, 1).start()
+            add(mine(k).at[p], land_c.at[slot, 0, p])
+            return
+        to = (mine(k), mine(k).at[p], mine(k).at[p, :, q])[level]
+        land = (land_c, land_p, land_q)[level]
+        for j in range(land.shape[1]):
+            add(to, land.at[slot, j])
+        s_hop(k, level + 1).start()
 
     def after(t, lag, act):
         k = t - lag
@@ -636,7 +654,7 @@
     tiles = width // 512
 
     def compute(k):
-        buf, dyk = xs.at[lax.rem(k, ring)], dys.at[lax.rem(k, 2)]
+        buf, dyk = xs.at[k], dys.at[lax.rem(k, 2)]
 
         @pl.when(k == 0)
         def _():
@@ -673,18 +691,20 @@
                 d_gu[here, to_gate] = (d * u * (sigma + swish * (1.0 - sigma))).astype(BF)
                 d_gu[here, to_up] = (d * swish).astype(BF)
 
-        mine = acc.at[lax.rem(k, acc_ring)]
+        kept = mine(k)
 
         def split(cols, total):
+            total = total.astype(BF).reshape((2,) + other.shape[:-1] + total.shape[1:])
+
             @pl.when(c == 0)
             def _():
-                mine[:, cols] = total[:rc].astype(BF)
-                other[:, cols] = total[rc:].astype(BF)
+                kept[..., cols] = total[0]
+                other[..., cols] = total[1]
 
             @pl.when(c == 1)
             def _():
-                other[:, cols] = total[:rc].astype(BF)
-                mine[:, cols] = total[rc:].astype(BF)
+                other[..., cols] = total[0]
+                kept[..., cols] = total[1]
 
         @pl.loop(0, tiles)
         def _(n):
@@ -694,47 +714,26 @@
 
         split(pl.ds(width, 128), lax.dot_general(
             product[...], marks[...], (((1,), (1,)), ((), ())), preferred_element_type=F32))
-        start_legs(s_core(k))
-        slot = lax.rem(k, 2)
-
-        @pl.when(k >= 2)
+        s_hop(k, 0).start()
+
+        @pl.when(k >= 1)
         def _():
-            pltpu.make_async_copy(stage.at[slot], moe.at[k - 2], stage_sem.at[slot]).wait()
+            pltpu.make_async_copy(stage, moe.at[k - 1], stage_sem.at[0]).wait()
 
         @pl.loop(0, tiles)
         def _(n):
             cols = pl.ds(pl.multiple_of(n * 512, 512), 512)
-            stage[slot, :, cols] = jnp.dot(gated[...], down[:, cols], preferred_element_type=F32).astype(BF)
+            stage[:, cols] = jnp.dot(gated[...], down[:, cols], preferred_element_type=F32).astype(BF)
             sum_wide[cols, :] += lax.dot_general(
                 buf[:, cols], d_gu[...], (((0,), (0,)), ((), ())), preferred_element_type=F32)
             sum_down[:, cols] += lax.dot_general(
                 gated[...], dyk[:, cols], (((0,), (0,)), ((), ())), preferred_element_type=F32)
 
-        pltpu.make_async_copy(stage.at[slot], moe.at[k], stage_sem.at[slot]).start()
-
-    def end_long(k):
-        end_legs(s_long(k))
-        buf = acc.at[lax.rem(k, acc_ring)]
-        total = buf[rows_at(p * rp + q * rq + z * rz, rz), :].astype(F32)
-        for j in range(zn - 1):
-            total = total + land_z[lax.rem(k, 2), j].astype(F32)
-        summed[k] = total.astype(BF)
-
-    def end_second(k):
-        end_legs(s_second(k))
-        add_and_send(acc.at[lax.rem(k, acc_ring)], p * rp + q * rq, land_q.at[lax.rem(k, 2)], rq, long, lambda: start_legs(s_long(k)))
-
-    def end_first(k):
-        end_legs(s_first(k))
-        add_and_send(acc.at[lax.rem(k, acc_ring)], p * rp, land_p.at[lax.rem(k, 2)], rp, second, lambda: start_legs(s_second(k)))
-
-    def end_core(k):
-        end_legs(s_core(k))
-        add_and_send(acc.at[lax.rem(k, acc_ring)], 0, land_c.at[lax.rem(k, 2)], rc, first, lambda: start_legs(s_first(k)))
+        pltpu.make_async_copy(stage, moe.at[k], stage_sem.at[0]).start()
 
     def begin(k):
-        xs[lax.rem(k, ring), rows_at(c * rc + p * rp + q * rq + z * rz, rz), :] = x[k]
-        start_legs(g_long(k))
+        xs[k, rows_at(c * rc + p * rp + z * rz + q * rq, rq), :] = x[k]
+        g_hop(k, 0).start()
 
         @pl.when(k == 0)
         def _():
@@ -744,12 +743,10 @@
             owner = base + lax.div(lax.broadcasted_iota(jnp.int32, marks.shape, 1), share)
             marks[...] = jnp.where((lanes == owner) | (lanes == owner + experts), 1.0, 0.0).astype(BF)
 
-    def then(one, two):
-        def act(k):
-            end_legs(one(k))
-            start_legs(two(k))
-
-        return act
+    def g_end(k, level):
+        g_hop(k, level).finish()
+        if level + 1 < levels:
+            g_hop(k, level + 1).start()
 
     def wide_out(i):
         here = pl.ds(pl.multiple_of(i * rows, rows), rows)
@@ -769,27 +766,22 @@
         d_gu[...] = sum_wide[pl.ds(pl.multiple_of(i * rows, rows), rows), :].astype(BF)
         wide_out(i).start()
 
-    @pl.loop(0, chunks + 8)
+    @pl.loop(0, chunks + levels + 4)
     def _(t):
-        after(t, 4, lambda k: end_legs(g_core(k)))
-        after(t, 3, then(g_first, g_core))
-        after(t, 2, then(g_second, g_first))
-        after(t, 1, then(g_long, g_second))
+        for level in reversed(range(levels)):
+            after(t, level + 1, functools.partial(g_end, level=level))
         after(t, 0, begin)
-        after(t, 8, end_long)
-        after(t, 7, end_second)
-        after(t, 6, end_first)
-        after(t, 5, end_core)
-        after(t, 4, compute)
-
-        @pl.when((t >= chunks + 4) & (t < chunks + 4 + width // rows))
+        for level in reversed(range(4)):
+            after(t, levels + level + 1, functools.partial(s_end, level=level))
+        after(t, levels, compute)
+
+        @pl.when((t >= chunks + levels) & (t < chunks + levels + min(4, width // rows)))
         def _():
-            store(t - chunks - 4)
+            store(t - chunks - levels)
 
     for i in range(4, width // rows):
         store(i)
-    for k in range(chunks - 2, chunks):
-        pltpu.make_async_copy(stage.at[k % 2], moe.at[k], stage_sem.at[k % 2]).wait()
+    pltpu.make_async_copy(stage, moe.at[chunks - 1], stage_sem.at[0]).wait()
     wide_out(width // rows - 1).wait()
     out_down.wait()
 
@@ -803,15 +795,14 @@
     local_exp, inner, width = shrink.shape
     share = inner // groups
     hidden = local_exp * share
-    half = ROWS * major * minor * xn
-    rows = 2 * half
-    ring, acc_ring = min(chunks, 6), 4
-    legs = major + minor + xn - 2
+    rows = 2 * ROWS * major * minor * xn
+    acc_ring = 4
+    legs = minor + xn - 1 + leg_count(major)
     vmem = pl.BlockSpec(memory_space=pltpu.VMEM)
     hbm = pl.BlockSpec(memory_space=pl.ANY)
     flops = 2 * chunks * rows * width * hidden * 9
     return pl.pallas_call(
-        functools.partial(experts_kernel, groups, parts, local_rows, ring, acc_ring, experts),
+        functools.partial(experts_kernel, groups, parts, local_rows, acc_ring, experts),
         out_shape=[
             jax.ShapeDtypeStruct((chunks, ROWS, wide), BF),
             jax.ShapeDtypeStruct((chunks, rows, width), BF),
@@ -821,18 +812,18 @@
         in_specs=[vmem, hbm, hbm, hbm],
         out_specs=[vmem, hbm, hbm, hbm],
         scratch_shapes=[
-            pltpu.VMEM((ring, rows, wide), BF),
+            pltpu.VMEM((chunks, rows, wide), BF),
             pltpu.VMEM((2, rows, width), BF),
             pltpu.VMEM((width, 2 * hidden), BF),
             pltpu.VMEM((hidden, width), BF),
             pltpu.VMEM((width, 2 * hidden), F32),
             pltpu.VMEM((hidden, width), F32),
-            pltpu.VMEM((2, rows, width), BF),
-            pltpu.VMEM((acc_ring, half, wide), BF),
-            pltpu.VMEM((half, wide), BF),
-            pltpu.VMEM((2, 1, half, wide), BF),
-            pltpu.VMEM((2, xn - 1, half // xn, wide), BF),
-            pltpu.VMEM((2, minor - 1, half // xn // minor, wide), BF),
+            pltpu.VMEM((rows, width), BF),
+            pltpu.VMEM((acc_ring, xn, major, minor, ROWS, wide), BF),
+            pltpu.VMEM((xn, major, minor, ROWS, wide), BF),
+            pltpu.VMEM((2, 1, xn, major, minor, ROWS, wide), BF),
+            pltpu.VMEM((2, xn - 1, major, minor, ROWS, wide), BF),
+            pltpu.VMEM((2, minor - 1, major, ROWS, wide), BF),
             pltpu.VMEM((2, major - 1, ROWS, wide), BF),
             pltpu.VMEM((rows, 4 * share), F32),
             pltpu.VMEM((rows, 2 * share), F32),
@@ -850,7 +841,7 @@
             pltpu.SemaphoreType.DMA((chunks, legs)),
         ],
         compiler_params=pltpu.CompilerParams(
-            collective_id=collective_id, has_side_effects=True, vmem_limit_bytes=60 * 2**20
+            collective_id=collective_id, has_side_effects=True, vmem_limit_bytes=63 * 2**20
         ),
         cost_estimate=pl.CostEstimate(flops=flops, bytes_accessed=80 * 2**20, transcendentals=chunks * rows * hidden),
     )(x, dy, widen, shrink)
@@ -929,25 +920,23 @@
     PACE = 2
 
     def __init__(self, groups, parts, part, out, acc, land_c, land_p, land_q, land_z, local, send, recv):
-        self.core, self.first, self.second, self.long = lines(groups, parts)
-        self.part, self.out, self.acc, self.lands = part, out, acc, (land_c, land_p, land_q, land_z)
+        self.core, self.first, self.third, self.fourth = lines(groups, parts)
+        self.part, self.out, self.acc, self.lands = part, out, acc, (land_c, land_p, land_q)
+        self.land_z = land_z
         self.local, self.send, self.recv = local, send, recv
         self.chunks = part.shape[0]
-        pn, qn, zn = self.first.size, self.second.size, self.long.size
-        self.rz, self.rq, self.rp, self.rc = ROWS, ROWS * zn, ROWS * zn * qn, ROWS * zn * qn * pn
-        self.levels = 3 + hop_count(zn)
+        self.levels = 3 + hop_count(self.third.size)
         self.lag = self.PACE * self.levels
 
     @staticmethod
     def scratch(chunks, width):
         major, minor, xn = mesh_sizes(lax.axis_size("grp"), lax.axis_size("ep"))
-        half = ROWS * major * minor * xn
         legs = minor + xn - 1 + leg_count(major)
         return [
-            pltpu.VMEM((min(chunks, 12), half, width), BF),
-            pltpu.VMEM((4, 1, half, width), BF),
-            pltpu.VMEM((4, xn - 1, half // xn, width), BF),
-            pltpu.VMEM((4, minor - 1, half // xn // minor, width), BF),
+            pltpu.VMEM((chunks, xn, major, minor, ROWS, width), BF),
+            pltpu.VMEM((4, 1, xn, major, minor, ROWS, width), BF),
+            pltpu.VMEM((4, xn - 1, major, minor, ROWS, width), BF),
+            pltpu.VMEM((4, minor - 1, major, ROWS, width), BF),
             pltpu.VMEM((chunks, leg_count(major), ROWS, width), BF),
             pltpu.SemaphoreType.DMA((chunks,)),
             pltpu.SemaphoreType.DMA((chunks, legs)),
@@ -955,60 +944,51 @@
         ]
 
     def near(self):
-        return [self.core, self.first, self.second, self.long]
-
-    def buf(self, k):
-        return self.acc.at[lax.rem(k, self.acc.shape[0])]
+        return [self.core, self.first, self.third, self.fourth]
 
     def own(self, k):
-        here = pl.ds(pl.multiple_of(self.core.place * self.rc, self.rc), self.rc)
-        return pltpu.make_async_copy(self.part.at[k, here, :], self.buf(k), self.local.at[k])
+        return pltpu.make_async_copy(self.part.at[k, self.core.place], self.acc.at[k], self.local.at[k])
 
     def hop(self, k, level):
-        c, p, q, z = self.core.place, self.first.place, self.second.place, self.long.place
-        pn, qn = self.first.size, self.second.size
-        at = lambda start, size: pl.ds(pl.multiple_of(start, ROWS), size)
+        p, q = self.first.place, self.fourth.place
+        pn, qn = self.first.size, self.fourth.size
+        if level >= 3:
+            offset = pn + qn - 1
+            land = self.land_z.at[k]
+            return reduce_hops(self.third, lambda i: self.acc.at[k, p, i, q], lambda i: land.at[i], add,
+                               lambda i: self.send.at[k, offset + i], lambda i: self.recv.at[k, offset + i])[level - 3]
         line, offset, source = [
-            (self.core, 0, lambda i: self.part.at[k, at(i * self.rc, self.rc), :]),
-            (self.first, 1, lambda i: self.buf(k).at[at(i * self.rp, self.rp), :]),
-            (self.second, pn, lambda i: self.buf(k).at[at(p * self.rp + i * self.rq, self.rq), :]),
+            (self.core, 0, lambda i: self.part.at[k, i]),
+            (self.first, 1, lambda i: self.acc.at[k, i]),
+            (self.fourth, pn, lambda i: self.acc.at[k, p, :, i]),
         ][level]
         land = self.lands[level]
-        return swap_legs(line, source, lambda j, i: land.at[lax.rem(k, 4), j],
-                         lambda j: self.send.at[k, offset + j], lambda j: self.recv.at[k, offset + j])
-
-    def long_hop(self, k, number):
-        base = self.first.place * self.rp + self.second.place * self.rq
-        offset = self.first.size + self.second.size - 1
-        at = lambda i: self.buf(k).at[pl.ds(pl.multiple_of(base + i * self.rz, ROWS), self.rz), :]
-        land = self.lands[3].at[k]
-        return reduce_hops(self.long, at, lambda i: land.at[i], add,
-                           lambda i: self.send.at[k, offset + i], lambda i: self.recv.at[k, offset + i])[number]
+        return Swap(line, source, lambda j, i: land.at[lax.rem(k, 4), j],
+                    lambda j: self.send.at[k, offset + j], lambda j: self.recv.at[k, offset + j])
 
     def end(self, k, level):
-        p, q, z = self.first.place, self.second.place, self.long.place
-        if level >= 3:
-            hop = self.long_hop(k, level - 3)
-            hop.arrive()
-            hop.sent()
-            if level + 1 < self.levels:
-                self.long_hop(k, level - 2).start()
-            else:
-                here = pl.ds(pl.multiple_of(p * self.rp + q * self.rq + z * self.rz, ROWS), ROWS)
-                self.out[k] = self.buf(k)[here, :]
+        p, q, z = self.first.place, self.fourth.place, self.third.place
+        self.hop(k, level).finish()
+        if level + 1 == self.levels:
+            self.out[k] = self.acc[k, p, z, q]
             return
-        end_legs(self.hop(k, level))
+        after = self.hop(k, level + 1)
         if level == 0:
             self.own(k).wait()
-        first = [0, p * self.rp, p * self.rp + q * self.rq][level]
-        size = [self.rc, self.rp, self.rq][level]
-        land = self.lands[level]
-        line = (self.first, self.second, self.long)[level]
-        then = (lambda: start_legs(self.hop(k, level + 1))) if level < 2 else self.long_hop(k, 0).start
-        add_and_send(self.buf(k), first, land.at[lax.rem(k, 4)], size, line, then)
+            if self.first.size == 2:
+                add(self.acc.at[k, 1 - p], self.lands[0].at[lax.rem(k, 4), 0, 1 - p])
+                after.start()
+                add(self.acc.at[k, p], self.lands[0].at[lax.rem(k, 4), 0, p])
+                return
+            add(self.acc.at[k], self.lands[0].at[lax.rem(k, 4), 0])
+        elif level < 3:
+            to = self.acc.at[k, p] if level == 1 else self.acc.at[k, p, :, q]
+            for j in range(self.lands[level].shape[1]):
+                add(to, self.lands[level].at[lax.rem(k, 4), j])
+        after.start()
 
     def begin(self, k):
-        start_legs(self.hop(k, 0))
+        self.hop(k, 0).start()
         self.own(k).start()
 
     def step(self, t):
@@ -1294,19 +1274,18 @@
 
 class BackGather:
     PACE = 3
-    LAG = 4 * PACE
 
     def __init__(self, groups, parts, own, out, local, send, recv):
-        self.core, self.first, self.second, self.long = lines(groups, parts)
+        self.lines = lines(groups, parts)
         self.own, self.out, self.local, self.send, self.recv = own, out, local, send, recv
         self.chunks = own.shape[0]
-        pn, qn, zn = self.first.size, self.second.size, self.long.size
-        self.rz, self.rq, self.rp, self.rc = ROWS, ROWS * zn, ROWS * zn * qn, ROWS * zn * qn * pn
+        self.levels = 4
+        self.lag = self.PACE * self.levels
 
     @staticmethod
     def scratch(chunks):
         major, minor, xn = mesh_sizes(lax.axis_size("grp"), lax.axis_size("ep"))
-        legs = major + minor + xn - 2
+        legs = minor + xn + major - 2
         return [
             pltpu.SemaphoreType.DMA((chunks,)),
             pltpu.SemaphoreType.DMA((chunks, legs)),
@@ -1314,45 +1293,41 @@
         ]
 
     def near(self):
-        return [self.core, self.first, self.second, self.long]
-
-    def rows(self, k, start, size):
-        return self.out.at[k, pl.ds(pl.multiple_of(start, ROWS), size), :]
+        return list(self.lines)
 
     def mine(self, k):
-        c, p, q, z = self.core.place, self.first.place, self.second.place, self.long.place
         return pltpu.make_async_copy(
-            self.own.at[k], self.rows(k, c * self.rc + p * self.rp + q * self.rq + z * self.rz, self.rz), self.local.at[k])
+            self.own.at[k], self.out.at[(k,) + tuple(line.place for line in self.lines)], self.local.at[k])
 
     def hop(self, k, level):
-        c, p, q, z = self.core.place, self.first.place, self.second.place, self.long.place
-        pn, qn, zn = self.first.size, self.second.size, self.long.size
+        core, first, third, fourth = self.lines
+        c, p, q = core.place, first.place, fourth.place
         line, offset, at = [
-            (self.long, 0, lambda i: self.rows(k, c * self.rc + p * self.rp + q * self.rq + i * self.rz, self.rz)),
-            (self.second, zn - 1, lambda i: self.rows(k, c * self.rc + p * self.rp + i * self.rq, self.rq)),
-            (self.first, zn + qn - 2, lambda i: self.rows(k, c * self.rc + i * self.rp, self.rp)),
-            (self.core, zn + qn + pn - 3, lambda i: self.rows(k, i * self.rc, self.rc)),
+            (third, 0, lambda i: self.out.at[k, c, p, i, q]),
+            (fourth, third.size - 1, lambda i: self.out.at[k, c, p, :, i]),
+            (first, third.size + fourth.size - 2, lambda i: self.out.at[k, c, i]),
+            (core, third.size + fourth.size + first.size - 3, lambda i: self.out.at[k, i]),
         ][level]
         source = (lambda i: self.own.at[k]) if level == 0 else (lambda i: at(line.place))
-        return swap_legs(line, source, lambda j, i: at(i),
-                         lambda j: self.send.at[k, offset + j], lambda j: self.recv.at[k, offset + j])
+        return Swap(line, source, lambda j, i: at(i),
+                    lambda j: self.send.at[k, offset + j], lambda j: self.recv.at[k, offset + j])
 
     def step(self, t):
-        for level in (3, 2, 1, 0):
+        for level in reversed(range(self.levels)):
             k = t - self.PACE * (level + 1)
 
             @pl.when((k >= 0) & (k < self.chunks))
             def _(k=k, level=level):
-                end_legs(self.hop(k, level))
+                self.hop(k, level).finish()
                 if level == 0:
                     self.mine(k).wait()
-                if level < 3:
-                    start_legs(self.hop(k, level + 1))
+                if level + 1 < self.levels:
+                    self.hop(k, level + 1).start()
 
         @pl.when((t >= 0) & (t < self.chunks))
         def _():
             self.mine(t).start()
-            start_legs(self.hop(t, 0))
+            self.hop(t, 0).start()
 
 
 def forward_kernel(
@@ -1373,7 +1348,7 @@
     for copy in loads:
         copy.start()
     back = BackGather(groups, parts, dy, dy_all, *behind)
-    step, steps = back.step, back.chunks + back.LAG
+    step, steps = back.step, back.chunks + back.lag
     gains[...] = gains_in[...].astype(F32)
     head_gains[...] = head_gains_in[...].astype(F32)
     lane = lax.broadcasted_iota(jnp.int32, (1, 128), 1)
@@ -1495,7 +1470,6 @@
     heads = local_width // HD
     tokens = micro * length
     chunks = micro * block // ROWS
-    rows = 2 * xn * minor * major * ROWS
     vmem = pl.BlockSpec(memory_space=pltpu.VMEM)
     hbm = pl.BlockSpec(memory_space=pl.ANY)
     low = jax.ShapeDtypeStruct((micro, length, local_width), BF)
@@ -1511,7 +1485,7 @@
             jax.ShapeDtypeStruct((micro, block, width), F32),
             jax.ShapeDtypeStruct((micro, block, width + 128), BF),
             jax.ShapeDtypeStruct((micro, block, 128), F32),
-            jax.ShapeDtypeStruct((chunks, rows, width), BF),
+            jax.ShapeDtypeStruct((chunks, 2, xn, major, minor, ROWS, width), BF),
         ],
         in_specs=[vmem] * 10 + [hbm] * 2,
         out_specs=[vmem] * 11 + [hbm],
@@ -1582,10 +1556,10 @@
     ffn_in = ffn_ext[..., :width]
 
     fused = xs == minor and share % 128 == 0 and local_exp % 2 == 0 and 2 * xs * minor * major * ROWS <= 512
-    chunk_shape = (micro * local_rows // ROWS, 2, xs, minor, major, ROWS)
+    chunk_shape = (micro * local_rows // ROWS, 2, xs, major, minor, ROWS)
     if fused:
         dx_sum, moe_part, grad_widen, grad_shrink = experts_together(
-            ffn_ext, dy_all, specialist_widen_matrix, specialist_shrink_matrix, experts, 1)
+            ffn_ext, dy_all.reshape(dy_all.shape[0], -1, width), specialist_widen_matrix, specialist_shrink_matrix, experts, 1)
     else:
         dx_sum, moe_part, grad_widen, grad_shrink = experts_apart(
             ffn_ext, dy_all, specialist_widen_matrix, specialist_shrink_matrix, experts)
@@ -1607,7 +1581,7 @@
     d_proj, d_attn_in, grad_heads, grad_out, grad_widen, moe = attention_back(
         d_hidden.astype(BF), heads_merge_matrix, triple, queries, keys, values, mixed, weights,
         qk_hat, qk_inv, probe_lookup_scalers, cos, signed_sin, grad_widen,
-        moe_part if fused else None, 5)
+        moe_part.reshape(chunk_shape + (width,)) if fused else None, 5)
     if not fused:
         moe = scatter_all(moe_part.reshape(chunk_shape + (width,)), 3)
     output = (hidden + moe.astype(F32).reshape(micro, local_rows, width)).astype(BF)

time: 655 us -> 651 us (level)
  no operation moved by 1% of the time
where the time goes in v6:
time: 651 us; the launch traced here: 650 us
  Pallas kernels  634 us (97%)
  other arithmetic  9.55 us (1%)
    pallas_call x1, Pallas kernels, experts_together(): pl.pallas_call(functools.partial(experts_kernel, groups, parts, local_row...  193 us
    pallas_call x1, Pallas kernels, total_over_groups(): pl.pallas_call(functools.partial(total_kernel, groups, parts, plan), out_...  161 us
    pallas_call x1, Pallas kernels, attention_back(): pl.pallas_call(functools.partial(back_kernel, groups, parts, backed), out...  154 us
    pallas_call x1, Pallas kernels, attention_forward(): pl.pallas_call(functools.partial(forward_kernel, groups, parts, experts),...  111 us
    pallas_call x1, Pallas kernels, finish(): pl.pallas_call(functools.partial(finish_kernel, share), grid=(steps, 2),...  15.3 us

profile of v6, /device:TPU:0, one launch (start us, length us, event | category | flops | bytes accessed | tf_op | source)
XLA Modules:
  0.0 650.3 jit_solution(2413111500986828034)
XLA Ops:
  0.6 110.6 %shard_map.205 = (bf16[2,256,2048]{2,1,0:T(8,128)(2,1)}, bf16[2,256,512]{2,1,0:T(8,128)(2,1)}, bf16[2,256,512]{2,1,0:T(8,128)(2,1)}, bf16[2,256,512]{2,1,0:T(8,1...) custom-call(bf16[2,64,2048]{2,1,0:T(8,128)(2,1)} %x.5, ...), custom_call_target="tpu_custom_call" | custom-call | flops 6000000000 | bytes 41943040 | tf_op jit(solution)/shard_map/pallas_call | solution.py:1477
  111.3 192.9 %shard_map.206 = (bf16[8,16,2176]{2,1,0:T(8,128)(2,1)}, bf16[8,512,2048]{2,1,0:T(8,128)(2,1)}, bf16[2048,1024]{1,0:T(8,128)(2,1)}, f32[512,2048]{1,0:T(8,128)}) custom-call(bf16[8,16,2176]{2,1,0:T(8,128)(2,1)} %bitcast.49, bf16[8,512,2048]{2,1,0:T(8,128)(2,1)} %bitcast.65, bf16[4,2048,2048]{2,1,0:T(8,128)(2,1)} %widen.1, bf16[4,1024,2048]{2,1,0:T(8,128)(2,1)} %shrink.1), custom_call_target="tpu_custom_call" | custom-call | flops 77309411328 | bytes 83886080 | tf_op jit(solution)/shard_map/pallas_call | solution.py:804
  304.2 1.2 bitcast_convert_fusion
  305.5 0.2 multiply_reduce_fusion.3
  305.6 0.2 multiply_reduce_fusion.2
  305.8 0.2 fusion.9
  306.0 0.9 multiply_reduce_fusion
  307.0 1.2 fusion.14.branch
  308.1 154.4 %shard_map.207 = (bf16[3,512,512]{2,1,0:T(8,128)(2,1)}, f32[2,64,2048]{2,1,0:T(8,128)}, f32[8,512]{1,0:T(8,128)}, bf16[512,2048]{1,0:T(8,128)(2,1)}, bf16[8,256,...) custom-call(bf16[2,64,2048]{2,1,0:T(8,128)(2,1)} %fusion.14.branch, bf16[512,2048]{1,0:T(8,128)(2,1)} %merge.3, ...), custom_call_target="tpu_custom_call" | custom-call | flops 10000000000 | bytes 41943040 | tf_op jit(solution)/shard_map/pallas_call | solution.py:1226
  462.6 2.3 fusion.8
  464.9 0.4 fusion
  465.4 0.1 pad_maximum_fusion
  465.5 0.1 reshape.129.shared
  465.6 0.7 fusion.13
  466.4 1.6 copy-done.2
  468.0 161.2 %shard_map.208 = (bf16[4,8,16,2048]{3,2,1,0:T(8,128)(2,1)S(1)}, bf16[12,8,64,512]{3,2,1,0:T(8,128)(2,1)}, bf16[1,8,16,384]{3,2,1,0:T(8,128)(2,1)S(1)}) custom-call(bf16[512,2048]{1,0:T(8,128)(2,1)S(1)} %bitcast.44, bf16[3,512,512]{2,1,0:T(8,128)(2,1)S(1)} %copy-done.3, bf16[4,8,16,2048]{3,2,1,0:T(8,128)(2,1)} %bitcast.67, ...), custom_call_target="tpu_custom_call" | custom-call | flops 3221225472 | bytes 41943040 | tf_op jit(solution)/shard_map/pallas_call | solution.py:493
  629.2 15.3 %shard_map.209 = (f32[6144,512]{1,0:T(8,128)}, f32[512,2048]{1,0:T(8,128)}, f32[4,256,2048]{2,1,0:T(8,128)}, f32[512,2048]{1,0:T(8,128)}) custom-call(bf16[6144,512]{1,0:T(8,128)(2,1)} %bitcast.45, bf16[512,2048]{1,0:T(8,128)(2,1)S(1)} %bitcast.43, bf16[8,256,1024]{2,1,0:T(8,128)(2,1)S(1)} %copy-done.1, f32[512,2048]{1,0:T(8,128)S(1)} %copy-done), custom_call_target="tpu_custom_call" | custom-call | tf_op jit(solution)/shard_map/pallas_call | solution.py:907
  644.5 0.1 reshape.131
  644.6 0.7 slice.73
  645.3 0.6 slice.68
  645.9 0.1 slice.69
  646.0 0.6 slice_convert_fusion.2
  646.6 0.7 broadcast_multiply_fusion
  647.3 3.0 fusion.7
  (42 shorter events, 0.3 us)
Async XLA Ops:
  111.3 194.2 %copy-start.11 = (f32[2,64,128]{2,1,0:T(8,128)S(1)}, f32[2,64,128]{2,1,0:T(8,128)}, u32[]{:S(2)}) copy-start(f32[2,64,128]{2,1,0:T(8,128)} %get-tuple-element.42) | copy-start | bytes 196612
  304.1 1.5 copy-start.4
  304.2 1.6 copy-start.8
  304.2 1.8 copy-start.14
  304.2 1.8 copy-start.13
  305.4 1.5 copy-start.9
  307.0 1.2 copy-start.6
  308.1 156.8 %copy-start.12 = (bf16[2,64,2176]{2,1,0:T(8,128)(2,1)S(1)}, bf16[2,64,2176]{2,1,0:T(8,128)(2,1)}, u32[]{:S(2)}) copy-start(bf16[2,64,2176]{2,1,0:T(8,128)(2,1)} %get-tuple-element.39) | copy-start | bytes 1671172
  462.6 3.8 copy-start.3
  466.4 1.6 copy-start.2
  468.0 161.2 %copy-start = (f32[512,2048]{1,0:T(8,128)S(1)}, f32[512,2048]{1,0:T(8,128)}, u32[]{:S(2)}) copy-start(f32[512,2048]{1,0:T(8,128)} %get-tuple-element.62.shrink) | copy-start | bytes 12582916
  468.0 161.2 %copy-start.1 = (bf16[8,256,1024]{2,1,0:T(8,128)(2,1)S(1)}, bf16[8,256,1024]{2,1,0:T(8,128)(2,1)}, u32[]{:S(2)}) copy-start(bf16[8,256,1024]{2,1,0:T(8,128)(2,1)} %get-tuple-element.61.wide) | copy-start | bytes 12582916
  629.2 18.1 %copy-start.5 = (f32[2,64,2048]{2,1,0:T(8,128)S(1)}, f32[2,64,2048]{2,1,0:T(8,128)}, u32[]{:S(2)}) copy-start(f32[2,64,2048]{2,1,0:T(8,128)} %get-tuple-element.38) | copy-start | bytes 3145732
  629.2 18.1 %copy-start.7 = (f32[2,64,2048]{2,1,0:T(8,128)S(1)}, f32[2,64,2048]{2,1,0:T(8,128)}, u32[]{:S(2)}) copy-start(f32[2,64,2048]{2,1,0:T(8,128)} %copy-done.6) | copy-start | bytes 3145732
  629.2 18.1 %copy-start.10 = (bf16[2,64,2048]{2,1,0:T(8,128)(2,1)S(1)}, bf16[2,64,2048]{2,1,0:T(8,128)(2,1)}, u32[]{:S(2)}) copy-start(bf16[2,64,2048]{2,1,0:T(8,128)(2,1)} %param.25) | copy-start | bytes 1572868

commit v7 on v6

--- a/solution.py
+++ b/solution.py
@@ -18,6 +18,8 @@
 ALL = ("grp", "ep")
 MESH = pl.DeviceIdType.MESH
 ROWS = 16
+CUTS = 8
+PER_STEP = 4
 BF = jnp.bfloat16
 F32 = jnp.float32
 
@@ -1102,10 +1104,10 @@
         back = Backdrop(groups, parts, part, summed, *behind)
         greet_lines([seq.line, over] + back.near())
         steps = back.chunks + back.lag
-        step = back.step
+        behind_step = back.step
     else:
         greet_lines([seq.line, over])
-        steps, step = 0, lambda t: None
+        steps, behind_step = 0, lambda t: None
         summed[...] = jnp.zeros_like(summed)
     for m in range(micro):
         rows_all[m, pl.ds(pl.multiple_of(seq.e * block, block), block), :] = branch[m]
@@ -1115,7 +1117,22 @@
     own_wide = pltpu.make_async_copy(wide.at[g], wide_all.at[g], load.at[8])
     own_wide.start()
     turn = swap_legs(over, lambda i: wide.at[i], lambda j, i: wide_all.at[i], lambda j: w_send.at[j], lambda j: w_recv.at[j])
-    start_legs(turn)
+    pieces = CUTS * (groups - 1)
+    tall = wide.shape[1] // CUTS
+
+    def step(t):
+        for u in range(PER_STEP):
+            i = t * PER_STEP + u
+
+            @pl.when((i >= 0) & (i < pieces))
+            def _(i=i):
+                j, cut = lax.rem(i, groups - 1), lax.div(i, groups - 1)
+                to = lax.rem(g + 1 + j, groups)
+                here = pl.ds(pl.multiple_of(cut * tall, ROWS), tall)
+                remote(wide.at[to, here, :], wide_all.at[g, here, :], w_send.at[j], w_recv.at[j], over.at(to - g)).start()
+
+        behind_step(t)
+
     step(0)
     step(1)
     step(2)
@@ -1206,7 +1223,7 @@
     step(done + 1)
     end_legs(reduce_x)
     seq.total_x(partial, land_x, d_in)
-    for t in range(done + 2, steps):
+    for t in range(done + 2, max(steps, -(-pieces // PER_STEP))):
         step(t)
     end_legs(turn)
     own_wide.wait()

time: 651 us -> 648 us (level)
  no operation moved by 1% of the time
where the time goes in v7:
time: 648 us
  Pallas kernels  632 us (98%)
  other arithmetic  9.55 us (1%)
    pallas_call x1, Pallas kernels, experts_together(): pl.pallas_call(functools.partial(experts_kernel, groups, parts, local_row...  193 us
    pallas_call x1, Pallas kernels, total_over_groups(): pl.pallas_call(functools.partial(total_kernel, groups, parts, plan), out_...  162 us
    pallas_call x1, Pallas kernels, attention_back(): pl.pallas_call(functools.partial(back_kernel, groups, parts, backed), out...  151 us
    pallas_call x1, Pallas kernels, attention_forward(): pl.pallas_call(functools.partial(forward_kernel, groups, parts, experts),...  111 us
    pallas_call x1, Pallas kernels, finish(): pl.pallas_call(functools.partial(finish_kernel, share), grid=(steps, 2),...  15.3 us

profile of v7, /device:TPU:0, one launch (start us, length us, event | category | flops | bytes accessed | tf_op | source)
XLA Modules:
  0.0 647.7 jit_solution(3451933846126386348)
XLA Ops:
  0.6 110.6 %shard_map.205 = (bf16[2,256,2048]{2,1,0:T(8,128)(2,1)}, bf16[2,256,512]{2,1,0:T(8,128)(2,1)}, bf16[2,256,512]{2,1,0:T(8,128)(2,1)}, bf16[2,256,512]{2,1,0:T(8,1...) custom-call(bf16[2,64,2048]{2,1,0:T(8,128)(2,1)} %x.5, ...), custom_call_target="tpu_custom_call" | custom-call | flops 6000000000 | bytes 41943040 | tf_op jit(solution)/shard_map/pallas_call | solution.py:1494
  111.3 192.9 %shard_map.206 = (bf16[8,16,2176]{2,1,0:T(8,128)(2,1)}, bf16[8,512,2048]{2,1,0:T(8,128)(2,1)}, bf16[2048,1024]{1,0:T(8,128)(2,1)}, f32[512,2048]{1,0:T(8,128)}) custom-call(bf16[8,16,2176]{2,1,0:T(8,128)(2,1)} %bitcast.49, bf16[8,512,2048]{2,1,0:T(8,128)(2,1)} %bitcast.65, bf16[4,2048,2048]{2,1,0:T(8,128)(2,1)} %widen.1, bf16[4,1024,2048]{2,1,0:T(8,128)(2,1)} %shrink.1), custom_call_target="tpu_custom_call" | custom-call | flops 77309411328 | bytes 83886080 | tf_op jit(solution)/shard_map/pallas_call | solution.py:806
  304.2 1.2 bitcast_convert_fusion
  305.5 0.2 multiply_reduce_fusion.3
  305.6 0.2 multiply_reduce_fusion.2
  305.8 0.2 fusion.9
  306.0 0.9 multiply_reduce_fusion
  307.0 1.2 fusion.14.branch
  308.1 151.0 %shard_map.207 = (bf16[3,512,512]{2,1,0:T(8,128)(2,1)}, f32[2,64,2048]{2,1,0:T(8,128)}, f32[8,512]{1,0:T(8,128)}, bf16[512,2048]{1,0:T(8,128)(2,1)}, bf16[8,256,...) custom-call(bf16[2,64,2048]{2,1,0:T(8,128)(2,1)} %fusion.14.branch, bf16[512,2048]{1,0:T(8,128)(2,1)} %merge.3, ...), custom_call_target="tpu_custom_call" | custom-call | flops 10000000000 | bytes 41943040 | tf_op jit(solution)/shard_map/pallas_call | solution.py:1243
  459.2 2.3 fusion.8
  461.5 0.4 fusion
  461.9 0.1 pad_maximum_fusion
  462.1 0.1 reshape.129.shared
  462.1 0.7 fusion.13
  463.0 1.6 copy-done.2
  464.5 162.1 %shard_map.208 = (bf16[4,8,16,2048]{3,2,1,0:T(8,128)(2,1)S(1)}, bf16[12,8,64,512]{3,2,1,0:T(8,128)(2,1)}, bf16[1,8,16,384]{3,2,1,0:T(8,128)(2,1)S(1)}) custom-call(bf16[512,2048]{1,0:T(8,128)(2,1)S(1)} %bitcast.44, bf16[3,512,512]{2,1,0:T(8,128)(2,1)S(1)} %copy-done.3, bf16[4,8,16,2048]{3,2,1,0:T(8,128)(2,1)} %bitcast.67, ...), custom_call_target="tpu_custom_call" | custom-call | flops 3221225472 | bytes 41943040 | tf_op jit(solution)/shard_map/pallas_call | solution.py:495
  626.7 15.3 %shard_map.209 = (f32[6144,512]{1,0:T(8,128)}, f32[512,2048]{1,0:T(8,128)}, f32[4,256,2048]{2,1,0:T(8,128)}, f32[512,2048]{1,0:T(8,128)}) custom-call(bf16[6144,512]{1,0:T(8,128)(2,1)} %bitcast.45, bf16[512,2048]{1,0:T(8,128)(2,1)S(1)} %bitcast.43, bf16[8,256,1024]{2,1,0:T(8,128)(2,1)S(1)} %copy-done.1, f32[512,2048]{1,0:T(8,128)S(1)} %copy-done), custom_call_target="tpu_custom_call" | custom-call | tf_op jit(solution)/shard_map/pallas_call | solution.py:909
  642.0 0.1 reshape.131
  642.1 0.7 slice.73
  642.7 0.6 slice.68
  643.4 0.1 slice.69
  643.5 0.6 slice_convert_fusion.2
  644.1 0.7 broadcast_multiply_fusion
  644.7 3.0 fusion.7
  (42 shorter events, 0.3 us)
Async XLA Ops:
  111.3 194.2 %copy-start.11 = (f32[2,64,128]{2,1,0:T(8,128)S(1)}, f32[2,64,128]{2,1,0:T(8,128)}, u32[]{:S(2)}) copy-start(f32[2,64,128]{2,1,0:T(8,128)} %get-tuple-element.42) | copy-start | bytes 196612
  304.1 1.5 copy-start.4
  304.2 1.6 copy-start.8
  304.2 1.8 copy-start.14
  304.2 1.8 copy-start.13
  305.4 1.5 copy-start.9
  307.0 1.2 copy-start.6
  308.1 153.3 %copy-start.12 = (bf16[2,64,2176]{2,1,0:T(8,128)(2,1)S(1)}, bf16[2,64,2176]{2,1,0:T(8,128)(2,1)}, u32[]{:S(2)}) copy-start(bf16[2,64,2176]{2,1,0:T(8,128)(2,1)} %get-tuple-element.39) | copy-start | bytes 1671172
  459.2 3.8 copy-start.3
  462.9 1.6 copy-start.2
  464.5 162.1 %copy-start = (f32[512,2048]{1,0:T(8,128)S(1)}, f32[512,2048]{1,0:T(8,128)}, u32[]{:S(2)}) copy-start(f32[512,2048]{1,0:T(8,128)} %get-tuple-element.62.shrink) | copy-start | bytes 12582916
  464.5 162.1 %copy-start.1 = (bf16[8,256,1024]{2,1,0:T(8,128)(2,1)S(1)}, bf16[8,256,1024]{2,1,0:T(8,128)(2,1)}, u32[]{:S(2)}) copy-start(bf16[8,256,1024]{2,1,0:T(8,128)(2,1)} %get-tuple-element.61.wide) | copy-start | bytes 12582916
  626.6 18.1 %copy-start.5 = (f32[2,64,2048]{2,1,0:T(8,128)S(1)}, f32[2,64,2048]{2,1,0:T(8,128)}, u32[]{:S(2)}) copy-start(f32[2,64,2048]{2,1,0:T(8,128)} %get-tuple-element.38) | copy-start | bytes 3145732
  626.6 18.1 %copy-start.7 = (f32[2,64,2048]{2,1,0:T(8,128)S(1)}, f32[2,64,2048]{2,1,0:T(8,128)}, u32[]{:S(2)}) copy-start(f32[2,64,2048]{2,1,0:T(8,128)} %copy-done.6) | copy-start | bytes 3145732
  626.7 18.1 %copy-start.10 = (bf16[2,64,2048]{2,1,0:T(8,128)(2,1)S(1)}, bf16[2,64,2048]{2,1,0:T(8,128)(2,1)}, u32[]{:S(2)}) copy-start(bf16[2,64,2048]{2,1,0:T(8,128)(2,1)} %param.25) | copy-start | bytes 1572868

commit v8 on v7

--- a/solution.py
+++ b/solution.py
@@ -903,17 +903,17 @@
         wide = wide.reshape(groups, rows, local_exp // 2, 2, 2, share).transpose(2, 4, 1, 3, 0, 5)
         return qkv.astype(F32), out.astype(F32), wide.reshape(whole).astype(F32), shrink
     steps = 2 * local_exp
-    cut = lambda a: pl.BlockSpec((a.shape[0] // (2 * steps), a.shape[1]), lambda i, j: (2 * i + j, 0))
+    cut = lambda a: pl.BlockSpec((a.shape[0] // steps, a.shape[1]), lambda i: (i, 0))
     outs = [jax.ShapeDtypeStruct(a.shape, F32) for a in (qkv, out)] + [
         jax.ShapeDtypeStruct(whole, F32), jax.ShapeDtypeStruct(shrink.shape, F32)]
     return pl.pallas_call(
         functools.partial(finish_kernel, share),
-        grid=(steps, 2),
+        grid=(steps,),
         out_shape=outs,
         in_specs=[cut(qkv), cut(out),
-                  pl.BlockSpec((groups, rows // 2, share), lambda i, j: (0, j, i // 4 * 4 + i % 2 * 2 + i // 2 % 2)), cut(shrink)],
+                  pl.BlockSpec((groups, rows, share), lambda i: (0, 0, i // 4 * 4 + i % 2 * 2 + i // 2 % 2)), cut(shrink)],
         out_specs=[cut(qkv), cut(out),
-                   pl.BlockSpec((1, rows // 2, groups * share), lambda i, j: (i // 2, j, i % 2)), cut(shrink)],
+                   pl.BlockSpec((1, rows, groups * share), lambda i: (i // 2, 0, i % 2)), cut(shrink)],
         compiler_params=pltpu.CompilerParams(vmem_limit_bytes=40 * 2**20),
     )(qkv, out, wide, shrink)
 

time: 648 us -> 645 us (level)
  no operation moved by 1% of the time
where the time goes in v8:
time: 645 us
  Pallas kernels  629 us (98%)
  other arithmetic  9.55 us (1%)
    pallas_call x1, Pallas kernels, experts_together(): pl.pallas_call(functools.partial(experts_kernel, groups, parts, local_row...  193 us
    pallas_call x1, Pallas kernels, total_over_groups(): pl.pallas_call(functools.partial(total_kernel, groups, parts, plan), out_...  162 us
    pallas_call x1, Pallas kernels, attention_back(): pl.pallas_call(functools.partial(back_kernel, groups, parts, backed), out...  151 us
    pallas_call x1, Pallas kernels, attention_forward(): pl.pallas_call(functools.partial(forward_kernel, groups, parts, experts),...  111 us

profile of v8, /device:TPU:0, one launch (start us, length us, event | category | flops | bytes accessed | tf_op | source)
XLA Modules:
  0.0 644.9 jit_solution(18331140510206566690)
XLA Ops:
  0.6 110.6 %shard_map.205 = (bf16[2,256,2048]{2,1,0:T(8,128)(2,1)}, bf16[2,256,512]{2,1,0:T(8,128)(2,1)}, bf16[2,256,512]{2,1,0:T(8,128)(2,1)}, bf16[2,256,512]{2,1,0:T(8,1...) custom-call(bf16[2,64,2048]{2,1,0:T(8,128)(2,1)} %x.5, ...), custom_call_target="tpu_custom_call" | custom-call | flops 6000000000 | bytes 41943040 | tf_op jit(solution)/shard_map/pallas_call | solution.py:1494
  111.3 192.9 %shard_map.206 = (bf16[8,16,2176]{2,1,0:T(8,128)(2,1)}, bf16[8,512,2048]{2,1,0:T(8,128)(2,1)}, bf16[2048,1024]{1,0:T(8,128)(2,1)}, f32[512,2048]{1,0:T(8,128)}) custom-call(bf16[8,16,2176]{2,1,0:T(8,128)(2,1)} %bitcast.49, bf16[8,512,2048]{2,1,0:T(8,128)(2,1)} %bitcast.65, bf16[4,2048,2048]{2,1,0:T(8,128)(2,1)} %widen.1, bf16[4,1024,2048]{2,1,0:T(8,128)(2,1)} %shrink.1), custom_call_target="tpu_custom_call" | custom-call | flops 77309411328 | bytes 83886080 | tf_op jit(solution)/shard_map/pallas_call | solution.py:806
  304.2 1.2 bitcast_convert_fusion
  305.5 0.2 multiply_reduce_fusion.3
  305.6 0.2 multiply_reduce_fusion.2
  305.8 0.2 fusion.9
  306.0 0.9 multiply_reduce_fusion
  307.0 1.2 fusion.14.branch
  308.1 151.0 %shard_map.207 = (bf16[3,512,512]{2,1,0:T(8,128)(2,1)}, f32[2,64,2048]{2,1,0:T(8,128)}, f32[8,512]{1,0:T(8,128)}, bf16[512,2048]{1,0:T(8,128)(2,1)}, bf16[8,256,...) custom-call(bf16[2,64,2048]{2,1,0:T(8,128)(2,1)} %fusion.14.branch, bf16[512,2048]{1,0:T(8,128)(2,1)} %merge.3, ...), custom_call_target="tpu_custom_call" | custom-call | flops 10000000000 | bytes 41943040 | tf_op jit(solution)/shard_map/pallas_call | solution.py:1243
  459.2 2.3 fusion.8
  461.5 0.4 fusion
  461.9 0.1 pad_maximum_fusion
  462.1 0.1 reshape.129.shared
  462.1 0.7 fusion.13
  463.0 1.6 copy-done.2
  464.5 162.1 %shard_map.208 = (bf16[4,8,16,2048]{3,2,1,0:T(8,128)(2,1)S(1)}, bf16[12,8,64,512]{3,2,1,0:T(8,128)(2,1)}, bf16[1,8,16,384]{3,2,1,0:T(8,128)(2,1)S(1)}) custom-call(bf16[512,2048]{1,0:T(8,128)(2,1)S(1)} %bitcast.44, bf16[3,512,512]{2,1,0:T(8,128)(2,1)S(1)} %copy-done.3, bf16[4,8,16,2048]{3,2,1,0:T(8,128)(2,1)} %bitcast.67, ...), custom_call_target="tpu_custom_call" | custom-call | flops 3221225472 | bytes 41943040 | tf_op jit(solution)/shard_map/pallas_call | solution.py:495
  626.7 12.4 %shard_map.209 = (f32[6144,512]{1,0:T(8,128)}, f32[512,2048]{1,0:T(8,128)}, f32[4,256,2048]{2,1,0:T(8,128)}, f32[512,2048]{1,0:T(8,128)}) custom-call(bf16[6144,512]{1,0:T(8,128)(2,1)} %bitcast.45, bf16[512,2048]{1,0:T(8,128)(2,1)S(1)} %bitcast.43, bf16[8,256,1024]{2,1,0:T(8,128)(2,1)S(1)} %copy-done.1, f32[512,2048]{1,0:T(8,128)S(1)} %copy-done), custom_call_target="tpu_custom_call" | custom-call | tf_op jit(solution)/shard_map/pallas_call | solution.py:909
  639.1 0.1 reshape.131
  639.2 0.7 slice.73
  639.9 0.6 slice.68
  640.5 0.1 slice.69
  640.6 0.6 slice_convert_fusion.2
  641.2 0.7 broadcast_multiply_fusion
  641.9 3.0 fusion.7
  (42 shorter events, 0.3 us)
Async XLA Ops:
  111.3 194.2 %copy-start.11 = (f32[2,64,128]{2,1,0:T(8,128)S(1)}, f32[2,64,128]{2,1,0:T(8,128)}, u32[]{:S(2)}) copy-start(f32[2,64,128]{2,1,0:T(8,128)} %get-tuple-element.42) | copy-start | bytes 196612
  304.1 1.5 copy-start.4
  304.2 1.6 copy-start.8
  304.2 1.8 copy-start.14
  304.2 1.8 copy-start.13
  305.4 1.5 copy-start.9
  307.0 1.2 copy-start.6
  308.1 153.3 %copy-start.12 = (bf16[2,64,2176]{2,1,0:T(8,128)(2,1)S(1)}, bf16[2,64,2176]{2,1,0:T(8,128)(2,1)}, u32[]{:S(2)}) copy-start(bf16[2,64,2176]{2,1,0:T(8,128)(2,1)} %get-tuple-element.39) | copy-start | bytes 1671172
  459.2 3.8 copy-start.3
  462.9 1.6 copy-start.2
  464.5 162.1 %copy-start = (f32[512,2048]{1,0:T(8,128)S(1)}, f32[512,2048]{1,0:T(8,128)}, u32[]{:S(2)}) copy-start(f32[512,2048]{1,0:T(8,128)} %get-tuple-element.62.shrink) | copy-start | bytes 12582916
  464.5 162.1 %copy-start.1 = (bf16[8,256,1024]{2,1,0:T(8,128)(2,1)S(1)}, bf16[8,256,1024]{2,1,0:T(8,128)(2,1)}, u32[]{:S(2)}) copy-start(bf16[8,256,1024]{2,1,0:T(8,128)(2,1)} %get-tuple-element.61.wide) | copy-start | bytes 12582916
  626.6 15.2 %copy-start.5 = (f32[2,64,2048]{2,1,0:T(8,128)S(1)}, f32[2,64,2048]{2,1,0:T(8,128)}, u32[]{:S(2)}) copy-start(f32[2,64,2048]{2,1,0:T(8,128)} %get-tuple-element.38) | copy-start | bytes 3145732
  626.6 15.2 %copy-start.7 = (f32[2,64,2048]{2,1,0:T(8,128)S(1)}, f32[2,64,2048]{2,1,0:T(8,128)}, u32[]{:S(2)}) copy-start(f32[2,64,2048]{2,1,0:T(8,128)} %copy-done.6) | copy-start | bytes 3145732
  626.7 15.2 %copy-start.10 = (bf16[2,64,2048]{2,1,0:T(8,128)(2,1)S(1)}, bf16[2,64,2048]{2,1,0:T(8,128)(2,1)}, u32[]{:S(2)}) copy-start(bf16[2,64,2048]{2,1,0:T(8,128)(2,1)} %param.25) | copy-start | bytes 1572868

commit v9 on v8

--- a/solution.py
+++ b/solution.py
@@ -19,7 +19,7 @@
 MESH = pl.DeviceIdType.MESH
 ROWS = 16
 CUTS = 8
-PER_STEP = 4
+PER_STEP = 6
 BF = jnp.bfloat16
 F32 = jnp.float32
 

time: 645 us -> 648 us (level)
  no operation moved by 1% of the time
where the time goes in v9:
time: 648 us
  Pallas kernels  632 us (98%)
  other arithmetic  9.55 us (1%)
    pallas_call x1, Pallas kernels, experts_together(): pl.pallas_call(functools.partial(experts_kernel, groups, parts, local_row...  193 us
    pallas_call x1, Pallas kernels, total_over_groups(): pl.pallas_call(functools.partial(total_kernel, groups, parts, plan), out_...  161 us
    pallas_call x1, Pallas kernels, attention_back(): pl.pallas_call(functools.partial(back_kernel, groups, parts, backed), out...  155 us
    pallas_call x1, Pallas kernels, attention_forward(): pl.pallas_call(functools.partial(forward_kernel, groups, parts, experts),...  111 us

profile of v9, /device:TPU:0, one launch (start us, length us, event | category | flops | bytes accessed | tf_op | source)
XLA Modules:
  0.0 647.9 jit_solution(14796429854171101950)
XLA Ops:
  0.6 110.6 %shard_map.205 = (bf16[2,256,2048]{2,1,0:T(8,128)(2,1)}, bf16[2,256,512]{2,1,0:T(8,128)(2,1)}, bf16[2,256,512]{2,1,0:T(8,128)(2,1)}, bf16[2,256,512]{2,1,0:T(8,1...) custom-call(bf16[2,64,2048]{2,1,0:T(8,128)(2,1)} %x.5, ...), custom_call_target="tpu_custom_call" | custom-call | flops 6000000000 | bytes 41943040 | tf_op jit(solution)/shard_map/pallas_call | solution.py:1494
  111.3 192.9 %shard_map.206 = (bf16[8,16,2176]{2,1,0:T(8,128)(2,1)}, bf16[8,512,2048]{2,1,0:T(8,128)(2,1)}, bf16[2048,1024]{1,0:T(8,128)(2,1)}, f32[512,2048]{1,0:T(8,128)}) custom-call(bf16[8,16,2176]{2,1,0:T(8,128)(2,1)} %bitcast.49, bf16[8,512,2048]{2,1,0:T(8,128)(2,1)} %bitcast.65, bf16[4,2048,2048]{2,1,0:T(8,128)(2,1)} %widen.1, bf16[4,1024,2048]{2,1,0:T(8,128)(2,1)} %shrink.1), custom_call_target="tpu_custom_call" | custom-call | flops 77309411328 | bytes 83886080 | tf_op jit(solution)/shard_map/pallas_call | solution.py:806
  304.2 1.2 bitcast_convert_fusion
  305.5 0.2 multiply_reduce_fusion.3
  305.6 0.2 multiply_reduce_fusion.2
  305.8 0.2 fusion.9
  306.0 0.9 multiply_reduce_fusion
  307.0 1.2 fusion.14.branch
  308.1 154.6 %shard_map.207 = (bf16[3,512,512]{2,1,0:T(8,128)(2,1)}, f32[2,64,2048]{2,1,0:T(8,128)}, f32[8,512]{1,0:T(8,128)}, bf16[512,2048]{1,0:T(8,128)(2,1)}, bf16[8,256,...) custom-call(bf16[2,64,2048]{2,1,0:T(8,128)(2,1)} %fusion.14.branch, bf16[512,2048]{1,0:T(8,128)(2,1)} %merge.3, ...), custom_call_target="tpu_custom_call" | custom-call | flops 10000000000 | bytes 41943040 | tf_op jit(solution)/shard_map/pallas_call | solution.py:1243
  462.8 2.3 fusion.8
  465.1 0.4 fusion
  465.5 0.1 pad_maximum_fusion
  465.7 0.1 reshape.129.shared
  465.7 0.7 fusion.13
  466.5 1.6 copy-done.2
  468.1 161.5 %shard_map.208 = (bf16[4,8,16,2048]{3,2,1,0:T(8,128)(2,1)S(1)}, bf16[12,8,64,512]{3,2,1,0:T(8,128)(2,1)}, bf16[1,8,16,384]{3,2,1,0:T(8,128)(2,1)S(1)}) custom-call(bf16[512,2048]{1,0:T(8,128)(2,1)S(1)} %bitcast.44, bf16[3,512,512]{2,1,0:T(8,128)(2,1)S(1)} %copy-done.3, bf16[4,8,16,2048]{3,2,1,0:T(8,128)(2,1)} %bitcast.67, ...), custom_call_target="tpu_custom_call" | custom-call | flops 3221225472 | bytes 41943040 | tf_op jit(solution)/shard_map/pallas_call | solution.py:495
  629.7 12.4 %shard_map.209 = (f32[6144,512]{1,0:T(8,128)}, f32[512,2048]{1,0:T(8,128)}, f32[4,256,2048]{2,1,0:T(8,128)}, f32[512,2048]{1,0:T(8,128)}) custom-call(bf16[6144,512]{1,0:T(8,128)(2,1)} %bitcast.45, bf16[512,2048]{1,0:T(8,128)(2,1)S(1)} %bitcast.43, bf16[8,256,1024]{2,1,0:T(8,128)(2,1)S(1)} %copy-done.1, f32[512,2048]{1,0:T(8,128)S(1)} %copy-done), custom_call_target="tpu_custom_call" | custom-call | tf_op jit(solution)/shard_map/pallas_call | solution.py:909
  642.1 0.1 reshape.131
  642.2 0.7 slice.73
  642.9 0.6 slice.68
  643.5 0.1 slice.69
  643.6 0.6 slice_convert_fusion.2
  644.2 0.7 broadcast_multiply_fusion
  644.9 3.0 fusion.7
  (42 shorter events, 0.3 us)
Async XLA Ops:
  111.3 194.2 %copy-start.11 = (f32[2,64,128]{2,1,0:T(8,128)S(1)}, f32[2,64,128]{2,1,0:T(8,128)}, u32[]{:S(2)}) copy-start(f32[2,64,128]{2,1,0:T(8,128)} %get-tuple-element.42) | copy-start | bytes 196612
  304.1 1.5 copy-start.4
  304.2 1.6 copy-start.8
  304.2 1.8 copy-start.14
  304.2 1.8 copy-start.13
  305.4 1.5 copy-start.9
  307.0 1.2 copy-start.6
  308.1 156.9 %copy-start.12 = (bf16[2,64,2176]{2,1,0:T(8,128)(2,1)S(1)}, bf16[2,64,2176]{2,1,0:T(8,128)(2,1)}, u32[]{:S(2)}) copy-start(bf16[2,64,2176]{2,1,0:T(8,128)(2,1)} %get-tuple-element.39) | copy-start | bytes 1671172
  462.7 3.8 copy-start.3
  466.5 1.6 copy-start.2
  468.1 161.5 %copy-start = (f32[512,2048]{1,0:T(8,128)S(1)}, f32[512,2048]{1,0:T(8,128)}, u32[]{:S(2)}) copy-start(f32[512,2048]{1,0:T(8,128)} %get-tuple-element.62.shrink) | copy-start | bytes 12582916
  468.1 161.5 %copy-start.1 = (bf16[8,256,1024]{2,1,0:T(8,128)(2,1)S(1)}, bf16[8,256,1024]{2,1,0:T(8,128)(2,1)}, u32[]{:S(2)}) copy-start(bf16[8,256,1024]{2,1,0:T(8,128)(2,1)} %get-tuple-element.61.wide) | copy-start | bytes 12582916
  629.7 15.2 %copy-start.5 = (f32[2,64,2048]{2,1,0:T(8,128)S(1)}, f32[2,64,2048]{2,1,0:T(8,128)}, u32[]{:S(2)}) copy-start(f32[2,64,2048]{2,1,0:T(8,128)} %get-tuple-element.38) | copy-start | bytes 3145732
  629.7 15.2 %copy-start.7 = (f32[2,64,2048]{2,1,0:T(8,128)S(1)}, f32[2,64,2048]{2,1,0:T(8,128)}, u32[]{:S(2)}) copy-start(f32[2,64,2048]{2,1,0:T(8,128)} %copy-done.6) | copy-start | bytes 3145732
  629.7 15.2 %copy-start.10 = (bf16[2,64,2048]{2,1,0:T(8,128)(2,1)S(1)}, bf16[2,64,2048]{2,1,0:T(8,128)(2,1)}, u32[]{:S(2)}) copy-start(bf16[2,64,2048]{2,1,0:T(8,128)(2,1)} %param.25) | copy-start | bytes 1572868
